TPU v7x, 32 devices: a whole 2x2x4 slice. The times are simulated.
32 devices in a mesh: rows: 8 (over z, core), heads: 4 (over y, x).
Axes of the slice: x: 2, y: 2, z: 4, core: 2. Of those that a mesh axis runs over, the one named last changes fastest.
Arguments:
- media: bfloat16 [1024, 32, 1536], P('heads', 'rows'), may hold values from -6 to 6
- latents: float32 [32, 64, 1536], P('rows', 'heads'), may hold values from -6 to 6
- frame_count: int32 [32], P('rows'), may hold values from 1 to 8, as said below
- cotangent: float32 [32, 64, 1536], P('rows', 'heads'), may hold values from -96 to 96
- inward: float32 [2, 3, 1536, 1536], P(None, None, 'rows', 'heads'), may hold values from -0.15625 to 0.15625
- inward_first: float32 [2, 3, 1536, 1536], P(None, None, 'rows', 'heads'), may hold values from -0.00048828125 to 0.00048828125
- inward_second: float32 [2, 3, 1536, 1536], P(None, None, 'rows', 'heads'), may hold values from 1.1037897e-09 to 4.415159e-09
- outward: float32 [2, 1536, 1536], P(None, 'heads', 'rows'), may hold values from -3.5 to 3.5
- outward_first: float32 [2, 1536, 1536], P(None, 'heads', 'rows'), may hold values from -0.00048828125 to 0.00048828125
- outward_second: float32 [2, 1536, 1536], P(None, 'heads', 'rows'), may hold values from 1.1037897e-09 to 4.415159e-09
- widen: float32 [2, 1536, 6144], P(None, 'rows', 'heads'), may hold values from -0.15625 to 0.15625
- widen_first: float32 [2, 1536, 6144], P(None, 'rows', 'heads'), may hold values from -0.00048828125 to 0.00048828125
- widen_second: float32 [2, 1536, 6144], P(None, 'rows', 'heads'), may hold values from 1.1037897e-09 to 4.415159e-09
- narrow: float32 [2, 6144, 1536], P(None, 'heads', 'rows'), may hold values from -0.078125 to 0.078125
- narrow_first: float32 [2, 6144, 1536], P(None, 'heads', 'rows'), may hold values from -0.001953125 to 0.001953125
- narrow_second: float32 [2, 6144, 1536], P(None, 'heads', 'rows'), may hold values from 1.7660636e-08 to 7.064254e-08
- norm_gains: float32 [2, 6, 1536], replicated, may hold values from -1 to 2, as said below
- gain_first: float32 [2, 6, 1536], replicated, may hold values from -0.009765625 to 0.009765625
- gain_second: float32 [2, 6, 1536], replicated, may hold values from 4.4151588e-07 to 1.7660635e-06
Outputs:
- latents_next: float32 [32, 64, 1536], P('rows', 'heads')
- latent_gradient: float32 [32, 64, 1536], P('rows', 'heads')
- media_gradient: float32 [1024, 32, 1536], P('heads', 'rows')
- gradient_norm: float32 [], replicated
- inward_mean: float32 [2, 3, 1536, 1536], P(None, None, 'rows', 'heads')
- inward_square: float32 [2, 3, 1536, 1536], P(None, None, 'rows', 'heads')
- inward_next: float32 [2, 3, 1536, 1536], P(None, None, 'rows', 'heads')
- inward_copy: bfloat16 [2, 3, 1536, 1536], P(None, None, 'rows', 'heads')
- outward_mean: float32 [2, 1536, 1536], P(None, 'heads', 'rows')
- outward_square: float32 [2, 1536, 1536], P(None, 'heads', 'rows')
- outward_next: float32 [2, 1536, 1536], P(None, 'heads', 'rows')
- outward_copy: bfloat16 [2, 1536, 1536], P(None, 'heads', 'rows')
- widen_mean: float32 [2, 1536, 6144], P(None, 'rows', 'heads')
- widen_square: float32 [2, 1536, 6144], P(None, 'rows', 'heads')
- widen_next: float32 [2, 1536, 6144], P(None, 'rows', 'heads')
- widen_copy: bfloat16 [2, 1536, 6144], P(None, 'rows', 'heads')
- narrow_mean: float32 [2, 6144, 1536], P(None, 'heads', 'rows')
- narrow_square: float32 [2, 6144, 1536], P(None, 'heads', 'rows')
- narrow_next: float32 [2, 6144, 1536], P(None, 'heads', 'rows')
- narrow_copy: bfloat16 [2, 6144, 1536], P(None, 'heads', 'rows')
- gain_mean: float32 [2, 6, 1536], replicated
- gain_square: float32 [2, 6, 1536], replicated
- gain_next: float32 [2, 6, 1536], replicated
- feed_norm_gradient: float32 [2, 2, 1536], replicated
Inputs may be any that keep to these rules, and one draw needn't show every extreme that they name: `frame_count`: in every run of 4 consecutive videos starting at a multiple of 4, at least one video has 8 frames. `norm_gains`: rows 0, 2 and 4 of each layer are gains, rows 1, 3 and 5 biases.
All inputs are finite; a program needn't handle non-finite values.
Results may differ from a plain program's by a relative error of at most 0.014.
Values may be sent and summed in bfloat16 or wider, within the bound.
A program may use at most 384 MiB of HBM per device.

v0:
```python
import jax
import jax.numpy as jnp
from jax import lax
from jax.sharding import PartitionSpec as P

HD = 96
STEP = 10
PATCHES = 128


EPS_NORM = 1e-05
BETA_ONE = 0.5
BETA_TWO = 0.5
ADAM_EPS = 1e-08
WEIGHT_DECAY = 0.1
CLIP_LEVEL = 1.0
MASKED_SCORE = -1e30
RATE_INWARD = 0.02
RATE_OUTWARD = 0.5
RATE_WIDEN = 0.02
RATE_NARROW = 0.01
RATE_GAINS = 0.1


def layer_norm(rows, gain, shift):
    middle = jnp.mean(rows, axis=-1, keepdims=True)
    centred = rows - middle
    spread = jnp.mean(centred * centred, axis=-1, keepdims=True)
    return centred * lax.rsqrt(spread + EPS_NORM) * gain + shift


def norm_back(rows, gain, shift, slope):
    _, pullback = jax.vjp(layer_norm, rows, gain, shift)
    return pullback(slope)


def adam_step(weight, first, second, gradient, rate, decay):
    mean_new = BETA_ONE * first + (1.0 - BETA_ONE) * gradient
    square_new = BETA_TWO * second + (1.0 - BETA_TWO) * gradient * gradient
    mean_hat = mean_new / (1.0 - BETA_ONE**STEP)
    square_hat = square_new / (1.0 - BETA_TWO**STEP)
    weight_new = weight - rate * (mean_hat / (jnp.sqrt(square_hat) + ADAM_EPS) + decay * weight)
    return (mean_new, square_new, weight_new)


def gather_slots(rows):
    return lax.all_gather(rows, "heads", axis=1, tiled=True)


def scatter_slots(terms):
    return lax.psum_scatter(terms, "heads", scatter_dimension=1, tiled=True)


def gather_slopes(rows):
    return lax.all_gather(rows, "heads", axis=1, tiled=True)


def scatter_slopes(terms):
    return lax.psum_scatter(terms, "heads", scatter_dimension=1, tiled=True)


def both_scores(query, media_pair, latent_pair, live, scale):
    score_media = (
        jnp.einsum("vnhe,pvhe->vhnp", query, media_pair[0], preferred_element_type=jnp.float32)
        * scale
    )
    score_media = jnp.where(live[:, None, None, :], score_media, MASKED_SCORE)
    score_latent = (
        jnp.einsum("vnhe,vmhe->vhnm", query, latent_pair[0], preferred_element_type=jnp.float32)
        * scale
    )
    return (score_media, score_latent)


def attend(query, media_pair, latent_pair, live, scale):
    score_media, score_latent = both_scores(query, media_pair, latent_pair, live, scale)
    top = jnp.maximum(
        jnp.max(score_media, axis=-1, keepdims=True), jnp.max(score_latent, axis=-1, keepdims=True)
    )
    exponent_media = jnp.exp(score_media - top)
    exponent_latent = jnp.exp(score_latent - top)
    total = jnp.sum(exponent_media, axis=-1, keepdims=True) + jnp.sum(
        exponent_latent, axis=-1, keepdims=True
    )
    share_media = (exponent_media / total).astype(jnp.bfloat16)
    share_latent = (exponent_latent / total).astype(jnp.bfloat16)
    mixed = jnp.einsum(
        "vhnp,pvhe->vnhe", share_media, media_pair[1], preferred_element_type=jnp.float32
    )
    mixed = mixed + jnp.einsum(
        "vhnm,vmhe->vnhe", share_latent, latent_pair[1], preferred_element_type=jnp.float32
    )
    return (mixed.astype(jnp.bfloat16), top + jnp.log(total))


def attend_back(query, media_pair, latent_pair, live, log_total, mixed_slope, scale):
    score_media, score_latent = both_scores(query, media_pair, latent_pair, live, scale)
    share_media = jnp.exp(score_media - log_total)
    share_latent = jnp.exp(score_latent - log_total)
    share_slope_media = jnp.einsum(
        "vnhe,pvhe->vhnp", mixed_slope, media_pair[1], preferred_element_type=jnp.float32
    )
    share_slope_latent = jnp.einsum(
        "vnhe,vmhe->vhnm", mixed_slope, latent_pair[1], preferred_element_type=jnp.float32
    )
    row_total = jnp.sum(share_media * share_slope_media, axis=-1, keepdims=True)
    row_total = row_total + jnp.sum(share_latent * share_slope_latent, axis=-1, keepdims=True)
    score_slope_media = (share_media * (share_slope_media - row_total)).astype(jnp.bfloat16)
    score_slope_latent = (share_latent * (share_slope_latent - row_total)).astype(jnp.bfloat16)
    query_slope = jnp.einsum(
        "vhnp,pvhe->vnhe", score_slope_media, media_pair[0], preferred_element_type=jnp.float32
    )
    query_slope = query_slope + jnp.einsum(
        "vhnm,vmhe->vnhe", score_slope_latent, latent_pair[0], preferred_element_type=jnp.float32
    )
    query_slope = (query_slope * scale).astype(jnp.bfloat16)
    key_media = (
        jnp.einsum("vhnp,vnhe->pvhe", score_slope_media, query, preferred_element_type=jnp.float32)
        * scale
    ).astype(jnp.bfloat16)
    value_media = jnp.einsum(
        "vhnp,vnhe->pvhe",
        share_media.astype(jnp.bfloat16),
        mixed_slope,
        preferred_element_type=jnp.float32,
    ).astype(jnp.bfloat16)
    key_latent = (
        jnp.einsum("vhnm,vnhe->vmhe", score_slope_latent, query, preferred_element_type=jnp.float32)
        * scale
    ).astype(jnp.bfloat16)
    value_latent = jnp.einsum(
        "vhnm,vnhe->vmhe",
        share_latent.astype(jnp.bfloat16),
        mixed_slope,
        preferred_element_type=jnp.float32,
    ).astype(jnp.bfloat16)
    return (query_slope, jnp.stack((key_media, value_media)), jnp.stack((key_latent, value_latent)))


def local(
    media,
    latents,
    frame_count,
    cotangent,
    inward,
    inward_first,
    inward_second,
    outward,
    outward_first,
    outward_second,
    widen,
    widen_first,
    widen_second,
    narrow,
    narrow_first,
    narrow_second,
    norm_gains,
    gain_first,
    gain_second,
):
    heads_count = lax.axis_size("heads")
    layers, _, row_share, head_columns = inward.shape
    local_positions, videos, width = media.shape
    positions = local_positions * heads_count
    latent_count = latents.shape[1] * heads_count
    local_heads = head_columns // HD
    scale = HD ** (-0.5)
    live = (jnp.arange(positions, dtype=jnp.int32) // PATCHES)[None, :] < frame_count[:, None]
    inward_columns, outward_rows, widen_columns, narrow_rows = (
        lax.all_gather(inward.astype(jnp.bfloat16), "rows", axis=2, tiled=True),
        lax.all_gather(outward.astype(jnp.bfloat16), "rows", axis=2, tiled=True),
        lax.all_gather(widen.astype(jnp.bfloat16), "rows", axis=1, tiled=True),
        lax.all_gather(narrow.astype(jnp.bfloat16), "rows", axis=2, tiled=True),
    )
    media_rows = media.astype(jnp.float32)
    latent = latents
    kept = []
    for layer in range(layers):
        gains = norm_gains[layer]
        media_norm = layer_norm(media_rows, gains[0], gains[1]).astype(jnp.bfloat16)
        latent_norm = gather_slots(layer_norm(latent, gains[2], gains[3]).astype(jnp.bfloat16))
        triple = jnp.einsum(
            "vnd,tdc->tvnc", latent_norm, inward_columns[layer], preferred_element_type=jnp.float32
        ).astype(jnp.bfloat16)
        pair_columns = inward_columns[layer, 1:3]
        media_pair = jnp.einsum(
            "pvd,tdc->tpvc",
            lax.all_gather(media_norm, "heads", axis=0, tiled=True),
            pair_columns,
            preferred_element_type=jnp.float32,
        ).astype(jnp.bfloat16)
        query = triple[0].reshape(videos, latent_count, local_heads, HD)
        latent_pair = triple[1:3].reshape(2, videos, latent_count, local_heads, HD)
        heads_pair = media_pair.reshape(2, positions, videos, local_heads, HD)
        mixed, log_total = attend(query, heads_pair, latent_pair, live, scale)
        mixed = mixed.reshape(videos, latent_count, head_columns)
        middle = latent + scatter_slots(
            jnp.einsum(
                "vnc,cd->vnd", mixed, outward_rows[layer], preferred_element_type=jnp.float32
            )
        )
        feed_norm = gather_slots(layer_norm(middle, gains[4], gains[5]).astype(jnp.bfloat16))
        hidden_pre = jnp.einsum(
            "vnd,df->vnf", feed_norm, widen_columns[layer], preferred_element_type=jnp.float32
        )
        hidden = jax.nn.gelu(hidden_pre).astype(jnp.bfloat16)
        kept.append(
            (
                latent,
                middle,
                media_norm,
                latent_norm,
                query,
                heads_pair,
                latent_pair,
                mixed,
                log_total,
                feed_norm,
                hidden_pre,
                hidden,
            )
        )
        latent = middle + scatter_slots(
            jnp.einsum(
                "vnf,fd->vnd", hidden, narrow_rows[layer], preferred_element_type=jnp.float32
            )
        )
    slope = cotangent
    media_slope = jnp.zeros(media_rows.shape, jnp.float32)
    inward_parts, outward_parts, widen_parts, narrow_parts, gain_parts = ([], [], [], [], [])
    for layer in reversed(range(layers)):
        (
            latent_in,
            middle,
            media_norm,
            latent_norm,
            query,
            heads_pair,
            latent_pair,
            mixed,
            log_total,
            feed_norm,
            hidden_pre,
            hidden,
        ) = kept[layer]
        gains = norm_gains[layer]
        feed_slope = gather_slopes(slope.astype(jnp.bfloat16))
        narrow_grad = jnp.einsum(
            "vnf,vnd->fd", hidden, feed_slope, preferred_element_type=jnp.float32
        )
        hidden_slope = jnp.einsum(
            "vnd,fd->vnf", feed_slope, narrow_rows[layer], preferred_element_type=jnp.float32
        )
        _, gelu_back = jax.vjp(jax.nn.gelu, hidden_pre)
        pre_slope = gelu_back(hidden_slope)[0].astype(jnp.bfloat16)
        widen_grad = jnp.einsum(
            "vnd,vnf->df", feed_norm, pre_slope, preferred_element_type=jnp.float32
        )
        norm_slope = scatter_slopes(
            jnp.einsum(
                "vnf,df->vnd", pre_slope, widen_columns[layer], preferred_element_type=jnp.float32
            )
        )
        middle_part, gain_feed, shift_feed = norm_back(middle, gains[4], gains[5], norm_slope)
        middle_slope = slope + middle_part
        branch_slope = gather_slopes(middle_slope.astype(jnp.bfloat16))
        outward_grad = jnp.einsum(
            "vnc,vnd->cd", mixed, branch_slope, preferred_element_type=jnp.float32
        )
        mixed_slope = jnp.einsum(
            "vnd,cd->vnc", branch_slope, outward_rows[layer], preferred_element_type=jnp.float32
        ).astype(jnp.bfloat16)
        mixed_slope = mixed_slope.reshape(videos, latent_count, local_heads, HD)
        query_slope, media_slopes, latent_slopes = attend_back(
            query, heads_pair, latent_pair, live, log_total, mixed_slope, scale
        )
        triple_slope = jnp.concatenate(
            (
                query_slope.reshape(1, videos, latent_count, head_columns),
                latent_slopes.reshape(2, videos, latent_count, head_columns),
            ),
            axis=0,
        )
        inward_grad = jnp.einsum(
            "vnd,tvnc->tdc", latent_norm, triple_slope, preferred_element_type=jnp.float32
        )
        norm_slope = scatter_slopes(
            jnp.einsum(
                "tvnc,tdc->vnd",
                triple_slope,
                inward_columns[layer],
                preferred_element_type=jnp.float32,
            )
        )
        latent_part, gain_latent, shift_latent = norm_back(
            latent_in, gains[2], gains[3], norm_slope
        )
        slope = middle_slope + latent_part
        pair_slope = media_slopes.reshape(2, positions, videos, head_columns)
        media_columns = jnp.einsum(
            "pvd,tpvc->tdc",
            lax.all_gather(media_norm, "heads", axis=0, tiled=True),
            pair_slope,
            preferred_element_type=jnp.float32,
        )
        inward_grad = jnp.concatenate((inward_grad[:1], inward_grad[1:] + media_columns), axis=0)
        pair_columns = inward_columns[layer, 1:3]
        media_norm_slope = lax.psum_scatter(
            jnp.einsum(
                "tpvc,tdc->pvd", pair_slope, pair_columns, preferred_element_type=jnp.float32
            ),
            "heads",
            scatter_dimension=0,
            tiled=True,
        )
        media_part, gain_media, shift_media = norm_back(
            media_rows, gains[0], gains[1], media_norm_slope
        )
        media_slope = media_slope + media_part
        inward_parts.append(inward_grad)
        outward_parts.append(outward_grad)
        widen_parts.append(widen_grad)
        narrow_parts.append(narrow_grad)
        gain_parts.append(
            jnp.stack((gain_media, shift_media, gain_latent, shift_latent, gain_feed, shift_feed))
        )
    inward_grad, outward_grad, widen_grad, narrow_grad = (
        lax.psum_scatter(jnp.stack(inward_parts[::-1]), "rows", scatter_dimension=2, tiled=True),
        lax.psum_scatter(jnp.stack(outward_parts[::-1]), "rows", scatter_dimension=2, tiled=True),
        lax.psum_scatter(jnp.stack(widen_parts[::-1]), "rows", scatter_dimension=1, tiled=True),
        lax.psum_scatter(jnp.stack(narrow_parts[::-1]), "rows", scatter_dimension=2, tiled=True),
    )
    squares = jnp.sum(inward_grad * inward_grad) + jnp.sum(outward_grad * outward_grad)
    squares = squares + jnp.sum(widen_grad * widen_grad) + jnp.sum(narrow_grad * narrow_grad)
    gain_total, square_total = lax.psum((jnp.stack(gain_parts[::-1]), squares), ("rows", "heads"))
    gradient_norm = jnp.sqrt(square_total + jnp.sum(gain_total * gain_total))
    factor = CLIP_LEVEL / jnp.maximum(gradient_norm, CLIP_LEVEL)
    table = (
        (inward, inward_first, inward_second, inward_grad, RATE_INWARD, WEIGHT_DECAY),
        (outward, outward_first, outward_second, outward_grad, RATE_OUTWARD, WEIGHT_DECAY),
        (widen, widen_first, widen_second, widen_grad, RATE_WIDEN, WEIGHT_DECAY),
        (narrow, narrow_first, narrow_second, narrow_grad, RATE_NARROW, WEIGHT_DECAY),
    )
    results = [latent, slope, media_slope, gradient_norm]
    for weight, first, second, gradient, rate, decay in table:
        mean_new, square_new, weight_new = adam_step(
            weight, first, second, gradient * factor, rate, decay
        )
        results = results + [mean_new, square_new, weight_new, weight_new.astype(jnp.bfloat16)]
    mean_new, square_new, weight_new = adam_step(
        norm_gains, gain_first, gain_second, gain_total * factor, RATE_GAINS, 0.0
    )
    results = results + [mean_new, square_new, weight_new, gain_total[:, 4:6]]
    return tuple(results)


def solution(mesh):
    placed = (
        P("heads", "rows", None),
        P("rows", "heads", None),
        P("rows"),
        P("rows", "heads", None),
        P(None, None, "rows", "heads"),
        P(None, None, "rows", "heads"),
        P(None, None, "rows", "heads"),
        P(None, "heads", "rows"),
        P(None, "heads", "rows"),
        P(None, "heads", "rows"),
        P(None, "rows", "heads"),
        P(None, "rows", "heads"),
        P(None, "rows", "heads"),
        P(None, "heads", "rows"),
        P(None, "heads", "rows"),
        P(None, "heads", "rows"),
        P(),
        P(),
        P(),
    )
    return jax.shard_map(
        local,
        mesh=mesh,
        in_specs=placed,
        out_specs=(
            P("rows", "heads", None),
            P("rows", "heads", None),
            P("heads", "rows", None),
            P(),
            P(None, None, "rows", "heads"),
            P(None, None, "rows", "heads"),
            P(None, None, "rows", "heads"),
            P(None, None, "rows", "heads"),
            P(None, "heads", "rows"),
            P(None, "heads", "rows"),
            P(None, "heads", "rows"),
            P(None, "heads", "rows"),
            P(None, "rows", "heads"),
            P(None, "rows", "heads"),
            P(None, "rows", "heads"),
            P(None, "rows", "heads"),
            P(None, "heads", "rows"),
            P(None, "heads", "rows"),
            P(None, "heads", "rows"),
            P(None, "heads", "rows"),
            P(),
            P(),
            P(),
            P(),
        ),
        check_vma=False,
    )
```

profile of v0, /device:TPU:0, one launch (start us, length us, event | category | flops | bytes accessed | tf_op | source)
XLA Modules:
  0.0 2577.0 jit_solution(1278266295087237182)
XLA Ops:
  26.2 14.5 all_gather.46
  56.7 60.5 %all-gather.9.cloned.1.call-done = bf16[2,3,1536,384]{3,0,1,2:T(2,128)(2,1)} async-done(((bf16[2,3,192,384]{3,0,1,2:T(2,128)(2,1)}), bf16[2,3,1536,384]{3,0,1,2:T(2,128)(2,1)}) %all-gather.9.cloned.1.call-update) | async-done | bytes 7077904 | tf_op jit(solution)/shard_map/all_gather | solution.py:170
  138.1 15.5 fusion.208
  158.9 81.3 %all-gather.7.cloned.1.call-done = bf16[1024,4,1536]{2,0,1:T(8,128)(2,1)} async-done(((bf16[256,4,1536]{2,0,1:T(8,128)(2,1)}), bf16[1024,4,1536]{2,0,1:T(8,128)(2,1)}) %all-gather.7.cloned.1.call-update) | async-done | bytes 12582928 | tf_op jit(solution)/shard_map/all_gather | solution.py:188
  240.2 12.9 convert_bitcast_fusion.1
  268.2 64.8 %all-gather.15.cloned.1.call-done = bf16[2,1536,1536]{1,0,2:T(2,128)(2,1)} async-done(((bf16[2,1536,192]{1,0,2:T(2,128)(2,1)}), bf16[2,1536,1536]{1,0,2:T(2,128)(2,1)}) %all-gather.15.cloned.1.call-update) | async-done | bytes 9437200 | tf_op jit(solution)/shard_map/all_gather | solution.py:173
  333.1 19.0 fusion.207
  352.1 22.4 copy.407
  377.3 13.6 all_gather.48
  390.9 67.8 %all-gather.13.cloned.1.call-done = bf16[2,1536,1536]{2,1,0:T(8,128)(2,1)} async-done(((bf16[2,192,1536]{2,1,0:T(8,128)(2,1)}), bf16[2,1536,1536]{2,1,0:T(8,128)(2,1)}) %all-gather.13.cloned.1.call-update) | async-done | bytes 9437200 | tf_op jit(solution)/shard_map/all_gather | solution.py:172
  487.7 93.8 %all-gather.17.cloned.1.call-done = bf16[1024,4,1536]{2,0,1:T(8,128)(2,1)} async-done(((bf16[256,4,1536]{2,0,1:T(8,128)(2,1)}), bf16[1024,4,1536]{2,0,1:T(8,128)(2,1)}) %all-gather.17.cloned.1.call-update) | async-done | bytes 12582928 | tf_op jit(solution)/shard_map/all_gather | solution.py:188
  581.6 13.6 convert_bitcast_fusion
  599.2 16.9 reduce-scatter.14.cloned.1.call-done
  657.9 15.6 all_gather.54
  673.5 22.2 copy.411
  726.2 25.5 reduce-scatter.20.cloned.1.call-done
  755.0 31.3 %reduce-scatter.18.cloned.1.call-done = f32[4,16,1536]{2,1,0:T(8,128)} async-done(((f32[4,64,1536]{2,1,0:T(8,128)}), f32[4,16,1536]{2,1,0:T(8,128)}) %reduce-scatter.18.cloned.1.call-update) | async-done | bytes 393232 | tf_op jit(solution)/shard_map/reduce_scatter | solution.py:51
  840.6 31.0 %reduce-scatter.22.cloned.1.call-done = f32[4,16,1536]{2,1,0:T(8,128)} async-done(((f32[4,64,1536]{2,1,0:T(8,128)}), f32[4,16,1536]{2,1,0:T(8,128)}) %reduce-scatter.22.cloned.1.call-update) | async-done | bytes 393232 | tf_op jit(solution)/shard_map/reduce_scatter | solution.py:59
  900.2 31.0 %reduce-scatter.24.cloned.1.call-done = f32[4,16,1536]{2,1,0:T(8,128)} async-done(((f32[4,64,1536]{2,1,0:T(8,128)}), f32[4,16,1536]{2,1,0:T(8,128)}) %reduce-scatter.24.cloned.1.call-update) | async-done | bytes 393232 | tf_op jit(solution)/shard_map/reduce_scatter | solution.py:59
  989.0 28.7 %copy.374 = f32[2,1536,1536]{1,0,2:T(2,128)} copy(f32[2,1536,1536]{2,1,0:T(8,128)} %pad_maximum_fusion.1) | data formatting | bytes 37748736 | tf_op jit(solution)/shard_map/stack | solution.py:331
  1044.4 14.5 slice_add_fusion
  1111.1 13.6 pad_maximum_fusion.2
  1124.7 21.6 copy.372
  1159.4 16.0 convolution_bitcast_fusion.1
  1177.4 16.1 convolution_bitcast_fusion
  1200.0 189.9 %all-reduce.10.cloned.1.call-done = f32[2,1536,1536]{1,0,2:T(2,128)} async-done(((f32[2,1536,1536]{1,0,2:T(2,128)}), f32[2,1536,1536]{1,0,2:T(2,128)}) %all-reduce.10.cloned.1.call-update) | async-done | bytes 18874384
  1396.0 369.6 %all-reduce.12.cloned.1.call-done = (f32[2,3,1536,384]{3,0,1,2:T(2,128)}, f32[2,384,1536]{1,0,2:T(2,128)}) async-done(((f32[2,3,1536,384]{3,0,1,2:T(2,128)}, f32[2,384,1536]{1,0,2:T(2,128)}), (f32[2,3,1536,384]{3,0,1,2:T(2,128)}, f32[2,384,1536]{1,0,2:T(2,128)})) %all-reduce.12.cloned.1.call-update) | async-done | bytes 18874384
  1775.1 180.8 %reduce-scatter.32.cloned.1.call-done = f32[2,192,1536]{2,1,0:T(8,128)} async-done(((f32[2,1536,1536]{2,1,0:T(8,128)}), f32[2,192,1536]{2,1,0:T(8,128)}) %reduce-scatter.32.cloned.1.call-update) | async-done | bytes 2359312 | tf_op jit(solution)/shard_map/reduce_scatter | solution.py:330
  1960.1 38.4 %psum.14 = f32[]{:T(128)} all-reduce(f32[]{:T(128)S(6)} %add.414), channel_id=1, replica_groups=mesh['rows'=8,'heads'=4] {'rows','heads'}, use_global_device_ids=true, to_apply=%region_52.53 | all-reduce | flops 1 | bytes 8 | tf_op jit(solution)/shard_map/psum | solution.py:335
  1998.5 181.7 %reduce-scatter.28.cloned.1.call-done = f32[256,4,1536]{2,0,1:T(8,128)} async-done(((f32[1024,4,1536]{2,0,1:T(8,128)}), f32[256,4,1536]{2,0,1:T(8,128)}) %reduce-scatter.28.cloned.1.call-update) | async-done | bytes 6291472 | tf_op jit(solution)/shard_map/reduce_scatter | solution.py:308
  2180.2 225.3 %reduce-scatter.30.cloned.1.call-done = f32[256,4,1536]{2,0,1:T(8,128)} async-done(((f32[1024,4,1536]{2,0,1:T(8,128)}), f32[256,4,1536]{2,0,1:T(8,128)}) %reduce-scatter.30.cloned.1.call-update) | async-done | bytes 6291472 | tf_op jit(solution)/shard_map/reduce_scatter | solution.py:308
  2434.3 106.5 %all-reduce.8.cloned.1.call-done = f32[2,6,1536]{2,1,0:T(8,128)} async-done(((f32[2,6,1536]{2,1,0:T(8,128)}), f32[2,6,1536]{2,1,0:T(8,128)}) %all-reduce.8.cloned.1.call-update) | async-done | bytes 73744 | tf_op jit(solution)/shard_map/psum | solution.py:335
  (523 shorter events, 498.6 us)
Async XLA Ops:
  7.2 37.4 %all-gather.11.cloned.1.call-start = ((), (), s32[]{:S(2)}) async-start(), calls=%async_computation.13 | async-start | bytes 2654208 | tf_op jit(solution)/shard_map/all_gather | solution.py:171
  9.7 107.6 %all-gather.9.cloned.1.call-start = ((), (), s32[]{:S(2)}) async-start(), calls=%async_computation.12 | async-start | bytes 7962624 | tf_op jit(solution)/shard_map/all_gather | solution.py:170
  13.5 226.7 %all-gather.7.cloned.1.call-start = ((), (), s32[]{:S(2)}) async-start(), calls=%async_computation.11 | async-start | bytes 15728640 | tf_op jit(solution)/shard_map/all_gather | solution.py:188
  20.5 312.6 %all-gather.15.cloned.1.call-start = ((), (), s32[]{:S(2)}) async-start(), calls=%async_computation.16 | async-start | bytes 10616832 | tf_op jit(solution)/shard_map/all_gather | solution.py:173
  25.1 349.4 %reduce-scatter.12.cloned.1.call-start = ((), (), s32[]{:S(2)}) async-start(), calls=%async_computation.14 | async-start | bytes 1966080 | tf_op jit(solution)/shard_map/reduce_scatter | solution.py:51
  138.1 102.1 %copy-start.55 = (bf16[1,2,1536,384]{2,3,1,0:T(8,128)(2,1)}, bf16[1,2,1536,384]{2,3,1,0:T(8,128)(2,1)S(1)}, u32[]{:S(2)}) copy-start(bf16[1,2,1536,384]{2,3,1,0:T(8,128)(2,1)S(1)} %copy.404) | copy-start | bytes 7077892
  264.5 194.2 %all-gather.13.cloned.1.call-start = ((), (), s32[]{:S(2)}) async-start(), calls=%async_computation.15 | async-start | bytes 10616832 | tf_op jit(solution)/shard_map/all_gather | solution.py:172
  267.4 314.1 %all-gather.17.cloned.1.call-start = ((), (), s32[]{:S(2)}) async-start(), calls=%async_computation.18 | async-start | bytes 15728640 | tf_op jit(solution)/shard_map/all_gather | solution.py:188
  268.2 347.9 %reduce-scatter.14.cloned.1.call-start = ((), (), s32[]{:S(2)}) async-start(), calls=%async_computation.17 | async-start | bytes 1966080 | tf_op jit(solution)/shard_map/reduce_scatter | solution.py:51
  375.7 87.0 %copy-start.99 = (f32[4,16]{1,0:T(4,128)}, f32[4,16]{1,0:T(4,128)S(1)}, u32[]{:S(2)}) copy-start(f32[4,16]{1,0:T(4,128)S(1)} %broadcast_multiply_fusion.3) | copy-start | bytes 772
  375.9 86.8 %copy-start.119 = (f32[4,16]{1,0:T(4,128)}, f32[4,16]{1,0:T(4,128)S(1)}, u32[]{:S(2)}) copy-start(f32[4,16]{1,0:T(4,128)S(1)} %multiply_reduce_fusion.18) | copy-start | bytes 772
  375.9 86.8 %copy-start.105 = (f32[4,16]{1,0:T(4,128)}, f32[4,16]{1,0:T(4,128)S(1)}, u32[]{:S(2)}) copy-start(f32[4,16]{1,0:T(4,128)S(1)} %fusion.177) | copy-start | bytes 772
  469.4 226.4 %reduce-scatter.16.cloned.1.call-start = ((), (), s32[]{:S(2)}) async-start(), calls=%async_computation.19 | async-start | bytes 1966080 | tf_op jit(solution)/shard_map/reduce_scatter | solution.py:51
  656.8 94.9 %reduce-scatter.20.cloned.1.call-start = ((), (), s32[]{:S(2)}) async-start(), calls=%async_computation.21 | async-start | bytes 1966080 | tf_op jit(solution)/shard_map/reduce_scatter | solution.py:59
  720.6 65.6 %reduce-scatter.18.cloned.1.call-start = ((), (), s32[]{:S(2)}) async-start(), calls=%async_computation.20 | async-start | bytes 1966080 | tf_op jit(solution)/shard_map/reduce_scatter | solution.py:51
  726.2 145.4 %reduce-scatter.22.cloned.1.call-start = ((), (), s32[]{:S(2)}) async-start(), calls=%async_computation.22 | async-start | bytes 1966080 | tf_op jit(solution)/shard_map/reduce_scatter | solution.py:59
  840.5 90.7 %reduce-scatter.24.cloned.1.call-start = ((), (), s32[]{:S(2)}) async-start(), calls=%async_computation.23 | async-start | bytes 1966080 | tf_op jit(solution)/shard_map/reduce_scatter | solution.py:59
  900.1 295.3 %reduce-scatter.26.cloned.1.call-start = ((), (), s32[]{:S(2)}) async-start(), calls=%async_computation.24 | async-start | bytes 1966080 | tf_op jit(solution)/shard_map/reduce_scatter | solution.py:59
  977.4 412.5 %all-reduce.10.cloned.1.call-start = ((), (), s32[]{:S(2)}) async-start(), calls=%async_computation.29 | async-start | bytes 37748736
  1017.7 747.9 %all-reduce.12.cloned.1.call-start = ((), (), s32[]{:S(2)}) async-start(), calls=%async_computation.30 | async-start | bytes 37748736
  1146.3 809.6 %reduce-scatter.32.cloned.1.call-start = ((), (), s32[]{:S(2)}) async-start(), calls=%async_computation.27 | async-start | bytes 21233664 | tf_op jit(solution)/shard_map/reduce_scatter | solution.py:330
  1157.6 1022.6 %reduce-scatter.28.cloned.1.call-start = ((), (), s32[]{:S(2)}) async-start(), calls=%async_computation.25 | async-start | bytes 31457280 | tf_op jit(solution)/shard_map/reduce_scatter | solution.py:308
  1175.5 1230.0 %reduce-scatter.30.cloned.1.call-start = ((), (), s32[]{:S(2)}) async-start(), calls=%async_computation.26 | async-start | bytes 31457280 | tf_op jit(solution)/shard_map/reduce_scatter | solution.py:308
  1193.6 1347.3 %all-reduce.8.cloned.1.call-start = ((), (), s32[]{:S(2)}) async-start(), calls=%async_computation.28 | async-start | bytes 196608 | tf_op jit(solution)/shard_map/psum | solution.py:335
  1768.6 636.9 %copy-start.4 = (bf16[256,4,1536]{2,1,0:T(4,128)(2,1)S(1)}, bf16[256,4,1536]{2,1,0:T(4,128)(2,1)}, u32[]{:S(2)}) copy-start(bf16[256,4,1536]{2,1,0:T(4,128)(2,1)} %param.19) | copy-start | bytes 9437188
  1768.6 636.9 %copy-start.82 = (f32[1536]{0:T(1024)S(1)}, f32[1536]{0:T(1024)}, u32[]{:S(2)}) copy-start(f32[1536]{0:T(1024)} %copy-done.81) | copy-start | bytes 18436
  1768.6 636.9 %copy-start.84 = (f32[1536]{0:T(1024)S(1)}, f32[1536]{0:T(1024)}, u32[]{:S(2)}) copy-start(f32[1536]{0:T(1024)} %copy-done.83) | copy-start | bytes 18436
  1768.6 636.9 %copy-start.93 = (f32[256,4]{0,1:T(4,128)S(1)}, f32[256,4]{0,1:T(4,128)}, u32[]{:S(2)}) copy-start(f32[256,4]{0,1:T(4,128)} %copy-done.92) | copy-start | bytes 12292
  1998.5 413.1 %copy-start.102 = (f32[256,4]{0,1:T(4,128)S(1)}, f32[256,4]{0,1:T(4,128)}, u32[]{:S(2)}) copy-start(f32[256,4]{0,1:T(4,128)} %copy-done.101) | copy-start | bytes 12292
  1998.5 413.2 %copy-start.98 = (f32[256,4]{0,1:T(4,128)S(1)}, f32[256,4]{0,1:T(4,128)}, u32[]{:S(2)}) copy-start(f32[256,4]{0,1:T(4,128)} %copy-done.97) | copy-start | bytes 12292
  2434.3 116.0 %copy-start.37 = (f32[2,3,192,384]{3,2,1,0:T(8,128)S(1)}, f32[2,3,192,384]{3,2,1,0:T(8,128)}, u32[]{:S(2)}) copy-start(f32[2,3,192,384]{3,2,1,0:T(8,128)} %param.23) | copy-start | bytes 5308420
  2434.3 116.0 %copy-start.38 = (f32[2,3,192,384]{3,0,1,2:T(2,128)S(1)}, f32[2,3,192,384]{3,0,1,2:T(2,128)}, u32[]{:S(2)}) copy-start(f32[2,3,192,384]{3,0,1,2:T(2,128)} %get-tuple-element.182) | copy-start | bytes 5308420
  (125 other events, 781.3 us)
Sparse Core Ops, SparseCore 0:
  10.3 34.3 all-gather.10
  46.8 70.3 all-gather.8
  119.1 121.0 all-gather.6
  242.3 90.7 all-gather.14
  336.5 29.3 reduce-scatter.11
  367.9 90.7 all-gather.12
  460.5 120.9 all-gather.16
  585.1 30.9 reduce-scatter.13
  657.0 33.5 reduce-scatter.15
  720.8 30.9 reduce-scatter.19
  755.3 30.8 reduce-scatter.17
  840.6 30.8 reduce-scatter.21
  900.3 30.9 reduce-scatter.23
  977.5 30.8 reduce-scatter.25
  1017.8 372.1 all-reduce.9
  1392.4 373.1 all-reduce.11
  1767.8 188.0 reduce-scatter.31
  1958.9 221.2 reduce-scatter.27
  2183.6 221.8 reduce-scatter.29
  2420.3 120.5 all-reduce.7
where the time goes:
time: 2590 us; the launch traced here: 2580 us
  waiting for transfers between devices  1760 us (68%)
  local copies, waits for them, and re-layouts  294 us (11%)
  matrix products  211 us (8%)
  other arithmetic  147 us (6%)
  blocking collectives  139 us (5%)
    unnamed x22, waiting for transfers between devices  561 us
    reduce_scatter x2, waiting for transfers between devices, local(): lax.psum_scatter(jnp.einsum('tpvc,tdc->pvd', pair_slope, pair_columns, pr...  407 us
    reduce_scatter x1, waiting for transfers between devices, local(): lax.psum_scatter(jnp.stack(widen_parts[::-1]), 'rows', scatter_dimension=...  181 us
    all_gather x2, waiting for transfers between devices, local(): lax.all_gather(media_norm, 'heads', axis=0, tiled=True)  175 us
    unnamed x288, local copies, waits for them, and re-layouts  129 us
    psum x1, waiting for transfers between devices, local(): lax.psum((jnp.stack(gain_parts[::-1]), squares), ('rows', 'heads'))  107 us
    reduce_scatter x4, waiting for transfers between devices, scatter_slopes(): return lax.psum_scatter(terms, 'heads', scatter_dimension=1, tiled=True)  87.6 us
    all_gather x1, waiting for transfers between devices, local(): lax.all_gather(widen.astype(jnp.bfloat16), 'rows', axis=1, tiled=True)  67.8 us
  transfers between devices with their start and end apart: 20, of which 17 were waited for; matrix products, arithmetic and copies ran while one was open for 18% of the time, Pallas kernels for 0%

commit v1 on v0

--- a/solution.py
+++ b/solution.py
@@ -1,6 +1,10 @@
+import functools
+
 import jax
 import jax.numpy as jnp
 from jax import lax
+from jax.experimental import pallas as pl
+from jax.experimental.pallas import tpu as pltpu
 from jax.sharding import PartitionSpec as P
 
 HD = 96
@@ -137,7 +141,7 @@
     return (query_slope, jnp.stack((key_media, value_media)), jnp.stack((key_latent, value_latent)))
 
 
-def local(
+def local_plain(
     media,
     latents,
     frame_count,
@@ -354,6 +358,710 @@
     return tuple(results)
 
 
+BF = jnp.bfloat16
+F32 = jnp.float32
+VMEM_LIMIT = 60 * 1024 * 1024
+NT = (((1,), (1,)), ((), ()))
+TN = (((0,), (0,)), ((), ()))
+X_SWAP = ((0, 1), (1, 0), (2, 3), (3, 2))
+Y_SWAP = ((0, 2), (2, 0), (1, 3), (3, 1))
+
+
+def vmem_spec():
+    return pl.BlockSpec(memory_space=pltpu.VMEM)
+
+
+def mm(left, right, dims=None, out=BF):
+    dims = dims or (((1,), (0,)), ((), ()))
+    return lax.dot_general(left, right, dims, preferred_element_type=F32).astype(out)
+
+
+def media_kernel(first_ref, second_ref, gain_ref, weight_ref, *rest):
+    keys_ref, hat_ref, rows_ref = rest[-3:]
+    half, layer = pl.program_id(0), pl.program_id(1)
+
+    @pl.when(layer == 0)
+    def _():
+        @pl.when(half == 0)
+        def _():
+            rows_ref[...] = first_ref[...].astype(F32).reshape(rows_ref.shape)
+
+        @pl.when(half == 1)
+        def _():
+            rows_ref[...] = second_ref[...].astype(F32).reshape(rows_ref.shape)
+
+        rows = rows_ref[...]
+        centred = rows - jnp.mean(rows, axis=-1, keepdims=True)
+        spread = jnp.mean(centred * centred, axis=-1, keepdims=True)
+        hat = centred * lax.rsqrt(spread + EPS_NORM)
+        rows_ref[...] = hat
+        hat_ref[...] = hat.astype(BF).reshape(hat_ref.shape)
+
+    gain = gain_ref[pl.ds(layer, 1), 0]
+    shift = gain_ref[pl.ds(layer, 1), 1]
+    normed = (rows_ref[...] * gain + shift).astype(BF)
+    keys_ref[...] = jnp.dot(normed, weight_ref[...], preferred_element_type=F32).astype(BF).reshape(keys_ref.shape)
+
+
+def media_part(first, second, gains, weight, group, earlier):
+    videos, patches, width = first.shape
+    columns = weight.shape[1]
+    kinds = (
+        jax.ShapeDtypeStruct((8, videos, patches, columns), BF),
+        jax.ShapeDtypeStruct((8, videos, patches, width), BF),
+    )
+    whole = pl.BlockSpec((videos, patches, width), lambda i, j: (0, 0, 0))
+    in_specs = [
+        whole,
+        whole,
+        pl.BlockSpec(gains.shape, lambda i, j: (0, 0, 0)),
+        pl.BlockSpec((width, columns // 2), lambda i, j: (0, j)),
+    ]
+    aliases = {}
+    if earlier:
+        in_specs += [pl.BlockSpec(memory_space=pl.ANY)] * 2
+        aliases = {4: 0, 5: 1}
+    rows = videos * patches
+    return pl.pallas_call(
+        media_kernel,
+        grid=(2, 2),
+        out_shape=kinds,
+        in_specs=in_specs,
+        out_specs=(
+            pl.BlockSpec((1, videos, patches, columns // 2), lambda i, j: (2 * group + i, 0, 0, j)),
+            pl.BlockSpec((1, videos, patches, width), lambda i, j: (2 * group + i, 0, 0, 0)),
+        ),
+        scratch_shapes=[pltpu.VMEM((rows, width), F32)],
+        input_output_aliases=aliases,
+        compiler_params=pltpu.CompilerParams(vmem_limit_bytes=VMEM_LIMIT),
+        cost_estimate=pl.CostEstimate(
+            flops=4 * rows * width * columns, bytes_accessed=8 * rows * width, transcendentals=0
+        ),
+        name="media_part",
+    )(first, second, gains, weight, *earlier)
+
+
+def head_mask(rows, columns, head):
+    place = lax.broadcasted_iota(jnp.int32, (rows, columns), 1)
+    return (place >= head * HD) & (place < (head + 1) * HD)
+
+
+def spread_heads(rows):
+    heads = rows.shape[1] // HD
+    zero = jnp.zeros_like(rows)
+    return jnp.concatenate(
+        [jnp.where(head_mask(*rows.shape, head), rows, zero) for head in range(heads)], axis=0
+    )
+
+
+def gather_heads(rows, count):
+    heads = rows.shape[1] // HD
+    total = jnp.zeros((count, rows.shape[1]), F32)
+    for head in range(heads):
+        part = rows[head * count : (head + 1) * count]
+        total = total + jnp.where(head_mask(*part.shape, head), part, 0.0)
+    return total
+
+
+def attend_kernel(live_ref, query_ref, latent_key_ref, latent_value_ref, key_ref, value_ref, mixed_ref, *, scale):
+    video = pl.program_id(0)
+    slots, patches = key_ref.shape[0], key_ref.shape[2]
+    query = spread_heads(query_ref[...])
+    rows, columns = query.shape
+    place = lax.broadcasted_iota(jnp.int32, (rows, 2 * patches), 1)
+    scores = []
+    for pair in range(slots // 2):
+        keys = key_ref[2 * pair : 2 * pair + 2, 0].reshape(2 * patches, columns)
+        score = lax.dot_general(query, keys, NT, preferred_element_type=F32) * scale
+        live = jnp.where(place < patches, live_ref[video, 2 * pair], live_ref[video, 2 * pair + 1])
+        scores.append(jnp.where(live > 0, score, MASKED_SCORE))
+    scores.append(lax.dot_general(query, latent_key_ref[...], NT, preferred_element_type=F32) * scale)
+    top = functools.reduce(jnp.maximum, [jnp.max(score, axis=-1, keepdims=True) for score in scores])
+    exponents = [jnp.exp(score - top) for score in scores]
+    total = functools.reduce(jnp.add, [jnp.sum(e, axis=-1, keepdims=True) for e in exponents])
+    mixed = jnp.zeros((rows, columns), F32)
+    for pair in range(slots // 2):
+        values = value_ref[2 * pair : 2 * pair + 2, 0].reshape(2 * patches, columns)
+        mixed = mixed + jnp.dot((exponents[pair] / total).astype(BF), values, preferred_element_type=F32)
+    mixed = mixed + jnp.dot(
+        (exponents[-1] / total).astype(BF), latent_value_ref[...], preferred_element_type=F32
+    )
+    mixed_ref[...] = gather_heads(mixed, query_ref.shape[0]).astype(BF)
+
+
+def attend_fast(live, query, latent_pair, keys, layer, scale):
+    slots, videos, patches, _ = keys.shape
+    count, columns = query.shape[0] // videos, query.shape[1]
+    row_block = pl.BlockSpec((count, columns), lambda v: (v, 0))
+    return pl.pallas_call(
+        functools.partial(attend_kernel, scale=scale),
+        grid=(videos,),
+        out_shape=jax.ShapeDtypeStruct(query.shape, BF),
+        in_specs=[
+            pl.BlockSpec(memory_space=pltpu.SMEM),
+            row_block,
+            row_block,
+            pl.BlockSpec((count, columns), lambda v: (v, 1)),
+            pl.BlockSpec((slots, 1, patches, columns), lambda v: (0, v, 0, 2 * layer)),
+            pl.BlockSpec((slots, 1, patches, columns), lambda v: (0, v, 0, 2 * layer + 1)),
+        ],
+        out_specs=row_block,
+        compiler_params=pltpu.CompilerParams(vmem_limit_bytes=VMEM_LIMIT),
+        cost_estimate=pl.CostEstimate(
+            flops=8 * slots * patches * videos * count * 2 * columns,
+            bytes_accessed=4 * slots * videos * patches * columns,
+            transcendentals=slots * patches * videos * count * 4,
+        ),
+        name="attend",
+    )(live, query, latent_pair, latent_pair, keys, keys)
+
+
+def attend_back_kernel(
+    live_ref, query_ref, latent_key_ref, latent_value_ref, key_ref, value_ref, slope_ref, *rest, scale
+):
+    query_slope_ref, latent_slope_ref, media_slope_ref = rest[-3:]
+    video = pl.program_id(0)
+    slots, patches = key_ref.shape[0], key_ref.shape[2]
+    pairs = slots // 2
+    count = query_ref.shape[0]
+    query, slope = spread_heads(query_ref[...]), spread_heads(slope_ref[...])
+    rows, columns = query.shape
+    place = lax.broadcasted_iota(jnp.int32, (2 * patches, rows), 0)
+
+    def keys_of(ref, pair):
+        return ref[2 * pair : 2 * pair + 2, 0].reshape(2 * patches, columns)
+
+    scores = []
+    for pair in range(pairs):
+        score = lax.dot_general(keys_of(key_ref, pair), query, NT, preferred_element_type=F32) * scale
+        live = jnp.where(place < patches, live_ref[video, 2 * pair], live_ref[video, 2 * pair + 1])
+        scores.append(jnp.where(live > 0, score, MASKED_SCORE))
+    scores.append(lax.dot_general(latent_key_ref[...], query, NT, preferred_element_type=F32) * scale)
+    top = functools.reduce(jnp.maximum, [jnp.max(score, axis=0, keepdims=True) for score in scores])
+    exponents = [jnp.exp(score - top) for score in scores]
+    total = functools.reduce(jnp.add, [jnp.sum(e, axis=0, keepdims=True) for e in exponents])
+    shares = [e / total for e in exponents]
+    share_slopes = [
+        lax.dot_general(keys_of(value_ref, pair), slope, NT, preferred_element_type=F32)
+        for pair in range(pairs)
+    ]
+    share_slopes.append(
+        lax.dot_general(latent_value_ref[...], slope, NT, preferred_element_type=F32)
+    )
+    row_total = functools.reduce(
+        jnp.add,
+        [jnp.sum(a * b, axis=0, keepdims=True) for a, b in zip(shares, share_slopes)],
+    )
+    query_slope = jnp.zeros((rows, columns), F32)
+    for at in range(pairs + 1):
+        keys = keys_of(key_ref, at) if at < pairs else latent_key_ref[...]
+        score_slope = (shares[at] * (share_slopes[at] - row_total)).astype(BF)
+        key_slope = (jnp.dot(score_slope, query, preferred_element_type=F32) * scale).astype(BF)
+        value_slope = jnp.dot(shares[at].astype(BF), slope, preferred_element_type=F32).astype(BF)
+        query_slope = query_slope + lax.dot_general(
+            score_slope, keys, TN, preferred_element_type=F32
+        )
+        if at < pairs:
+            media_slope_ref[2 * at : 2 * at + 2, 0, :, :columns] = key_slope.reshape(2, patches, columns)
+            media_slope_ref[2 * at : 2 * at + 2, 0, :, columns:] = value_slope.reshape(2, patches, columns)
+        else:
+            latent_slope_ref[:, :columns] = key_slope
+            latent_slope_ref[:, columns:] = value_slope
+    query_slope_ref[...] = (gather_heads(query_slope, count) * scale).astype(BF)
+
+
+def attend_back_fast(live, query, latent_pair, keys, slope, layer, scale, earlier):
+    slots, videos, patches, _ = keys.shape
+    count, columns = query.shape[0] // videos, query.shape[1]
+    row_block = pl.BlockSpec((count, columns), lambda v: (v, 0))
+    in_specs = [
+        pl.BlockSpec(memory_space=pltpu.SMEM),
+        row_block,
+        row_block,
+        pl.BlockSpec((count, columns), lambda v: (v, 1)),
+        pl.BlockSpec((slots, 1, patches, columns), lambda v: (0, v, 0, 2 * layer)),
+        pl.BlockSpec((slots, 1, patches, columns), lambda v: (0, v, 0, 2 * layer + 1)),
+        row_block,
+    ]
+    aliases = {}
+    if earlier:
+        in_specs += [pl.BlockSpec(memory_space=pl.ANY)]
+        aliases = {7: 2}
+    return pl.pallas_call(
+        functools.partial(attend_back_kernel, scale=scale),
+        grid=(videos,),
+        out_shape=(
+            jax.ShapeDtypeStruct(query.shape, BF),
+            jax.ShapeDtypeStruct(latent_pair.shape, BF),
+            jax.ShapeDtypeStruct(keys.shape, BF),
+        ),
+        in_specs=in_specs,
+        out_specs=(
+            row_block,
+            pl.BlockSpec((count, 2 * columns), lambda v: (v, 0)),
+            pl.BlockSpec((slots, 1, patches, 2 * columns), lambda v: (0, v, 0, layer)),
+        ),
+        input_output_aliases=aliases,
+        compiler_params=pltpu.CompilerParams(vmem_limit_bytes=VMEM_LIMIT),
+        cost_estimate=pl.CostEstimate(
+            flops=20 * slots * patches * videos * count * 2 * columns,
+            bytes_accessed=8 * slots * videos * patches * columns,
+            transcendentals=slots * patches * videos * count * 4,
+        ),
+        name="attend_back",
+    )(live, query, latent_pair, latent_pair, keys, keys, slope, *earlier)
+
+
+def greet(count):
+    me = lax.axis_index("heads")
+    barrier = pltpu.get_barrier_semaphore()
+    for step in range(1, count):
+        pl.semaphore_signal(barrier, inc=1, device_id={"heads": (me + step) % count})
+    pl.semaphore_wait(barrier, count - 1)
+    return me
+
+
+def own_rows(ref, place, share):
+    return ref.at[:, pl.ds(pl.multiple_of(place * share, share), share), :]
+
+
+def start_gather(me, count, share, own_ref, full_ref, send_sem, recv_sem):
+    copies = []
+    for step in range(1, count):
+        copy = pltpu.make_async_remote_copy(
+            src_ref=own_ref,
+            dst_ref=own_rows(full_ref, me, share),
+            send_sem=send_sem.at[step - 1],
+            recv_sem=recv_sem.at[step - 1],
+            device_id={"heads": (me + step) % count},
+        )
+        copy.start()
+        copies.append(copy)
+    return copies
+
+
+def start_scatter(me, count, share, part_ref, landed_ref, send_sem, recv_sem):
+    copies = []
+    for step in range(1, count):
+        peer = (me + step) % count
+        copy = pltpu.make_async_remote_copy(
+            src_ref=own_rows(part_ref, peer, share),
+            dst_ref=landed_ref.at[step - 1],
+            send_sem=send_sem.at[step - 1],
+            recv_sem=recv_sem.at[step - 1],
+            device_id={"heads": peer},
+        )
+        copy.start()
+        copies.append(copy)
+    return copies
+
+
+def gather_kernel(count, arrays, *refs):
+    own, full = refs[:arrays], refs[arrays : 2 * arrays]
+    sems = refs[2 * arrays :]
+    me = greet(count)
+    share = own[0].shape[1]
+    copies = []
+    for at in range(arrays):
+        copies += start_gather(me, count, share, own[at], full[at], sems[2 * at], sems[2 * at + 1])
+        full[at][:, pl.ds(pl.multiple_of(me * share, share), share), :] = own[at][...]
+    for copy in copies:
+        copy.wait()
+
+
+def gather_fast(arrays, count):
+    videos, share, width = arrays[0].shape
+    kind = jax.ShapeDtypeStruct((videos, share * count, width), arrays[0].dtype)
+    number = len(arrays)
+    return pl.pallas_call(
+        functools.partial(gather_kernel, count, number),
+        out_shape=(kind,) * number,
+        in_specs=[vmem_spec()] * number,
+        out_specs=(vmem_spec(),) * number,
+        scratch_shapes=[pltpu.SemaphoreType.DMA((count - 1,))] * (2 * number),
+        compiler_params=pltpu.CompilerParams(
+            collective_id=1, has_side_effects=True, vmem_limit_bytes=VMEM_LIMIT
+        ),
+        cost_estimate=pl.CostEstimate(flops=0, bytes_accessed=30 * 1000 * 1000, transcendentals=0),
+        name="gather_latents",
+    )(*arrays)
+
+
+def forward_kernel(
+    count, last, part_ref, rest_ref, gain_ref, new_ref, *refs
+):
+    refs = list(refs)
+    full_ref = None if last else refs.pop(0)
+    landed_ref, own_ref, send_sem, recv_sem, send_more, recv_more = refs
+    me = greet(count)
+    share = rest_ref.shape[1]
+    copies = start_scatter(me, count, share, part_ref, landed_ref, send_sem, recv_sem)
+    mine = pl.ds(pl.multiple_of(me * share, share), share)
+    total = rest_ref[...] + part_ref[:, mine, :].astype(F32)
+    for step, copy in enumerate(copies):
+        copy.wait_recv()
+        total = total + landed_ref[step].astype(F32)
+    new_ref[...] = total
+    if not last:
+        own_ref[...] = layer_norm(total, gain_ref[0], gain_ref[1]).astype(BF)
+        more = start_gather(me, count, share, own_ref, full_ref, send_more, recv_more)
+        full_ref[:, mine, :] = own_ref[...]
+        for copy in more:
+            copy.wait()
+    for copy in copies:
+        copy.wait_send()
+
+
+def forward_exchange(part, rest, gain, count, last=False):
+    videos, share, width = rest.shape
+    outs = [jax.ShapeDtypeStruct(rest.shape, F32)]
+    if not last:
+        outs.append(jax.ShapeDtypeStruct(part.shape, BF))
+    got = pl.pallas_call(
+        functools.partial(forward_kernel, count, last),
+        out_shape=tuple(outs),
+        in_specs=[vmem_spec()] * 3,
+        out_specs=(vmem_spec(),) * len(outs),
+        scratch_shapes=[
+            pltpu.VMEM((count - 1, videos, share, width), BF),
+            pltpu.VMEM((videos, share, width), BF),
+        ]
+        + [pltpu.SemaphoreType.DMA((count - 1,))] * 4,
+        compiler_params=pltpu.CompilerParams(
+            collective_id=3 if last else 2, has_side_effects=True, vmem_limit_bytes=VMEM_LIMIT
+        ),
+        cost_estimate=pl.CostEstimate(flops=0, bytes_accessed=50 * 1000 * 1000, transcendentals=0),
+        name="forward_exchange",
+    )(part, rest, gain)
+    return got if not last else (got[0], None)
+
+
+def backward_kernel(
+    count, last, part_ref, rows_ref, rest_ref, gain_ref, new_ref, sums_ref, *refs
+):
+    refs = list(refs)
+    full_ref = None if last else refs.pop(0)
+    landed_ref, own_ref, send_sem, recv_sem, send_more, recv_more = refs
+    me = greet(count)
+    share = rest_ref.shape[1]
+    copies = start_scatter(me, count, share, part_ref, landed_ref, send_sem, recv_sem)
+    mine = pl.ds(pl.multiple_of(me * share, share), share)
+    rows = rows_ref[...]
+    centred = rows - jnp.mean(rows, axis=-1, keepdims=True)
+    scale = lax.rsqrt(jnp.mean(centred * centred, axis=-1, keepdims=True) + EPS_NORM)
+    hat = centred * scale
+    slope = part_ref[:, mine, :].astype(F32)
+    for step, copy in enumerate(copies):
+        copy.wait_recv()
+        slope = slope + landed_ref[step].astype(F32)
+    hat_slope = slope * gain_ref[0]
+    back = hat_slope - jnp.mean(hat_slope, axis=-1, keepdims=True)
+    back = back - hat * jnp.mean(hat_slope * hat, axis=-1, keepdims=True)
+    new = rest_ref[...] + back * scale
+    new_ref[...] = new
+    if not last:
+        own_ref[...] = new.astype(BF)
+        more = start_gather(me, count, share, own_ref, full_ref, send_more, recv_more)
+        full_ref[:, mine, :] = own_ref[...]
+    sums_ref[0:1] = jnp.sum(jnp.sum(slope * hat, axis=0), axis=0, keepdims=True)
+    sums_ref[1:2] = jnp.sum(jnp.sum(slope, axis=0), axis=0, keepdims=True)
+    if not last:
+        for copy in more:
+            copy.wait()
+    for copy in copies:
+        copy.wait_send()
+
+
+def backward_exchange(part, rows, rest, gain, count, last=False):
+    videos, share, width = rest.shape
+    outs = [jax.ShapeDtypeStruct(rest.shape, F32), jax.ShapeDtypeStruct((2, width), F32)]
+    if not last:
+        outs.append(jax.ShapeDtypeStruct(part.shape, BF))
+    got = pl.pallas_call(
+        functools.partial(backward_kernel, count, last),
+        out_shape=tuple(outs),
+        in_specs=[vmem_spec()] * 4,
+        out_specs=(vmem_spec(),) * len(outs),
+        scratch_shapes=[
+            pltpu.VMEM((count - 1, videos, share, width), BF),
+            pltpu.VMEM((videos, share, width), BF),
+        ]
+        + [pltpu.SemaphoreType.DMA((count - 1,))] * 4,
+        compiler_params=pltpu.CompilerParams(
+            collective_id=5 if last else 4, has_side_effects=True, vmem_limit_bytes=VMEM_LIMIT
+        ),
+        cost_estimate=pl.CostEstimate(flops=0, bytes_accessed=50 * 1000 * 1000, transcendentals=0),
+        name="backward_exchange",
+    )(part, rows, rest, gain)
+    return got if not last else (*got, None)
+
+
+def sum_kernel(heads, rows, term_ref, out_ref, plane_ref, line_ref, send_sem, recv_sem, send_more, recv_more):
+    me_head, me_row = lax.axis_index("heads"), lax.axis_index("rows")
+    barrier = pltpu.get_barrier_semaphore()
+    for step in range(1, heads):
+        pl.semaphore_signal(barrier, inc=1, device_id={"heads": (me_head + step) % heads})
+    for step in range(1, rows):
+        pl.semaphore_signal(barrier, inc=1, device_id={"rows": (me_row + step) % rows})
+    pl.semaphore_wait(barrier, heads - 1 + rows - 1)
+
+    def spread(axis, me, count, source, slots_ref, send, recv):
+        copies = []
+        for step in range(1, count):
+            copy = pltpu.make_async_remote_copy(
+                src_ref=source,
+                dst_ref=slots_ref.at[me],
+                send_sem=send.at[step - 1],
+                recv_sem=recv.at[step - 1],
+                device_id={axis: (me + step) % count},
+            )
+            copy.start()
+            copies.append(copy)
+        slots_ref[pl.ds(me, 1)] = source[...][None]
+        for copy in copies:
+            copy.wait()
+        total = slots_ref[0]
+        for at in range(1, count):
+            total = total + slots_ref[at]
+        return total
+
+    out_ref[...] = spread("heads", me_head, heads, term_ref, plane_ref, send_sem, recv_sem)
+    total = spread("rows", me_row, rows, out_ref, line_ref, send_more, recv_more)
+    out_ref[...] = total
+
+
+def sum_fast(term, heads, rows, identity):
+    return pl.pallas_call(
+        functools.partial(sum_kernel, heads, rows),
+        out_shape=jax.ShapeDtypeStruct(term.shape, F32),
+        in_specs=[vmem_spec()],
+        out_specs=vmem_spec(),
+        scratch_shapes=[
+            pltpu.VMEM((heads, *term.shape), F32),
+            pltpu.VMEM((rows, *term.shape), F32),
+            pltpu.SemaphoreType.DMA((heads - 1,)),
+            pltpu.SemaphoreType.DMA((heads - 1,)),
+            pltpu.SemaphoreType.DMA((rows - 1,)),
+            pltpu.SemaphoreType.DMA((rows - 1,)),
+        ],
+        compiler_params=pltpu.CompilerParams(
+            collective_id=identity, has_side_effects=True, vmem_limit_bytes=VMEM_LIMIT
+        ),
+        cost_estimate=pl.CostEstimate(flops=0, bytes_accessed=20 * 1000 * 1000, transcendentals=0),
+        name="sum_over_all",
+    )(term)
+
+
+def flat(rows):
+    return rows.reshape(-1, rows.shape[-1])
+
+
+def local_fast(
+    media,
+    latents,
+    frame_count,
+    cotangent,
+    inward,
+    inward_first,
+    inward_second,
+    outward,
+    outward_first,
+    outward_second,
+    widen,
+    widen_first,
+    widen_second,
+    narrow,
+    narrow_first,
+    narrow_second,
+    norm_gains,
+    gain_first,
+    gain_second,
+):
+    heads_count, rows_count = lax.axis_size("heads"), lax.axis_size("rows")
+    me = lax.axis_index("heads")
+    layers, _, row_share, head_columns = inward.shape
+    local_positions, videos, width = media.shape
+    latent_count = latents.shape[1] * heads_count
+    scale = HD ** (-0.5)
+
+    def swap_x(rows):
+        return lax.ppermute(rows, "heads", X_SWAP)
+
+    def swap_y(rows):
+        return lax.ppermute(rows, "heads", Y_SWAP)
+
+    def gather_rows(rows):
+        return lax.all_gather(rows, "rows", axis=0, tiled=True)
+
+    outward_t, narrow_t = (jnp.swapaxes(outward, 1, 2), jnp.swapaxes(narrow, 1, 2))
+    pair_weights = gather_rows(
+        jnp.concatenate([inward[l, t].astype(BF) for l in range(layers) for t in (1, 2)], axis=1)
+    )
+    query_out, widen_full, narrow_full = [], [], []
+    for layer in range(layers):
+        query_out.append(
+            gather_rows(jnp.concatenate((inward[layer, 0], outward_t[layer]), axis=1).astype(BF))
+        )
+        widen_full.append(gather_rows(widen[layer].astype(BF)))
+        narrow_full.append(gather_rows(narrow_t[layer].astype(BF)))
+
+    own = jnp.swapaxes(media, 0, 1).reshape(videos, 2, local_positions // 2, width)
+    own = (own[:, 0], own[:, 1])
+    from_x = (swap_x(own[0]), swap_x(own[1]))
+    from_y = (swap_y(own[0]), swap_y(own[1]))
+    from_far = (swap_x(from_y[0]), swap_y(from_x[1]))
+    frames = jnp.stack([2 * (me ^ group) + half for group in range(4) for half in range(2)])
+    live = (frames[None, :] < frame_count[:, None]).astype(jnp.int32)
+    made = ()
+    media_gains = norm_gains[:, 0:2]
+    for group, parts in enumerate((own, from_x, from_y, from_far)):
+        made = media_part(parts[0], parts[1], media_gains, pair_weights, group, made)
+    keys, media_hat = made
+
+    latent = latents
+    normed = layer_norm(latent, norm_gains[0, 2], norm_gains[0, 3]).astype(BF)
+    latent_norm, feed_slope = gather_fast((normed, cotangent.astype(BF)), heads_count)
+    kept = []
+    for layer in range(layers):
+        query_weight, out_weight = query_out[layer][:, :head_columns], query_out[layer][:, head_columns:]
+        pair_weight = pair_weights[:, 2 * layer * head_columns : 2 * (layer + 1) * head_columns]
+        query = mm(flat(latent_norm), query_weight)
+        latent_pair = mm(flat(latent_norm), pair_weight)
+        mixed = attend_fast(live, query, latent_pair, keys, layer, scale)
+        part = mm(mixed, out_weight, NT).reshape(videos, latent_count, width)
+        middle, feed_norm = forward_exchange(part, latent, norm_gains[layer, 4:6], heads_count)
+        hidden_pre = mm(flat(feed_norm), widen_full[layer], None, F32)
+        hidden = jax.nn.gelu(hidden_pre).astype(BF)
+        part = mm(hidden, narrow_full[layer], NT).reshape(videos, latent_count, width)
+        last = layer == layers - 1
+        gain = norm_gains[0 if last else layer + 1, 2:4]
+        kept.append((latent, middle, latent_norm, query, latent_pair, mixed, feed_norm, hidden_pre, hidden))
+        latent, latent_norm = forward_exchange(part, middle, gain, heads_count, last)
+
+    slope = cotangent
+    gain_parts = [None] * layers
+    shares = [None] * layers
+    media_slopes = ()
+
+    def scatter_rows(gradient):
+        return lax.psum_scatter(gradient, "rows", scatter_dimension=0, tiled=True)
+
+    for layer in reversed(range(layers)):
+        latent_in, middle, latent_norm, query, latent_pair, mixed, feed_norm, hidden_pre, hidden = kept[layer]
+        query_weight, out_weight = query_out[layer][:, :head_columns], query_out[layer][:, head_columns:]
+        pair_weight = pair_weights[:, 2 * layer * head_columns : 2 * (layer + 1) * head_columns]
+        feed_slope = flat(feed_slope)
+        narrow_grad = scatter_rows(mm(feed_slope, hidden, TN))
+        hidden_slope = mm(feed_slope, narrow_full[layer], None, F32)
+        _, gelu_back = jax.vjp(jax.nn.gelu, hidden_pre)
+        pre_slope = gelu_back(hidden_slope)[0].astype(BF)
+        part = mm(pre_slope, widen_full[layer], NT).reshape(videos, latent_count, width)
+        middle_slope, feed_sums, branch_slope = backward_exchange(
+            part, middle, slope, norm_gains[layer, 4:6], heads_count
+        )
+        widen_grad = scatter_rows(mm(flat(feed_norm), pre_slope, TN))
+        branch_slope = flat(branch_slope)
+        mixed_slope = mm(branch_slope, out_weight)
+        out_grad = mm(branch_slope, mixed, TN)
+        query_slope, latent_slopes, media_slopes = attend_back_fast(
+            live, query, latent_pair, keys, mixed_slope, layer, scale, (media_slopes,) if layer < layers - 1 else ()
+        )
+        part = (mm(query_slope, query_weight, NT, F32) + mm(latent_slopes, pair_weight, NT, F32)).astype(BF)
+        part = part.reshape(videos, latent_count, width)
+        last = layer == 0
+        slope, latent_sums, feed_slope = backward_exchange(
+            part, latent_in, middle_slope, norm_gains[layer, 2:4], heads_count, last
+        )
+        query_grad = mm(flat(latent_norm), query_slope, TN)
+        pair_slope = flat(media_slopes[..., 2 * layer * head_columns : 2 * (layer + 1) * head_columns])
+        hat_grad = mm(flat(media_hat), pair_slope, TN, F32)
+        slope_sum = jnp.sum(pair_slope.astype(F32), axis=0)
+        gain, shift = norm_gains[layer, 0], norm_gains[layer, 1]
+        pair_grad = (
+            mm(flat(latent_norm), latent_slopes, TN, F32)
+            + gain[:, None] * hat_grad
+            + shift[:, None] * slope_sum[None, :]
+        ).astype(BF)
+        wide = pair_weight.astype(F32)
+        media_sums = jnp.stack(
+            (jnp.sum(wide * hat_grad, axis=1), jnp.sum(wide * slope_sum[None, :], axis=1))
+        )
+        inward_grad = scatter_rows(jnp.concatenate((out_grad, query_grad, pair_grad), axis=1))
+        shares[layer] = (narrow_grad, widen_grad, inward_grad)
+        gain_parts[layer] = jnp.concatenate((media_sums, latent_sums, feed_sums), axis=0)
+
+    scaled = jnp.concatenate(
+        [
+            (
+                pair_weights[:, 2 * l * head_columns : 2 * (l + 1) * head_columns].astype(F32)
+                * norm_gains[l, 0][:, None]
+            ).astype(BF)
+            for l in range(layers)
+        ],
+        axis=1,
+    )
+
+    def hat_slope(group, half):
+        return mm(flat(media_slopes[2 * group + half]), scaled, NT).reshape(videos, -1, width)
+
+    over_x = swap_x(hat_slope(3, 0))
+    over_y = swap_y(hat_slope(3, 1))
+    back = [hat_slope(0, 0).astype(F32), hat_slope(0, 1).astype(F32)]
+    in_x = [swap_x(hat_slope(1, 0)), None]
+    in_y = [None, swap_y(hat_slope(2, 1))]
+    in_x[1] = swap_x(hat_slope(1, 1) + over_y)
+    in_y[0] = swap_y(hat_slope(2, 0) + over_x)
+    pieces = []
+    for half in range(2):
+        total = back[half] + in_x[half].astype(F32) + in_y[half].astype(F32)
+        rows = own[half].astype(F32)
+        centred = rows - jnp.mean(rows, axis=-1, keepdims=True)
+        spread = lax.rsqrt(jnp.mean(centred * centred, axis=-1, keepdims=True) + EPS_NORM)
+        hat = centred * spread
+        total = total - jnp.mean(total, axis=-1, keepdims=True) - hat * jnp.mean(total * hat, axis=-1, keepdims=True)
+        pieces.append(jnp.swapaxes(total * spread, 0, 1))
+    media_slope = jnp.concatenate(pieces, axis=0)
+
+    gain_total = sum_fast(jnp.concatenate(gain_parts, axis=0), heads_count, rows_count, 6)
+    gain_total = gain_total.reshape(layers, 6, width)
+    squares = jnp.zeros((), F32)
+    for share in shares:
+        for piece in share:
+            wide = piece.astype(F32)
+            squares = squares + jnp.sum(wide * wide)
+    square_total = sum_fast(jnp.full((8, 128), squares, F32), heads_count, rows_count, 7)[0, 0]
+    gradient_norm = jnp.sqrt(square_total + jnp.sum(gain_total * gain_total))
+    factor = CLIP_LEVEL / jnp.maximum(gradient_norm, CLIP_LEVEL)
+
+    def wide_part(index, begin, end):
+        return jnp.stack([share[index][:, begin:end] for share in shares]).astype(F32)
+
+    columns = head_columns
+    inward_grad = jnp.stack(
+        [
+            jnp.stack([share[2][:, (1 + t) * columns : (2 + t) * columns] for t in range(3)])
+            for share in shares
+        ]
+    ).astype(F32)
+    table = (
+        (inward, inward_first, inward_second, inward_grad, RATE_INWARD),
+        (outward, outward_first, outward_second, jnp.swapaxes(wide_part(2, 0, columns), 1, 2), RATE_OUTWARD),
+        (widen, widen_first, widen_second, wide_part(1, 0, None), RATE_WIDEN),
+        (narrow, narrow_first, narrow_second, jnp.swapaxes(wide_part(0, 0, None), 1, 2), RATE_NARROW),
+    )
+    results = [latent, slope, media_slope, gradient_norm]
+    for weight, first, second, gradient, rate in table:
+        mean_new, square_new, weight_new = adam_step(
+            weight, first, second, gradient * factor, rate, WEIGHT_DECAY
+        )
+        results = results + [mean_new, square_new, weight_new, weight_new.astype(BF)]
+    mean_new, square_new, weight_new = adam_step(
+        norm_gains, gain_first, gain_second, gain_total * factor, RATE_GAINS, 0.0
+    )
+    results = results + [mean_new, square_new, weight_new, gain_total[:, 4:6]]
+    return tuple(results)
+
+
 def solution(mesh):
     placed = (
         P("heads", "rows", None),
@@ -376,6 +1084,7 @@
         P(),
         P(),
     )
+    local = local_fast if (mesh.shape["rows"], mesh.shape["heads"]) == (8, 4) else local_plain
     return jax.shard_map(
         local,
         mesh=mesh,

time: 2590 us -> 855 us (0.33)
  waiting for transfers between devices: 1760 us -> 120 us
  Pallas kernels: 0 us -> 419 us
  local copies, waits for them, and re-layouts: 294 us -> 53.5 us
  blocking collectives: 139 us -> 0 us
  other arithmetic: 147 us -> 64.8 us
  matrix products: 211 us -> 157 us
    reduce_scatter x11 -> x6, waiting for transfers between devices: 724 us -> 0.09 us  [scatter_rows(): return lax.psum_scatter(gradient, 'rows', scatter_dimension=0, tiled=True)]
    unnamed x22 -> x13, waiting for transfers between devices: 561 us -> 1.4 us
    pallas_call x0 -> x19, Pallas kernels: none -> 419 us  [the longest x4 113 us: forward_exchange(): pl.pallas_call(functools.partial(forward_kernel, count, last), out_shape=...]
    all_gather x6 -> x7, waiting for transfers between devices: 372 us -> 61.5 us  [gather_rows(): return lax.all_gather(rows, 'rows', axis=0, tiled=True)]
    psum x1 -> x0, waiting for transfers between devices: 107 us -> none  [local(): lax.psum((jnp.stack(gain_parts[::-1]), squares), ('rows', 'heads'))]
    all_gather x8 -> x0, blocking collectives: 101 us -> none  [the longest x4 51 us: gather_slots(): return lax.all_gather(rows, 'heads', axis=1, tiled=True)]
    unnamed x288 -> x165, local copies, waits for them, and re-layouts: 129 us -> 31 us
    another operation x27 -> x7, local copies, waits for them, and re-layouts: 83.6 us -> 1.36 us  [the longest x2 1.25 us: wide_part(): jnp.stack([share[index][:, begin:end] for share in shares]).astype(F32)]
  transfers between devices with their start and end apart: 20 -> 25, of which waited for: 17 -> 4; matrix products, arithmetic and copies ran while one was open for 18% -> 26% of each run, Pallas kernels for 0% -> 40%
where the time goes in v1:
time: 855 us; the launch traced here: 849 us
  Pallas kernels  419 us (49%)
  matrix products  157 us (18%)
  waiting for transfers between devices  120 us (14%)
  other arithmetic  64.8 us (8%)
  local copies, waits for them, and re-layouts  53.5 us (6%)
  between operations  21.8 us (3%)
  starting transfers between devices  13.6 us (2%)
    dot_general x40, matrix products, mm(): lax.dot_general(left, right, dims, preferred_element_type=F32).astype(out)  157 us
    pallas_call x4, Pallas kernels, forward_exchange(): pl.pallas_call(functools.partial(forward_kernel, count, last), out_shape=...  113 us
    pallas_call x4, Pallas kernels, backward_exchange(): pl.pallas_call(functools.partial(backward_kernel, count, last), out_shape...  84.7 us
    pallas_call x1, Pallas kernels, gather_fast(): pl.pallas_call(functools.partial(gather_kernel, count, number), out_shape...  81.3 us
    all_gather x7, waiting for transfers between devices, gather_rows(): return lax.all_gather(rows, 'rows', axis=0, tiled=True)  61.5 us
    ppermute x6, waiting for transfers between devices, swap_y(): return lax.ppermute(rows, 'heads', Y_SWAP)  57.1 us
    pallas_call x2, Pallas kernels, sum_fast(): pl.pallas_call(functools.partial(sum_kernel, heads, rows), out_shape=jax....  50.8 us
    pallas_call x4, Pallas kernels, media_part(): pl.pallas_call(media_kernel, grid=(2, 2), out_shape=kinds, in_specs=in_sp...  48.9 us
  transfers between devices with their start and end apart: 25, of which 4 were waited for; matrix products, arithmetic and copies ran while one was open for 26% of the time, Pallas kernels for 40%

profile of v1, /device:TPU:0, one launch (start us, length us, event | category | flops | bytes accessed | tf_op | source)
XLA Modules:
  0.0 848.9 jit_solution(15747972808675411603)
XLA Ops:
  30.3 81.3 %gather_latents.1 = (bf16[4,64,1536]{2,1,0:T(8,128)(2,1)}, bf16[4,64,1536]{2,1,0:T(8,128)(2,1)}) custom-call(bf16[4,16,1536]{2,1,0:T(8,128)(2,1)} %add_convert_fusion.refs_0_, bf16[4,16,1536]{2,1,0:T(8,128)(2,1)} %convert_element_type.247.refs_1_), custom_call_target="tpu_custom_call" | custom-call | bytes 30000000 | tf_op jit(solution)/shard_map/gather_latents/pallas_call | solution.py:676
  119.8 12.3 %media_part.4 = (bf16[8,4,128,1536]{3,2,1,0:T(8,128)(2,1)}, bf16[8,4,128,1536]{3,2,1,0:T(8,128)(2,1)}) custom-call(bf16[4,128,1536]{2,1,0:T(8,128)(2,1)} %get-tuple-element.187.first_ref, bf16[4,128,1536]{2,1,0:T(8,128)(2,1)} %get-tuple-element.186.second_ref, f32[2,2,1536]{2,1,0:T(2,128)} %slice.240.gain_ref, ...), custom_call_target="tpu_custom_call" | custom-call | flops 4831838208 | bytes 6291456 | tf_op jit(solution)/shard_map/media_part/pallas_call | solution.py:425
  132.1 12.1 %media_part.5 = (bf16[8,4,128,1536]{3,2,1,0:T(8,128)(2,1)}, bf16[8,4,128,1536]{3,2,1,0:T(8,128)(2,1)}) custom-call(bf16[4,128,1536]{2,1,0:T(8,128)(2,1)} %collective-permute-done.5.first_ref, bf16[4,128,1536]{2,1,0:T(8,128)(2,1)} %copy-done.27, f32[2,2,1536]{2,1,0:T(2,128)} %slice.240.gain_ref, ...), custom_call_target="tpu_custom_call", output_to_operand_aliasing={{0}: (4, {}), {1}: (5, {})} | custom-call | flops 4831838208 | bytes 6291456 | tf_op jit(solution)/shard_map/media_part/pallas_call | solution.py:425
  144.2 12.2 %media_part.6 = (bf16[8,4,128,1536]{3,2,1,0:T(8,128)(2,1)}, bf16[8,4,128,1536]{3,2,1,0:T(8,128)(2,1)}) custom-call(bf16[4,128,1536]{2,1,0:T(8,128)(2,1)} %collective-permute-done.first_ref, bf16[4,128,1536]{2,1,0:T(8,128)(2,1)} %collective-permute-done.4.second_ref, f32[2,2,1536]{2,1,0:T(2,128)} %slice.240.gain_ref, ...), custom_call_target="tpu_custom_call", output_to_operand_aliasing={{0}: (4, {}), {1}: (5, {})} | custom-call | flops 4831838208 | bytes 6291456 | tf_op jit(solution)/shard_map/media_part/pallas_call | solution.py:425
  156.4 12.2 %media_part.7 = (bf16[8,4,128,1536]{3,2,1,0:T(8,128)(2,1)}, bf16[8,4,128,1536]{3,2,1,0:T(8,128)(2,1)}) custom-call(bf16[4,128,1536]{2,1,0:T(8,128)(2,1)} %collective-permute-done.1.first_ref, bf16[4,128,1536]{2,1,0:T(8,128)(2,1)} %collective-permute-done.3.second_ref, f32[2,2,1536]{2,1,0:T(2,128)} %slice.240.gain_ref, ...), custom_call_target="tpu_custom_call", output_to_operand_aliasing={{0}: (4, {}), {1}: (5, {})} | custom-call | flops 4831838208 | bytes 6291456 | tf_op jit(solution)/shard_map/media_part/pallas_call | solution.py:425
  168.6 7.7 attend.2
  178.8 22.0 %forward_exchange.4 = (f32[4,16,1536]{2,1,0:T(8,128)}, bf16[4,64,1536]{2,1,0:T(8,128)(2,1)}) custom-call(bf16[4,64,1536]{2,1,0:T(8,128)(2,1)} %bitcast.289, f32[4,16,1536]{2,1,0:T(8,128)} %rows_ref.1, f32[2,1536]{1,0:T(2,128)} %get-tuple-element.211.gain_ref), custom_call_target="tpu_custom_call" | custom-call | bytes 50000000 | tf_op jit(solution)/shard_map/forward_exchange/pallas_call | solution.py:720
  204.8 5.3 fusion.57
  210.1 23.7 %forward_exchange.5 = (f32[4,16,1536]{2,1,0:T(8,128)}, bf16[4,64,1536]{2,1,0:T(8,128)(2,1)}) custom-call(bf16[4,64,1536]{2,1,0:T(8,128)(2,1)} %bitcast.287, f32[4,16,1536]{2,1,0:T(8,128)} %get-tuple-element.66.rest_ref.rows_ref, f32[2,1536]{1,0:T(2,128)} %get-tuple-element.210.gain_ref), custom_call_target="tpu_custom_call" | custom-call | bytes 50000000 | tf_op jit(solution)/shard_map/forward_exchange/pallas_call | solution.py:720
  242.3 7.8 attend.3
  252.5 25.6 %forward_exchange.6 = (f32[4,16,1536]{2,1,0:T(8,128)}, bf16[4,64,1536]{2,1,0:T(8,128)(2,1)}) custom-call(bf16[4,64,1536]{2,1,0:T(8,128)(2,1)} %bitcast.288, f32[4,16,1536]{2,1,0:T(8,128)} %get-tuple-element.68.rest_ref.rows_ref, f32[2,1536]{1,0:T(2,128)} %get-tuple-element.209.gain_ref), custom_call_target="tpu_custom_call" | custom-call | bytes 50000000 | tf_op jit(solution)/shard_map/forward_exchange/pallas_call | solution.py:720
  278.0 11.2 %all-gather.22.cloned.1.call-done = bf16[1,1536,1536]{2,1,0:T(8,128)(2,1)} async-done(((bf16[1,192,1536]{2,1,0:T(8,128)(2,1)}), bf16[1,1536,1536]{2,1,0:T(8,128)(2,1)}) %all-gather.22.cloned.1.call-update) | async-done | bytes 4718608 | tf_op jit(solution)/shard_map/all_gather | solution.py:894
  294.4 47.6 %all-gather.24.cloned.1.call-done = bf16[1,1536,1536]{2,1,0:T(8,128)(2,1)} async-done(((bf16[1,192,1536]{2,1,0:T(8,128)(2,1)}), bf16[1,1536,1536]{2,1,0:T(8,128)(2,1)}) %all-gather.24.cloned.1.call-update) | async-done | bytes 4718608 | tf_op jit(solution)/shard_map/all_gather | solution.py:894
  349.4 25.8 %backward_exchange.4 = (f32[4,16,1536]{2,1,0:T(8,128)}, f32[2,1536]{1,0:T(2,128)}, bf16[4,64,1536]{2,1,0:T(8,128)(2,1)}) custom-call(bf16[4,64,1536]{2,1,0:T(8,128)(2,1)} %bitcast.286, f32[4,16,1536]{2,1,0:T(8,128)} %get-tuple-element.70.rest_ref.rows_ref, f32[4,16,1536]{2,1,0:T(8,128)} %rest_ref.3, f32[2,1536]{1,0:T(2,128)} %get-tuple-element.209.gain_ref), custom_call_target="tpu_custom_call" | custom-call | bytes 50000000 | tf_op jit(solution)/shard_map/backward_exchange/pallas_call | solution.py:780
  377.5 12.2 %attend_back.2 = (bf16[256,384]{1,0:T(8,128)(2,1)}, bf16[256,768]{1,0:T(8,128)(2,1)}, bf16[8,4,128,1536]{3,2,1,0:T(8,128)(2,1)}) custom-call(s32[4,8]{1,0:T(4,128)} %compare_convert_fusion.live_ref, bf16[256,384]{1,0:T(8,128)(2,1)} %convolution_convert_fusion.22.query_ref, bf16[256,768]{1,0:T(8,128)(2,1)} %convolution_convert_fusion.18.latent_key_ref.latent_value_ref, ...), custom_call_target="tpu_custom_call" | custom-call | flops 4026531840 | bytes 12582912 | tf_op jit(solution)/shard_map/attend_back/pallas_call | solution.py:590
  393.9 23.6 %backward_exchange.5 = (f32[4,16,1536]{2,1,0:T(8,128)}, f32[2,1536]{1,0:T(2,128)}, bf16[4,64,1536]{2,1,0:T(8,128)(2,1)}) custom-call(bf16[4,64,1536]{2,1,0:T(8,128)(2,1)} %bitcast.261, f32[4,16,1536]{2,1,0:T(8,128)} %get-tuple-element.68.rest_ref.rows_ref, f32[4,16,1536]{2,1,0:T(8,128)} %get-tuple-element.75.rest_ref, f32[2,1536]{1,0:T(2,128)} %get-tuple-element.210.gain_ref), custom_call_target="tpu_custom_call" | custom-call | bytes 50000000 | tf_op jit(solution)/shard_map/backward_exchange/pallas_call | solution.py:780
  417.5 5.4 convolution_convert_fusion.3
  431.8 11.0 %copy.134.rest_0_ = bf16[8,4,128,1536]{3,2,1,0:T(8,128)(2,1)} copy(bf16[8,4,128,1536]{3,2,1,0:T(8,128)(2,1)} %get-tuple-element.79) | data formatting | bytes 25165824
  447.5 24.0 %backward_exchange.6 = (f32[4,16,1536]{2,1,0:T(8,128)}, f32[2,1536]{1,0:T(2,128)}, bf16[4,64,1536]{2,1,0:T(8,128)(2,1)}) custom-call(bf16[4,64,1536]{2,1,0:T(8,128)(2,1)} %bitcast.285, f32[4,16,1536]{2,1,0:T(8,128)} %get-tuple-element.66.rest_ref.rows_ref, f32[4,16,1536]{2,1,0:T(8,128)} %get-tuple-element.77.rest_ref, f32[2,1536]{1,0:T(2,128)} %get-tuple-element.211.gain_ref), custom_call_target="tpu_custom_call" | custom-call | bytes 50000000 | tf_op jit(solution)/shard_map/backward_exchange/pallas_call | solution.py:780
  476.1 11.9 %attend_back.3 = (bf16[256,384]{1,0:T(8,128)(2,1)}, bf16[256,768]{1,0:T(8,128)(2,1)}, bf16[8,4,128,1536]{3,2,1,0:T(8,128)(2,1)}) custom-call(s32[4,8]{1,0:T(4,128)} %compare_convert_fusion.live_ref, bf16[256,384]{1,0:T(8,128)(2,1)} %convolution_convert_fusion.23.query_ref, ...), custom_call_target="tpu_custom_call", output_to_operand_aliasing={{2}: (7, {})} | custom-call | flops 4026531840 | bytes 12582912 | tf_op jit(solution)/shard_map/attend_back/pallas_call | solution.py:590
  489.5 6.1 convert_reduce_fusion
  495.6 16.5 %fusion = f32[1536,768,1,1]{1,0,3,2:T(8,128)} fusion(bf16[8,4,128,1536]{3,2,1,0:T(8,128)(2,1)} %get-tuple-element.85, bf16[8,4,128,1536]{3,2,1,0:T(8,128)(2,1)} %get-tuple-element.79), kind=kOutput, calls=%fused_computation.13 | convolution fusion | flops 9663676416 | bytes 23592960 | tf_op jit(solution)/shard_map/dot_general | solution.py:376
  512.1 20.3 %fusion.9 = (f32[1536]{0:T(1024)S(1)}, f32[1536]{0:T(1024)S(1)}, f32[1536]{0:T(1024)S(1)}, f32[1536]{0:T(1024)S(1)}, bf16[1536,768]{1,0:T(8,128)(2,1)}, /*index=...) fusion(f32[768]{0:T(1024)S(1)} %get-tuple-element.213, bf16[1536,1536]{1,0:T(8,128)(2,1)S(1)} %bitcast.245, ...), kind=kOutput, calls=%fused_computation.22 | convolution fusion | flops 9680185344 | bytes 37791744 | tf_op jit(solution)/shard_map/dot_general | solution.py:376
  551.4 9.8 %fusion.114 = (bf16[1,4,128,1536]{3,2,1,0:T(8,128)(2,1)}, bf16[1,4,128,1536]{3,2,1,0:T(8,128)(2,1)}, bf16[1,4,128,1536]{3,2,1,0:T(8,128)(2,1)}, bf16[1,4,128,153...) fusion(bf16[8,4,128,1536]{3,2,1,0:T(8,128)(2,1)} %get-tuple-ele, ...), kind=kLoop, calls=%fused_computation.229 | loop fusion | bytes 25165824 | tf_op jit(solution)/shard_map/slice | solution.py:1005
  572.2 6.8 convolution_convert_fusion.10
  596.0 57.1 %collective-permute-done.9 = bf16[4,128,1536]{2,1,0:T(8,128)(2,1)S(1)} collective-permute-done((bf16[4,128,1536]{2,1,0:T(8,128)(2,1)S(1)}, bf16[4,128,1536]{2,1,0:T(8,128)(2,1)S(1)}, u32[]{:S(2)}, u32[]{:S(2)}) %collective-permute-start.9) | collective-permute-done | bytes 1572896 | tf_op jit(solution)/shard_map/ppermute | solution.py:891
  665.6 42.1 %forward_exchange.7 = f32[4,16,1536]{2,1,0:T(8,128)} custom-call(bf16[4,64,1536]{2,1,0:T(8,128)(2,1)} %bitcast.282, f32[4,16,1536]{2,1,0:T(8,128)} %get-tuple-element.70.rest_ref.rows_ref, f32[2,1536]{1,0:T(2,128)} %get-tuple-element.208.gain_ref), custom_call_target="tpu_custom_call" | custom-call | bytes 50000000 | tf_op jit(solution)/shard_map/forward_exchange/pallas_call | solution.py:720
  707.7 11.3 %backward_exchange.7 = (f32[4,16,1536]{2,1,0:T(8,128)}, f32[2,1536]{1,0:T(2,128)}) custom-call(bf16[4,64,1536]{2,1,0:T(8,128)(2,1)} %bitcast.260, f32[4,16,1536]{2,1,0:T(8,128)} %rows_ref.1, f32[4,16,1536]{2,1,0:T(8,128)} %get-tuple-element.82.rest_ref, f32[2,1536]{1,0:T(2,128)} %get-tuple-element.208.gain_ref), custom_call_target="tpu_custom_call" | custom-call | bytes 50000000 | tf_op jit(solution)/shard_map/backward_exchange/pallas_call | solution.py:780
  721.1 34.7 %sum_over_all.3 = f32[12,1536]{1,0:T(8,128)} custom-call(f32[12,1536]{1,0:T(8,128)} %concatenate.33.term_ref), custom_call_target="tpu_custom_call" | custom-call | bytes 20000000 | tf_op jit(solution)/shard_map/sum_over_all/pallas_call | solution.py:834
  758.9 5.5 convolution_convert_fusion.7
  776.3 6.7 copy.99
  799.8 16.1 %sum_over_all.2 = f32[8,128]{1,0:T(8,128)} custom-call(f32[8,128]{1,0:T(8,128)} %broadcast_in_dim.2.term_ref), custom_call_target="tpu_custom_call" | custom-call | bytes 20000000 | tf_op jit(solution)/shard_map/sum_over_all/pallas_call | solution.py:834
  (326 shorter events, 199.1 us)
Async XLA Ops:
  7.2 106.6 %all-gather.12.cloned.1.call-start = ((), (), s32[]{:S(2)}) async-start(), calls=%async_computation.6 | async-start | bytes 2654208 | tf_op jit(solution)/shard_map/all_gather | solution.py:894
  10.8 105.7 %all-gather.14.cloned.1.call-start = ((), (), s32[]{:S(2)}) async-start(), calls=%async_computation.7 | async-start | bytes 5308416 | tf_op jit(solution)/shard_map/all_gather | solution.py:894
  11.8 189.0 %all-gather.18.cloned.1.call-start = ((), (), s32[]{:S(2)}) async-start(), calls=%async_computation.15 | async-start | bytes 5308416 | tf_op jit(solution)/shard_map/all_gather | solution.py:894
  13.1 191.7 %all-gather.20.cloned.1.call-start = ((), (), s32[]{:S(2)}) async-start(), calls=%async_computation.16 | async-start | bytes 5308416 | tf_op jit(solution)/shard_map/all_gather | solution.py:894
  15.3 221.0 %all-gather.16.cloned.1.call-start = ((), (), s32[]{:S(2)}) async-start(), calls=%async_computation.8 | async-start | bytes 2654208 | tf_op jit(solution)/shard_map/all_gather | solution.py:894
  16.1 273.1 %all-gather.22.cloned.1.call-start = ((), (), s32[]{:S(2)}) async-start(), calls=%async_computation.17 | async-start | bytes 5308416 | tf_op jit(solution)/shard_map/all_gather | solution.py:894
  16.7 325.3 %all-gather.24.cloned.1.call-start = ((), (), s32[]{:S(2)}) async-start(), calls=%async_computation.18 | async-start | bytes 5308416 | tf_op jit(solution)/shard_map/all_gather | solution.py:894
  17.5 765.6 %reduce-scatter.7.cloned.1.call-start = ((), (), s32[]{:S(2)}) async-start(), calls=%async_computation.9 | async-start | bytes 5308416 | tf_op jit(solution)/shard_map/reduce_scatter | solution.py:947
  20.8 92.2 %collective-permute-start.2 = (bf16[4,128,1536]{2,1,0:T(8,128)(2,1)}, bf16[4,128,1536]{2,1,0:T(8,128)(2,1)S(1)}, u32[]{:S(2)}, u32[]{:S(2)}) collective-permute-start(bf16[4,128,1536]{2,1,0:T(8,128)(2,1)} %get-tuple-element.186.second_ref), channel_id=1, source_target_pairs={{0,1},{1,0},{2,3},{3,2},{4,5},{5,4},{6,7},{7,6},{8,9},{9,8},{10,11... | collective-permute-start | bytes 4718600 | tf_op jit(solution)/shard_map/ppermute | solution.py:888
  23.7 120.5 %collective-permute-start.4 = (bf16[4,128,1536]{2,1,0:T(8,128)(2,1)}, bf16[4,128,1536]{2,1,0:T(8,128)(2,1)}, u32[]{:S(2)}, u32[]{:S(2)}) collective-permute-start(bf16[4,128,1536]{2,1,0:T(8,128)(2,1)} %get-tuple-element.186.second_ref), channel_id=1, source_target_pairs={{0,2},{2,0},{1,3},{3,1},{4,6},{6,4},{5,7},{7,5},{8,10},{10,8},{9,1... | collective-permute-start | bytes 4718600 | tf_op jit(solution)/shard_map/ppermute | solution.py:891
  25.2 86.4 %collective-permute-start = (bf16[4,128,1536]{2,1,0:T(8,128)(2,1)}, bf16[4,128,1536]{2,1,0:T(8,128)(2,1)}, u32[]{:S(2)}, u32[]{:S(2)}) collective-permute-start(bf16[4,128,1536]{2,1,0:T(8,128)(2,1)} %get-tuple-element.187.first_ref), channel_id=1, source_target_pairs={{0,2},{2,0},{1,3},{3,1},{4,6},{6,4},{5,7},{7,5},{8,10},{10,8},{9,1... | collective-permute-start | bytes 4718600 | tf_op jit(solution)/shard_map/ppermute | solution.py:891
  25.7 106.3 %collective-permute-start.5 = (bf16[4,128,1536]{2,1,0:T(8,128)(2,1)}, bf16[4,128,1536]{2,1,0:T(8,128)(2,1)}, u32[]{:S(2)}, u32[]{:S(2)}) collective-permute-start(bf16[4,128,1536]{2,1,0:T(8,128)(2,1)} %get-tuple-element.187.first_ref), channel_id=1, source_target_pairs={{0,1},{1,0},{2,3},{3,2},{4,5},{5,4},{6,7},{7,6},{8,9},{9,8},{10,11... | collective-permute-start | bytes 4718600 | tf_op jit(solution)/shard_map/ppermute | solution.py:888
  111.7 44.7 %collective-permute-start.1 = (bf16[4,128,1536]{2,1,0:T(8,128)(2,1)}, bf16[4,128,1536]{2,1,0:T(8,128)(2,1)}, u32[]{:S(2)}, u32[]{:S(2)}) collective-permute-start(bf16[4,128,1536]{2,1,0:T(8,128)(2,1)} %collective-permute-done.first_ref), channel_id=1, source_target_pairs={{0,1},{1,0},{2,3},{3,2},{4,5},{5,4},{6,7},{7,6},{8,9},{9,8},{10,11... | collective-permute-start | bytes 4718600 | tf_op jit(solution)/shard_map/ppermute | solution.py:888
  113.0 43.4 %collective-permute-start.3 = (bf16[4,128,1536]{2,1,0:T(8,128)(2,1)S(1)}, bf16[4,128,1536]{2,1,0:T(8,128)(2,1)}, u32[]{:S(2)}, u32[]{:S(2)}) collective-permute-start(bf16[4,128,1536]{2,1,0:T(8,128)(2,1)S(1)} %collective-permute-done.2.second_ref), channel_id=1, source_target_pairs={{0,2},{2,0},{1,3},{3,1},{4,6},{6,4},{5,7},{7,5},{8,10},{10,8},{9,1... | collective-permute-start | bytes 4718600 | tf_op jit(solution)/shard_map/ppermute | solution.py:891
  289.2 52.8 %copy-start.61 = (bf16[4,64,1536]{2,1,0:T(8,128)(2,1)S(1)}, bf16[4,64,1536]{2,1,0:T(8,128)(2,1)}, u32[]{:S(2)}) copy-start(bf16[4,64,1536]{2,1,0:T(8,128)(2,1)} %get-tuple-element.71) | copy-start | bytes 2359300
  422.9 362.1 %reduce-scatter.9.cloned.1.call-start = ((), (), s32[]{:S(2)}) async-start(), calls=%async_computation.10 | async-start | bytes 5308416 | tf_op jit(solution)/shard_map/reduce_scatter | solution.py:947
  431.7 356.6 %reduce-scatter.11.cloned.1.call-start = ((), (), s32[]{:S(2)}) async-start(), calls=%async_computation.11 | async-start | bytes 5308416 | tf_op jit(solution)/shard_map/reduce_scatter | solution.py:947
  538.1 253.0 %reduce-scatter.13.cloned.1.call-start = ((), (), s32[]{:S(2)}) async-start(), calls=%async_computation.12 | async-start | bytes 5308416 | tf_op jit(solution)/shard_map/reduce_scatter | solution.py:947
  543.4 250.3 %reduce-scatter.15.cloned.1.call-start = ((), (), s32[]{:S(2)}) async-start(), calls=%async_computation.13 | async-start | bytes 5308416 | tf_op jit(solution)/shard_map/reduce_scatter | solution.py:947
  548.5 247.9 %reduce-scatter.17.cloned.1.call-start = ((), (), s32[]{:S(2)}) async-start(), calls=%async_computation.14 | async-start | bytes 5308416 | tf_op jit(solution)/shard_map/reduce_scatter | solution.py:947
  565.1 95.0 %collective-permute-start.7 = (bf16[4,128,1536]{2,1,0:T(8,128)(2,1)}, bf16[4,128,1536]{2,1,0:T(8,128)(2,1)}, u32[]{:S(2)}, u32[]{:S(2)}) collective-permute-start(bf16[4,128,1536]{2,1,0:T(8,128)(2,1)} %bitcast.54), channel_id=1, source_target_pairs={{0,1},{1,0},{2,3},{3,2},{4,5},{5,4},{6,7},{7,6},{8,9},{9,8},{10,11... | collective-permute-start | bytes 4718600 | tf_op jit(solution)/shard_map/ppermute | solution.py:888
  579.0 188.7 %collective-permute-start.6 = (bf16[4,128,1536]{2,1,0:T(8,128)(2,1)}, bf16[4,128,1536]{2,1,0:T(8,128)(2,1)}, u32[]{:S(2)}, u32[]{:S(2)}) collective-permute-start(bf16[4,128,1536]{2,1,0:T(8,128)(2,1)} %bitcast.50), channel_id=1, source_target_pairs={{0,1},{1,0},{2,3},{3,2},{4,5},{5,4},{6,7},{7,6},{8,9},{9,8},{10,11... | collective-permute-start | bytes 4718600 | tf_op jit(solution)/shard_map/ppermute | solution.py:888
  583.5 181.0 %collective-permute-start.11 = (bf16[4,128,1536]{2,1,0:T(8,128)(2,1)}, bf16[4,128,1536]{2,1,0:T(8,128)(2,1)}, u32[]{:S(2)}, u32[]{:S(2)}) collective-permute-start(bf16[4,128,1536]{2,1,0:T(8,128)(2,1)} %bitcast.63), channel_id=1, source_target_pairs={{0,2},{2,0},{1,3},{3,1},{4,6},{6,4},{5,7},{7,5},{8,10},{10,8},{9,1... | collective-permute-start | bytes 4718600 | tf_op jit(solution)/shard_map/ppermute | solution.py:891
  587.1 65.9 %collective-permute-start.9 = (bf16[4,128,1536]{2,1,0:T(8,128)(2,1)S(1)}, bf16[4,128,1536]{2,1,0:T(8,128)(2,1)S(1)}, u32[]{:S(2)}, u32[]{:S(2)}) collective-permute-start(bf16[4,128,1536]{2,1,0:T(8,128)(2,1)S(1)} %bitcast.292), channel_id=1, source_target_pairs={{0,2},{2,0},{1,3},{3,1},{4,6},{6,4},{5,7},{7,5},{8,10},{10,8},{9,1... | collective-permute-start | bytes 4718600 | tf_op jit(solution)/shard_map/ppermute | solution.py:891
  591.0 64.4 %slice-start.2 = ((s8[4718592]{0:T(1024)(128)(4,1)}), s8[4194304]{0:T(1024)(128)(4,1)S(1)}, s32[]{:S(2)}) async-start(s8[4718592]{0:T(1024)(128)(4,1)} %bitcast.246), calls=%async_computation.21 | async-start | bytes 8388608
  593.4 62.0 %slice-start.3 = ((s8[4718592]{0:T(1024)(128)(4,1)}), s8[524288]{0:T(1024)(128)(4,1)S(1)}, s32[]{:S(2)}) async-start(s8[4718592]{0:T(1024)(128)(4,1)} %bitcast.246), calls=%async_computation.22 | async-start | bytes 1048576
  654.6 109.9 %collective-permute-start.10 = (bf16[4,128,1536]{2,1,0:T(8,128)(2,1)}, bf16[4,128,1536]{2,1,0:T(8,128)(2,1)}, u32[]{:S(2)}, u32[]{:S(2)}) collective-permute-start(bf16[4,128,1536]{2,1,0:T(8,128)(2,1)} %add.227), channel_id=1, source_target_pairs={{0,1},{1,0},{2,3},{3,2},{4,5},{5,4},{6,7},{7,6},{8,9},{9,8},{10,11... | collective-permute-start | bytes 4718600 | tf_op jit(solution)/shard_map/ppermute | solution.py:888
  663.3 104.4 %collective-permute-start.8 = (bf16[4,128,1536]{2,1,0:T(8,128)(2,1)}, bf16[4,128,1536]{2,1,0:T(8,128)(2,1)}, u32[]{:S(2)}, u32[]{:S(2)}) collective-permute-start(bf16[4,128,1536]{2,1,0:T(8,128)(2,1)} %add.224), channel_id=1, source_target_pairs={{0,2},{2,0},{1,3},{3,1},{4,6},{6,4},{5,7},{7,5},{8,10},{10,8},{9,1... | collective-permute-start | bytes 4718600 | tf_op jit(solution)/shard_map/ppermute | solution.py:891
  665.6 53.5 %copy-start.56 = (f32[2,1536]{1,0:T(2,128)S(1)}, f32[2,1536]{1,0:T(2,128)}, u32[]{:S(2)}) copy-start(f32[2,1536]{1,0:T(2,128)} %get-tuple-element.89) | copy-start | bytes 36868
  665.6 53.5 %copy-start.57 = (f32[2,1536]{1,0:T(2,128)S(1)}, f32[2,1536]{1,0:T(2,128)}, u32[]{:S(2)}) copy-start(f32[2,1536]{1,0:T(2,128)} %get-tuple-element.88) | copy-start | bytes 36868
  665.6 53.5 %copy-start.58 = (f32[2,1536]{1,0:T(2,128)S(1)}, f32[2,1536]{1,0:T(2,128)}, u32[]{:S(2)}) copy-start(f32[2,1536]{1,0:T(2,128)} %get-tuple-element.87) | copy-start | bytes 36868
  783.0 35.4 %copy-start.54 = (f32[2,6,1536]{2,0,1:T(2,128)S(1)}, f32[2,6,1536]{2,0,1:T(2,128)}, u32[]{:S(2)}) copy-start(f32[2,6,1536]{2,0,1:T(2,128)} %param.36) | copy-start | bytes 221188
  (71 other events, 520.8 us)
Sparse Core Ops, SparseCore 0:
  11.0 34.3 all-gather.11
  47.5 50.8 all-gather.13
  100.6 50.5 all-gather.17
  153.2 50.5 all-gather.19
  205.8 30.4 all-gather.15
  238.4 50.8 all-gather.21
  291.4 50.5 all-gather.23
  423.0 53.9 reduce-scatter.6
  479.3 53.2 reduce-scatter.8
  538.2 53.1 reduce-scatter.10
  593.7 53.3 reduce-scatter.12
  649.2 53.3 reduce-scatter.14
  704.9 65.9 reduce-scatter.16

commit v2 on v1

--- a/solution.py
+++ b/solution.py
@@ -365,6 +365,7 @@
 TN = (((0,), (0,)), ((), ()))
 X_SWAP = ((0, 1), (1, 0), (2, 3), (3, 2))
 Y_SWAP = ((0, 2), (2, 0), (1, 3), (3, 1))
+FAR_SWAP = ((0, 3), (3, 0), (1, 2), (2, 1))
 
 
 def vmem_spec():
@@ -612,6 +613,47 @@
     )(live, query, latent_pair, latent_pair, keys, keys, slope, *earlier)
 
 
+def product_pair_kernel(first_ref, second_ref, third_ref, fourth_ref, *rest):
+    out_ref = rest[-1]
+
+    @pl.when(pl.program_id(0) == 0)
+    def _():
+        out_ref[...] = mm(first_ref[...], second_ref[...], TN)
+
+    @pl.when(pl.program_id(0) == 1)
+    def _():
+        out_ref[...] = mm(third_ref[...], fourth_ref[...], TN)
+
+    if len(rest) > 1:
+        @pl.when(pl.program_id(0) == 2)
+        def _():
+            out_ref[...] = rest[0][...]
+
+
+def product_pair(first, second, third, fourth, *extra):
+    rows, width, columns = first.shape[0], first.shape[1], second.shape[1]
+    cut = columns // 3
+    left = pl.BlockSpec((rows, width), lambda i, j: (0, 0))
+    return pl.pallas_call(
+        product_pair_kernel,
+        grid=(2 + len(extra), 3),
+        out_shape=jax.ShapeDtypeStruct((width, (2 + len(extra)) * columns), BF),
+        in_specs=[
+            left,
+            pl.BlockSpec((rows, cut), lambda i, j: (0, jnp.where(i == 0, j, 2))),
+            left,
+            pl.BlockSpec((rows, cut), lambda i, j: (0, jnp.where(i == 0, 0, jnp.where(i == 1, j, 2)))),
+        ]
+        + [pl.BlockSpec((width, cut), lambda i, j: (0, jnp.where(i == 2, j, 0)))] * len(extra),
+        out_specs=pl.BlockSpec((width, cut), lambda i, j: (0, 3 * i + j)),
+        compiler_params=pltpu.CompilerParams(vmem_limit_bytes=VMEM_LIMIT),
+        cost_estimate=pl.CostEstimate(
+            flops=4 * rows * width * columns, bytes_accessed=8 * width * columns, transcendentals=0
+        ),
+        name="feed_gradients",
+    )(first, second, third, fourth, *extra)
+
+
 def greet(count):
     me = lax.axis_index("heads")
     barrier = pltpu.get_barrier_semaphore()
@@ -654,37 +696,6 @@
         copy.start()
         copies.append(copy)
     return copies
-
-
-def gather_kernel(count, arrays, *refs):
-    own, full = refs[:arrays], refs[arrays : 2 * arrays]
-    sems = refs[2 * arrays :]
-    me = greet(count)
-    share = own[0].shape[1]
-    copies = []
-    for at in range(arrays):
-        copies += start_gather(me, count, share, own[at], full[at], sems[2 * at], sems[2 * at + 1])
-        full[at][:, pl.ds(pl.multiple_of(me * share, share), share), :] = own[at][...]
-    for copy in copies:
-        copy.wait()
-
-
-def gather_fast(arrays, count):
-    videos, share, width = arrays[0].shape
-    kind = jax.ShapeDtypeStruct((videos, share * count, width), arrays[0].dtype)
-    number = len(arrays)
-    return pl.pallas_call(
-        functools.partial(gather_kernel, count, number),
-        out_shape=(kind,) * number,
-        in_specs=[vmem_spec()] * number,
-        out_specs=(vmem_spec(),) * number,
-        scratch_shapes=[pltpu.SemaphoreType.DMA((count - 1,))] * (2 * number),
-        compiler_params=pltpu.CompilerParams(
-            collective_id=1, has_side_effects=True, vmem_limit_bytes=VMEM_LIMIT
-        ),
-        cost_estimate=pl.CostEstimate(flops=0, bytes_accessed=30 * 1000 * 1000, transcendentals=0),
-        name="gather_latents",
-    )(*arrays)
 
 
 def forward_kernel(
@@ -730,7 +741,7 @@
         compiler_params=pltpu.CompilerParams(
             collective_id=3 if last else 2, has_side_effects=True, vmem_limit_bytes=VMEM_LIMIT
         ),
-        cost_estimate=pl.CostEstimate(flops=0, bytes_accessed=50 * 1000 * 1000, transcendentals=0),
+        cost_estimate=pl.CostEstimate(flops=0, bytes_accessed=75 * 1000 * 1000, transcendentals=0),
         name="forward_exchange",
     )(part, rest, gain)
     return got if not last else (got[0], None)
@@ -790,13 +801,13 @@
         compiler_params=pltpu.CompilerParams(
             collective_id=5 if last else 4, has_side_effects=True, vmem_limit_bytes=VMEM_LIMIT
         ),
-        cost_estimate=pl.CostEstimate(flops=0, bytes_accessed=50 * 1000 * 1000, transcendentals=0),
+        cost_estimate=pl.CostEstimate(flops=0, bytes_accessed=75 * 1000 * 1000, transcendentals=0),
         name="backward_exchange",
     )(part, rows, rest, gain)
     return got if not last else (*got, None)
 
 
-def sum_kernel(heads, rows, term_ref, out_ref, plane_ref, line_ref, send_sem, recv_sem, send_more, recv_more):
+def sum_kernel(heads, rows, term_ref, out_ref, plane_ref, line_ref, part_ref, *sems):
     me_head, me_row = lax.axis_index("heads"), lax.axis_index("rows")
     barrier = pltpu.get_barrier_semaphore()
     for step in range(1, heads):
@@ -805,49 +816,59 @@
         pl.semaphore_signal(barrier, inc=1, device_id={"rows": (me_row + step) % rows})
     pl.semaphore_wait(barrier, heads - 1 + rows - 1)
 
-    def spread(axis, me, count, source, slots_ref, send, recv):
+    def spread(axis, me, count, source_of, slots_ref, own, send, recv):
         copies = []
         for step in range(1, count):
+            peer = (me + step) % count
             copy = pltpu.make_async_remote_copy(
-                src_ref=source,
+                src_ref=source_of(peer),
                 dst_ref=slots_ref.at[me],
                 send_sem=send.at[step - 1],
                 recv_sem=recv.at[step - 1],
-                device_id={axis: (me + step) % count},
+                device_id={axis: peer},
             )
             copy.start()
             copies.append(copy)
-        slots_ref[pl.ds(me, 1)] = source[...][None]
+        slots_ref[pl.ds(me, 1)] = own[None]
         for copy in copies:
             copy.wait()
+
+    def added(slots_ref, count):
         total = slots_ref[0]
         for at in range(1, count):
             total = total + slots_ref[at]
         return total
 
-    out_ref[...] = spread("heads", me_head, heads, term_ref, plane_ref, send_sem, recv_sem)
-    total = spread("rows", me_row, rows, out_ref, line_ref, send_more, recv_more)
-    out_ref[...] = total
+    mine = term_ref[pl.ds(me_head, 1)][0]
+    spread("heads", me_head, heads, lambda peer: term_ref.at[peer], plane_ref, mine, *sems[0:2])
+    part_ref[0] = added(plane_ref, heads)
+    spread("rows", me_row, rows, lambda peer: part_ref.at[0], line_ref, part_ref[0], *sems[2:4])
+    part_ref[1] = added(line_ref, rows)
+    spread("heads", me_head, heads, lambda peer: part_ref.at[1], out_ref, part_ref[1], *sems[4:6])
 
 
 def sum_fast(term, heads, rows, identity):
+    block = term.shape[1:]
     return pl.pallas_call(
         functools.partial(sum_kernel, heads, rows),
         out_shape=jax.ShapeDtypeStruct(term.shape, F32),
         in_specs=[vmem_spec()],
         out_specs=vmem_spec(),
         scratch_shapes=[
-            pltpu.VMEM((heads, *term.shape), F32),
-            pltpu.VMEM((rows, *term.shape), F32),
+            pltpu.VMEM((heads, *block), F32),
+            pltpu.VMEM((rows, *block), F32),
+            pltpu.VMEM((2, *block), F32),
             pltpu.SemaphoreType.DMA((heads - 1,)),
             pltpu.SemaphoreType.DMA((heads - 1,)),
             pltpu.SemaphoreType.DMA((rows - 1,)),
             pltpu.SemaphoreType.DMA((rows - 1,)),
+            pltpu.SemaphoreType.DMA((heads - 1,)),
+            pltpu.SemaphoreType.DMA((heads - 1,)),
         ],
         compiler_params=pltpu.CompilerParams(
             collective_id=identity, has_side_effects=True, vmem_limit_bytes=VMEM_LIMIT
         ),
-        cost_estimate=pl.CostEstimate(flops=0, bytes_accessed=20 * 1000 * 1000, transcendentals=0),
+        cost_estimate=pl.CostEstimate(flops=0, bytes_accessed=40 * 1000 * 1000, transcendentals=0),
         name="sum_over_all",
     )(term)
 
@@ -894,16 +915,36 @@
         return lax.all_gather(rows, "rows", axis=0, tiled=True)
 
     outward_t, narrow_t = (jnp.swapaxes(outward, 1, 2), jnp.swapaxes(narrow, 1, 2))
-    pair_weights = gather_rows(
-        jnp.concatenate([inward[l, t].astype(BF) for l in range(layers) for t in (1, 2)], axis=1)
-    )
-    query_out, widen_full, narrow_full = [], [], []
+    columns, units = head_columns, widen.shape[2]
+    first_set = [inward[l, t] for l in range(layers) for t in (1, 2)]
+    first_set = first_set + [inward[l, 0] for l in range(layers)] + [outward_t[l] for l in range(layers)]
+    first_set = jnp.concatenate([piece.astype(BF) for piece in first_set], axis=1)
+
+    latent = latents
+    normed = layer_norm(latent, norm_gains[0, 2], norm_gains[0, 3]).astype(BF)
+    slope_rows = cotangent.astype(BF)
+    first_set = gather_rows(first_set)
+    pair_weights = first_set[:, : 2 * layers * columns]
+    begin = 2 * layers * columns
+    query_full = [first_set[:, begin + l * columns : begin + (l + 1) * columns] for l in range(layers)]
+    begin = begin + layers * columns
+    out_full = [first_set[:, begin + l * columns : begin + (l + 1) * columns] for l in range(layers)]
+    widen_full, narrow_full = [], []
     for layer in range(layers):
-        query_out.append(
-            gather_rows(jnp.concatenate((inward[layer, 0], outward_t[layer]), axis=1).astype(BF))
-        )
-        widen_full.append(gather_rows(widen[layer].astype(BF)))
-        narrow_full.append(gather_rows(narrow_t[layer].astype(BF)))
+        later = gather_rows(jnp.concatenate((widen[layer].astype(BF), narrow_t[layer].astype(BF)), axis=1))
+        widen_full.append(later[:, :units])
+        narrow_full.append(later[:, units:])
+    share = latents.shape[1]
+    moved = [(normed, slope_rows)]
+    for swap in (X_SWAP, Y_SWAP, FAR_SWAP):
+        moved.append(tuple(lax.ppermute(rows, "heads", swap) for rows in (normed, slope_rows)))
+    gathered = []
+    for at in range(2):
+        full = jnp.zeros((videos, latent_count, width), BF)
+        for group in range(heads_count):
+            full = lax.dynamic_update_slice(full, moved[group][at], (0, (me ^ group) * share, 0))
+        gathered.append(full)
+    latent_norm, feed_slope = gathered
 
     own = jnp.swapaxes(media, 0, 1).reshape(videos, 2, local_positions // 2, width)
     own = (own[:, 0], own[:, 1])
@@ -918,12 +959,9 @@
         made = media_part(parts[0], parts[1], media_gains, pair_weights, group, made)
     keys, media_hat = made
 
-    latent = latents
-    normed = layer_norm(latent, norm_gains[0, 2], norm_gains[0, 3]).astype(BF)
-    latent_norm, feed_slope = gather_fast((normed, cotangent.astype(BF)), heads_count)
     kept = []
     for layer in range(layers):
-        query_weight, out_weight = query_out[layer][:, :head_columns], query_out[layer][:, head_columns:]
+        query_weight, out_weight = query_full[layer], out_full[layer]
         pair_weight = pair_weights[:, 2 * layer * head_columns : 2 * (layer + 1) * head_columns]
         query = mm(flat(latent_norm), query_weight)
         latent_pair = mm(flat(latent_norm), pair_weight)
@@ -936,30 +974,56 @@
         last = layer == layers - 1
         gain = norm_gains[0 if last else layer + 1, 2:4]
         kept.append((latent, middle, latent_norm, query, latent_pair, mixed, feed_norm, hidden_pre, hidden))
-        latent, latent_norm = forward_exchange(part, middle, gain, heads_count, last)
+        if last:
+            latent = middle
+            for group, swap in enumerate((None, X_SWAP, Y_SWAP, FAR_SWAP)):
+                term = lax.dynamic_slice_in_dim(part, (me ^ group) * share, share, axis=1)
+                latent = latent + (lax.ppermute(term, "heads", swap) if swap else term).astype(F32)
+        else:
+            latent, latent_norm = forward_exchange(part, middle, gain, heads_count)
 
     slope = cotangent
     gain_parts = [None] * layers
-    shares = [None] * layers
+    shares, waiting = [], []
     media_slopes = ()
 
+    scaled = jnp.concatenate(
+        [
+            (
+                pair_weights[:, 2 * l * head_columns : 2 * (l + 1) * head_columns].astype(F32)
+                * norm_gains[l, 0][:, None]
+            ).astype(BF)
+            for l in range(layers)
+        ],
+        axis=1,
+    )
+
+    def hat_slope(slopes, group, half):
+        return mm(flat(slopes[2 * group + half]), scaled, NT).reshape(videos, -1, width)
+
+    summed = []
+
     def scatter_rows(gradient):
-        return lax.psum_scatter(gradient, "rows", scatter_dimension=0, tiled=True)
+        if summed:
+            gradient, _ = lax.optimization_barrier((gradient, summed[-1]))
+        summed.append(lax.psum_scatter(gradient, "rows", scatter_dimension=0, tiled=True))
+        return summed[-1]
 
     for layer in reversed(range(layers)):
         latent_in, middle, latent_norm, query, latent_pair, mixed, feed_norm, hidden_pre, hidden = kept[layer]
-        query_weight, out_weight = query_out[layer][:, :head_columns], query_out[layer][:, head_columns:]
+        query_weight, out_weight = query_full[layer], out_full[layer]
         pair_weight = pair_weights[:, 2 * layer * head_columns : 2 * (layer + 1) * head_columns]
         feed_slope = flat(feed_slope)
-        narrow_grad = scatter_rows(mm(feed_slope, hidden, TN))
         hidden_slope = mm(feed_slope, narrow_full[layer], None, F32)
         _, gelu_back = jax.vjp(jax.nn.gelu, hidden_pre)
         pre_slope = gelu_back(hidden_slope)[0].astype(BF)
         part = mm(pre_slope, widen_full[layer], NT).reshape(videos, latent_count, width)
+        feed_grad = product_pair(feed_slope, hidden, flat(feed_norm), pre_slope, *waiting)
+        part, feed_grad = lax.optimization_barrier((part, feed_grad))
+        shares.append(scatter_rows(feed_grad))
         middle_slope, feed_sums, branch_slope = backward_exchange(
             part, middle, slope, norm_gains[layer, 4:6], heads_count
         )
-        widen_grad = scatter_rows(mm(flat(feed_norm), pre_slope, TN))
         branch_slope = flat(branch_slope)
         mixed_slope = mm(branch_slope, out_weight)
         out_grad = mm(branch_slope, mixed, TN)
@@ -972,6 +1036,16 @@
         slope, latent_sums, feed_slope = backward_exchange(
             part, latent_in, middle_slope, norm_gains[layer, 2:4], heads_count, last
         )
+        if last:
+            media_slopes, slope = lax.optimization_barrier((media_slopes, slope))
+            far = [hat_slope(media_slopes, 3, half) for half in range(2)]
+            media_slopes, *far = lax.optimization_barrier((media_slopes, *far))
+            over_x, over_y = swap_x(far[0]), swap_y(far[1])
+            near = [hat_slope(media_slopes, 1, 0), hat_slope(media_slopes, 2, 1)]
+            media_slopes, *near = lax.optimization_barrier((media_slopes, *near))
+            in_x, in_y = [swap_x(near[0]), None], [None, swap_y(near[1])]
+            near = [hat_slope(media_slopes, 1, 1), hat_slope(media_slopes, 2, 0)]
+            media_slopes, *near = lax.optimization_barrier((media_slopes, *near))
         query_grad = mm(flat(latent_norm), query_slope, TN)
         pair_slope = flat(media_slopes[..., 2 * layer * head_columns : 2 * (layer + 1) * head_columns])
         hat_grad = mm(flat(media_hat), pair_slope, TN, F32)
@@ -986,68 +1060,59 @@
         media_sums = jnp.stack(
             (jnp.sum(wide * hat_grad, axis=1), jnp.sum(wide * slope_sum[None, :], axis=1))
         )
-        inward_grad = scatter_rows(jnp.concatenate((out_grad, query_grad, pair_grad), axis=1))
-        shares[layer] = (narrow_grad, widen_grad, inward_grad)
+        inward_grad = jnp.concatenate((out_grad, query_grad, pair_grad), axis=1)
+        if last:
+            inward_grad, over_x, over_y, in_x[0], in_y[1] = lax.optimization_barrier(
+                (inward_grad, over_x, over_y, in_x[0], in_y[1])
+            )
+            shares.append(scatter_rows(inward_grad))
+        else:
+            inward_grad, latent = lax.optimization_barrier((inward_grad, latent))
+            waiting = [inward_grad]
         gain_parts[layer] = jnp.concatenate((media_sums, latent_sums, feed_sums), axis=0)
 
-    scaled = jnp.concatenate(
-        [
-            (
-                pair_weights[:, 2 * l * head_columns : 2 * (l + 1) * head_columns].astype(F32)
-                * norm_gains[l, 0][:, None]
-            ).astype(BF)
-            for l in range(layers)
-        ],
-        axis=1,
-    )
-
-    def hat_slope(group, half):
-        return mm(flat(media_slopes[2 * group + half]), scaled, NT).reshape(videos, -1, width)
-
-    over_x = swap_x(hat_slope(3, 0))
-    over_y = swap_y(hat_slope(3, 1))
-    back = [hat_slope(0, 0).astype(F32), hat_slope(0, 1).astype(F32)]
-    in_x = [swap_x(hat_slope(1, 0)), None]
-    in_y = [None, swap_y(hat_slope(2, 1))]
-    in_x[1] = swap_x(hat_slope(1, 1) + over_y)
-    in_y[0] = swap_y(hat_slope(2, 0) + over_x)
-    pieces = []
-    for half in range(2):
-        total = back[half] + in_x[half].astype(F32) + in_y[half].astype(F32)
-        rows = own[half].astype(F32)
-        centred = rows - jnp.mean(rows, axis=-1, keepdims=True)
-        spread = lax.rsqrt(jnp.mean(centred * centred, axis=-1, keepdims=True) + EPS_NORM)
-        hat = centred * spread
-        total = total - jnp.mean(total, axis=-1, keepdims=True) - hat * jnp.mean(total * hat, axis=-1, keepdims=True)
-        pieces.append(jnp.swapaxes(total * spread, 0, 1))
-    media_slope = jnp.concatenate(pieces, axis=0)
-
-    gain_total = sum_fast(jnp.concatenate(gain_parts, axis=0), heads_count, rows_count, 6)
-    gain_total = gain_total.reshape(layers, 6, width)
-    squares = jnp.zeros((), F32)
-    for share in shares:
-        for piece in share:
-            wide = piece.astype(F32)
-            squares = squares + jnp.sum(wide * wide)
-    square_total = sum_fast(jnp.full((8, 128), squares, F32), heads_count, rows_count, 7)[0, 0]
+    back = [hat_slope(media_slopes, 0, half).astype(F32) for half in range(2)]
+    in_x[1] = swap_x(near[0] + over_y)
+    in_y[0] = swap_y(near[1] + over_x)
+
+    def square_sum(rows):
+        wide = rows.astype(F32)
+        return jnp.sum(wide * wide)
+
+    early = sum(square_sum(piece) for piece in shares[:-1])
+    in_x[1], in_y[0], early = lax.optimization_barrier((in_x[1], in_y[0], early))
+    rows = jnp.stack(own, axis=1).astype(F32)
+    total = jnp.stack(back, axis=1) + jnp.stack(in_x, axis=1).astype(F32) + jnp.stack(in_y, axis=1).astype(F32)
+    centred = rows - jnp.mean(rows, axis=-1, keepdims=True)
+    spread = lax.rsqrt(jnp.mean(centred * centred, axis=-1, keepdims=True) + EPS_NORM)
+    hat = centred * spread
+    total = total - jnp.mean(total, axis=-1, keepdims=True) - hat * jnp.mean(total * hat, axis=-1, keepdims=True)
+    media_slope = (total * spread).reshape(videos, local_positions, width)
+    media_slope = jnp.swapaxes(media_slope, 0, 1)
+
+    media_slope, shares[-1] = lax.optimization_barrier((media_slope, shares[-1]))
+    gain_term = jnp.concatenate(gain_parts, axis=0).reshape(heads_count, -1, 128)
+    lines = gain_term.shape[1]
+    squares = jnp.full((heads_count, 8 - lines % 8, 128), early + square_sum(shares[-1]), F32)
+    totals = sum_fast(jnp.concatenate((gain_term, squares), axis=1), heads_count, rows_count, 6)
+    gain_total = totals[:, :lines].reshape(layers, 6, width)
+    square_total = totals[0, lines, 0]
+    feed_parts = [piece[:, : 2 * units] for piece in shares[-2::-1]]
+    inward_parts = [shares[-1]] + [piece[:, 2 * units :] for piece in shares[-2:0:-1]]
     gradient_norm = jnp.sqrt(square_total + jnp.sum(gain_total * gain_total))
     factor = CLIP_LEVEL / jnp.maximum(gradient_norm, CLIP_LEVEL)
 
-    def wide_part(index, begin, end):
-        return jnp.stack([share[index][:, begin:end] for share in shares]).astype(F32)
-
-    columns = head_columns
+    def wide_part(parts, begin, end):
+        return jnp.stack([piece[:, begin:end] for piece in parts]).astype(F32)
+
     inward_grad = jnp.stack(
-        [
-            jnp.stack([share[2][:, (1 + t) * columns : (2 + t) * columns] for t in range(3)])
-            for share in shares
-        ]
-    ).astype(F32)
+        [wide_part(inward_parts, (1 + t) * columns, (2 + t) * columns) for t in range(3)], axis=1
+    )
     table = (
         (inward, inward_first, inward_second, inward_grad, RATE_INWARD),
-        (outward, outward_first, outward_second, jnp.swapaxes(wide_part(2, 0, columns), 1, 2), RATE_OUTWARD),
-        (widen, widen_first, widen_second, wide_part(1, 0, None), RATE_WIDEN),
-        (narrow, narrow_first, narrow_second, jnp.swapaxes(wide_part(0, 0, None), 1, 2), RATE_NARROW),
+        (outward, outward_first, outward_second, jnp.swapaxes(wide_part(inward_parts, 0, columns), 1, 2), RATE_OUTWARD),
+        (widen, widen_first, widen_second, wide_part(feed_parts, units, None), RATE_WIDEN),
+        (narrow, narrow_first, narrow_second, jnp.swapaxes(wide_part(feed_parts, 0, units), 1, 2), RATE_NARROW),
     )
     results = [latent, slope, media_slope, gradient_norm]
     for weight, first, second, gradient, rate in table:

time: 855 us -> 719 us (0.84)
  Pallas kernels: 419 us -> 267 us
  waiting for transfers between devices: 120 us -> 148 us
  matrix products: 157 us -> 137 us
  starting transfers between devices: 13.6 us -> 32.2 us
  local copies, waits for them, and re-layouts: 53.5 us -> 44.1 us
    ppermute x0 -> x9, waiting for transfers between devices: none -> 87.6 us  [the longest x6 87.6 us: local_fast(): lax.ppermute(rows, 'heads', swap)]
    pallas_call x1 -> x2, Pallas kernels: 81.3 us -> 19.5 us  [product_pair(): pl.pallas_call(product_pair_kernel, grid=(2 + len(extra), 3), out_shape=j...]
    all_gather x7 -> x3, waiting for transfers between devices: 61.5 us -> 2.76 us  [gather_rows(): return lax.all_gather(rows, 'rows', axis=0, tiled=True)]
    pallas_call x4 -> x3, Pallas kernels: 113 us -> 54.7 us  [forward_exchange(): pl.pallas_call(functools.partial(forward_kernel, count, last), out_shape=...]
    ppermute x6, waiting for transfers between devices: 0.02 us -> 41.6 us  [swap_x(): return lax.ppermute(rows, 'heads', X_SWAP)]
    ppermute x6, waiting for transfers between devices: 57.1 us -> 15.5 us  [swap_y(): return lax.ppermute(rows, 'heads', Y_SWAP)]
    pallas_call x2 -> x1, Pallas kernels: 50.8 us -> 14.2 us  [sum_fast(): pl.pallas_call(functools.partial(sum_kernel, heads, rows), out_shape=jax....]
    dot_general x40 -> x36, matrix products: 157 us -> 137 us  [mm(): lax.dot_general(left, right, dims, preferred_element_type=F32).astype(out)]
  transfers between devices with their start and end apart: 25 -> 27, of which waited for: 4 -> 13; matrix products, arithmetic and copies ran while one was open for 26% -> 27% of each run, Pallas kernels for 40% -> 34%
where the time goes in v2:
time: 719 us; the launch traced here: 713 us
  Pallas kernels  267 us (37%)
  waiting for transfers between devices  148 us (21%)
  matrix products  137 us (19%)
  other arithmetic  65.1 us (9%)
  local copies, waits for them, and re-layouts  44.1 us (6%)
  starting transfers between devices  32.2 us (4%)
  between operations  20.2 us (3%)
    dot_general x36, matrix products, mm(): lax.dot_general(left, right, dims, preferred_element_type=F32).astype(out)  137 us
    pallas_call x4, Pallas kernels, backward_exchange(): pl.pallas_call(functools.partial(backward_kernel, count, last), out_shape...  90.3 us
    ppermute x6, waiting for transfers between devices, local_fast(): lax.ppermute(rows, 'heads', swap)  87.6 us
    pallas_call x3, Pallas kernels, forward_exchange(): pl.pallas_call(functools.partial(forward_kernel, count, last), out_shape=...  54.7 us
    pallas_call x4, Pallas kernels, media_part(): pl.pallas_call(media_kernel, grid=(2, 2), out_shape=kinds, in_specs=in_sp...  49 us
    ppermute x6, waiting for transfers between devices, swap_x(): return lax.ppermute(rows, 'heads', X_SWAP)  41.6 us
    pallas_call x2, Pallas kernels, attend_back_fast(): pl.pallas_call(functools.partial(attend_back_kernel, scale=scale), grid=(...  23.9 us
    pallas_call x2, Pallas kernels, product_pair(): pl.pallas_call(product_pair_kernel, grid=(2 + len(extra), 3), out_shape=j...  19.5 us
  transfers between devices with their start and end apart: 27, of which 13 were waited for; matrix products, arithmetic and copies ran while one was open for 27% of the time, Pallas kernels for 34%

profile of v2, /device:TPU:0, one launch (start us, length us, event | category | flops | bytes accessed | tf_op | source)
XLA Modules:
  0.0 712.5 jit_solution(12058605245816400076)
XLA Ops:
  32.0 63.3 %collective-permute-done.3 = bf16[4,16,1536]{2,1,0:T(8,128)(2,1)} collective-permute-done((bf16[4,16,1536]{2,1,0:T(8,128)(2,1)}, bf16[4,16,1536]{2,1,0:T(8,128)(2,1)}, u32[]{:S(2)}, u32[]{:S(2)}) %collective-permute-start.3) | collective-permute-done | bytes 196640 | tf_op jit(solution)/shard_map/ppermute | solution.py:940
  109.2 5.3 collective-permute-done.1
  125.1 6.3 collective-permute-done.2
  134.5 4.8 slice.292.weight_ref
  145.1 12.4 %media_part.4 = (bf16[8,4,128,1536]{3,2,1,0:T(8,128)(2,1)}, bf16[8,4,128,1536]{3,2,1,0:T(8,128)(2,1)}) custom-call(bf16[4,128,1536]{2,1,0:T(8,128)(2,1)} %get-tuple-element.263.first_ref, bf16[4,128,1536]{2,1,0:T(8,128)(2,1)} %get-tuple-element.262.second_ref, f32[2,2,1536]{2,1,0:T(2,128)} %slice.291.gain_ref, bf16[1536,1536]{1,0:T(8,128)(2,1)} %slice.292.weight_ref), custom_call_target="tpu_custom_call" | custom-call | flops 4831838208 | bytes 6291456 | tf_op jit(solution)/shard_map/media_part/pallas_call | solution.py:426
  157.5 12.2 %media_part.5 = (bf16[8,4,128,1536]{3,2,1,0:T(8,128)(2,1)}, bf16[8,4,128,1536]{3,2,1,0:T(8,128)(2,1)}) custom-call(bf16[4,128,1536]{2,1,0:T(8,128)(2,1)} %collective-permute-done.11.first_ref, bf16[4,128,1536]{2,1,0:T(8,128)(2,1)} %collective-permute-done.8.second_ref, f32[2,2,1536]{2,1,0:T(2,128)} %slice.291.gain_ref, ...), custom_call_target="tpu_custom_call", output_to_operand_aliasing={{0}: (4, {}), {1}: (5, {})} | custom-call | flops 4831838208 | bytes 6291456 | tf_op jit(solution)/shard_map/media_part/pallas_call | solution.py:426
  169.7 12.2 %media_part.6 = (bf16[8,4,128,1536]{3,2,1,0:T(8,128)(2,1)}, bf16[8,4,128,1536]{3,2,1,0:T(8,128)(2,1)}) custom-call(bf16[4,128,1536]{2,1,0:T(8,128)(2,1)} %copy-done.31, bf16[4,128,1536]{2,1,0:T(8,128)(2,1)} %collective-permute-done.10.second_ref, f32[2,2,1536]{2,1,0:T(2,128)} %slice.291.gain_ref, ...), custom_call_target="tpu_custom_call", output_to_operand_aliasing={{0}: (4, {}), {1}: (5, {})} | custom-call | flops 4831838208 | bytes 6291456 | tf_op jit(solution)/shard_map/media_part/pallas_call | solution.py:426
  182.0 12.1 %media_part.7 = (bf16[8,4,128,1536]{3,2,1,0:T(8,128)(2,1)}, bf16[8,4,128,1536]{3,2,1,0:T(8,128)(2,1)}) custom-call(bf16[4,128,1536]{2,1,0:T(8,128)(2,1)} %collective-permute-done.7.first_ref, bf16[4,128,1536]{2,1,0:T(8,128)(2,1)} %collective-permute-done.9.second_ref, f32[2,2,1536]{2,1,0:T(2,128)} %slice.291.gain_ref, ...), custom_call_target="tpu_custom_call", output_to_operand_aliasing={{0}: (4, {}), {1}: (5, {})} | custom-call | flops 4831838208 | bytes 6291456 | tf_op jit(solution)/shard_map/media_part/pallas_call | solution.py:426
  194.1 7.8 %attend.2 = bf16[256,384]{1,0:T(8,128)(2,1)} custom-call(s32[4,8]{1,0:T(4,128)} %compare_convert_fusion.live_ref, bf16[256,384]{1,0:T(8,128)(2,1)} %convolution_convert_fusion.19.query_ref, bf16[256,768]{1,0:T(8,128)(2,1)} %convolution_convert_fusion.15.latent_key_ref.latent_value_ref, ...), custom_call_target="tpu_custom_call" | custom-call | flops 1610612736 | bytes 6291456 | tf_op jit(solution)/shard_map/attend/pallas_call | solution.py:497
  205.0 18.0 %forward_exchange.3 = (f32[4,16,1536]{2,1,0:T(8,128)}, bf16[4,64,1536]{2,1,0:T(8,128)(2,1)}) custom-call(bf16[4,64,1536]{2,1,0:T(8,128)(2,1)} %bitcast.260, f32[4,16,1536]{2,1,0:T(8,128)} %rows_ref.1, f32[2,1536]{1,0:T(2,128)} %get-tuple-element.286.gain_ref), custom_call_target="tpu_custom_call" | custom-call | bytes 75000000 | tf_op jit(solution)/shard_map/forward_exchange/pallas_call | solution.py:731
  223.1 5.5 multiply_convert_fusion.1
  231.0 18.6 %forward_exchange.4 = (f32[4,16,1536]{2,1,0:T(8,128)}, bf16[4,64,1536]{2,1,0:T(8,128)(2,1)}) custom-call(bf16[4,64,1536]{2,1,0:T(8,128)(2,1)} %bitcast.258, f32[4,16,1536]{2,1,0:T(8,128)} %get-tuple-element.92.rest_ref.rows_ref, f32[2,1536]{1,0:T(2,128)} %get-tuple-element.285.gain_ref), custom_call_target="tpu_custom_call" | custom-call | bytes 75000000 | tf_op jit(solution)/shard_map/forward_exchange/pallas_call | solution.py:731
  255.7 7.4 %attend.3 = bf16[256,384]{1,0:T(8,128)(2,1)} custom-call(s32[4,8]{1,0:T(4,128)} %compare_convert_fusion.live_ref, bf16[256,384]{1,0:T(8,128)(2,1)} %convolution_convert_fusion.18.query_ref, bf16[256,768]{1,0:T(8,128)(2,1)} %convolution_convert_fusion.14.latent_key_ref.latent_value_ref, ...), custom_call_target="tpu_custom_call" | custom-call | flops 1610612736 | bytes 6291456 | tf_op jit(solution)/shard_map/attend/pallas_call | solution.py:497
  265.9 18.1 %forward_exchange.5 = (f32[4,16,1536]{2,1,0:T(8,128)}, bf16[4,64,1536]{2,1,0:T(8,128)(2,1)}) custom-call(bf16[4,64,1536]{2,1,0:T(8,128)(2,1)} %bitcast.259, f32[4,16,1536]{2,1,0:T(8,128)} %get-tuple-element.94.rest_ref.rows_ref, f32[2,1536]{1,0:T(2,128)} %get-tuple-element.284.gain_ref), custom_call_target="tpu_custom_call" | custom-call | bytes 75000000 | tf_op jit(solution)/shard_map/forward_exchange/pallas_call | solution.py:731
  286.7 5.2 multiply_convert_fusion
  295.1 8.0 %feed_gradients.2 = bf16[1536,3072]{1,0:T(8,128)(2,1)} custom-call(bf16[256,1536]{1,0:T(8,128)(2,1)} %bitcast.233, bf16[256,1536]{1,0:T(8,128)(2,1)} %get-tuple-element.291.second_ref, bf16[256,1536]{1,0:T(8,128)(2,1)} %bitcast.251, bf16[256,1536]{1,0:T(8,128)(2,1)} %fusion.71.fourth_ref), custom_call_target="tpu_custom_call" | custom-call | flops 2415919104 | bytes 18874368 | tf_op jit(solution)/shard_map/feed_gradients/pallas_call | solution.py:637
  316.4 28.9 %backward_exchange.4 = (f32[4,16,1536]{2,1,0:T(8,128)}, f32[2,1536]{1,0:T(2,128)}, bf16[4,64,1536]{2,1,0:T(8,128)(2,1)}) custom-call(bf16[4,64,1536]{2,1,0:T(8,128)(2,1)} %bitcast.255, f32[4,16,1536]{2,1,0:T(8,128)} %get-tuple-element.97.rows_ref, f32[4,16,1536]{2,1,0:T(8,128)} %rest_ref.3, f32[2,1536]{1,0:T(2,128)} %get-tuple-element.284.gain_ref), custom_call_target="tpu_custom_call" | custom-call | bytes 75000000 | tf_op jit(solution)/shard_map/backward_exchange/pallas_call | solution.py:791
  348.1 12.1 %attend_back.2 = (bf16[256,384]{1,0:T(8,128)(2,1)}, bf16[256,768]{1,0:T(8,128)(2,1)}, bf16[8,4,128,1536]{3,2,1,0:T(8,128)(2,1)}) custom-call(s32[4,8]{1,0:T(4,128)} %compare_convert_fusion.live_ref, bf16[256,384]{1,0:T(8,128)(2,1)} %convolution_convert_fusion.18.query_ref, bf16[256,768]{1,0:T(8,128)(2,1)} %convolution_convert_fusion.14.latent_key_ref.latent_value_ref, ...), custom_call_target="tpu_custom_call" | custom-call | flops 4026531840 | bytes 12582912 | tf_op jit(solution)/shard_map/attend_back/pallas_call | solution.py:591
  365.8 23.0 %backward_exchange.5 = (f32[4,16,1536]{2,1,0:T(8,128)}, f32[2,1536]{1,0:T(2,128)}, bf16[4,64,1536]{2,1,0:T(8,128)(2,1)}) custom-call(bf16[4,64,1536]{2,1,0:T(8,128)(2,1)} %bitcast.230, f32[4,16,1536]{2,1,0:T(8,128)} %get-tuple-element.94.rest_ref.rows_ref, f32[4,16,1536]{2,1,0:T(8,128)} %get-tuple-element.104.rest_ref, f32[2,1536]{1,0:T(2,128)} %get-tuple-element.285.gain_ref), custom_call_target="tpu_custom_call" | custom-call | bytes 75000000 | tf_op jit(solution)/shard_map/backward_exchange/pallas_call | solution.py:791
  394.4 14.3 %fusion.11 = f32[1536,768,1,1]{1,0,3,2:T(8,128)S(1)} fusion(bf16[8,4,128,1536]{3,2,1,0:T(8,128)(2,1)} %get-tuple-element.101, bf16[8,4,128,1536]{3,2,1,0:T(8,128)(2,1)} %get-tuple-element.102.rest_0_), kind=kOutput, calls=%fused_computation.23 | convolution fusion | flops 9663676416 | bytes 23592960 | tf_op jit(solution)/shard_map/dot_general | solution.py:377
  419.3 11.5 %feed_gradients.3 = bf16[1536,4608]{1,0:T(8,128)(2,1)} custom-call(bf16[256,1536]{1,0:T(8,128)(2,1)} %bitcast.248, bf16[256,1536]{1,0:T(8,128)(2,1)} %copy-done.39, bf16[256,1536]{1,0:T(8,128)(2,1)} %bitcast.247, bf16[256,1536]{1,0:T(8,128)(2,1)} %copy-done.41, bf16[1536,1536]{1,0:T(8,128)(2,1)} %pad_maximum_fusion.rest_0_), custom_call_target="tpu_custom_call" | custom-call | flops 2415919104 | bytes 18874368 | tf_op jit(solution)/shard_map/feed_gradients/pallas_call | solution.py:637
  434.7 24.8 %backward_exchange.6 = (f32[4,16,1536]{2,1,0:T(8,128)}, f32[2,1536]{1,0:T(2,128)}, bf16[4,64,1536]{2,1,0:T(8,128)(2,1)}) custom-call(bf16[4,64,1536]{2,1,0:T(8,128)(2,1)} %bitcast.254, f32[4,16,1536]{2,1,0:T(8,128)} %get-tuple-element.92.rest_ref.rows_ref, f32[4,16,1536]{2,1,0:T(8,128)} %get-tuple-element.108.rest_ref, f32[2,1536]{1,0:T(2,128)} %get-tuple-element.286.gain_ref), custom_call_target="tpu_custom_call" | custom-call | bytes 75000000 | tf_op jit(solution)/shard_map/backward_exchange/pallas_call | solution.py:791
  462.3 11.8 %attend_back.3 = (bf16[256,384]{1,0:T(8,128)(2,1)}, bf16[256,768]{1,0:T(8,128)(2,1)}, bf16[8,4,128,1536]{3,2,1,0:T(8,128)(2,1)}) custom-call(s32[4,8]{1,0:T(4,128)} %compare_convert_fusion.live_ref, bf16[256,384]{1,0:T(8,128)(2,1)} %convolution_convert_fusion.19.query_ref, ...), custom_call_target="tpu_custom_call", output_to_operand_aliasing={{2}: (7, {})} | custom-call | flops 4026531840 | bytes 12582912 | tf_op jit(solution)/shard_map/attend_back/pallas_call | solution.py:591
  479.6 13.6 %backward_exchange.7 = (f32[4,16,1536]{2,1,0:T(8,128)}, f32[2,1536]{1,0:T(2,128)}) custom-call(bf16[4,64,1536]{2,1,0:T(8,128)(2,1)} %bitcast.231, f32[4,16,1536]{2,1,0:T(8,128)} %rows_ref.1, f32[4,16,1536]{2,1,0:T(8,128)} %get-tuple-element.113.rest_ref, f32[2,1536]{1,0:T(2,128)} %get-tuple-element.283.gain_ref), custom_call_target="tpu_custom_call" | custom-call | bytes 75000000 | tf_op jit(solution)/shard_map/backward_exchange/pallas_call | solution.py:791
  525.4 19.7 %fusion.18 = (f32[1536]{0:T(1024)S(1)}, f32[1536]{0:T(1024)S(1)}, f32[1536]{0:T(1024)S(1)}, f32[1536]{0:T(1024)S(1)}, bf16[1536,768]{1,0:T(8,128)(2,1)S(1)}) fusion(f32[768]{0:T(1024)S(1)} %copy-done.60, bf16[1536,3072]{1,0:T(8,128)(2,1)} %all-gather.6.cloned.1.call-done, f32[768]{0:T(1024)S(1)} %convert_reduce_fusion, f32[1536,768,1,1]{1,0,3,2:T(8,128)} %copy-done.11, ...), kind=kOutput, calls=%fused_computation.30 | convolution fusion | flops 9681364992 | bytes 35432448 | tf_op jit(solution)/shard_map/dot_general | solution.py:377
  550.0 6.7 collective-permute-done.17
  558.2 30.5 %collective-permute-done.15 = bf16[4,128,1536]{2,1,0:T(8,128)(2,1)} collective-permute-done((bf16[4,128,1536]{2,1,0:T(8,128)(2,1)}, bf16[4,128,1536]{2,1,0:T(8,128)(2,1)}, u32[]{:S(2)}, u32[]{:S(2)}) %collective-permute-start.15) | collective-permute-done | bytes 1572896 | tf_op jit(solution)/shard_map/ppermute | solution.py:909
  608.2 6.8 convolution_convert_fusion
  620.1 13.6 %collective-permute-done.20 = bf16[4,128,1536]{2,1,0:T(8,128)(2,1)} collective-permute-done((bf16[4,128,1536]{2,1,0:T(8,128)(2,1)}, bf16[4,128,1536]{2,1,0:T(8,128)(2,1)}, u32[]{:S(2)}, u32[]{:S(2)}) %collective-permute-start.20) | collective-permute-done | bytes 1572896 | tf_op jit(solution)/shard_map/ppermute | solution.py:912
  654.7 14.2 %sum_over_all.1 = f32[4,40,128]{2,1,0:T(8,128)} custom-call(f32[4,40,128]{2,1,0:T(8,128)} %concatenate.52.term_ref), custom_call_target="tpu_custom_call" | custom-call | bytes 40000000 | tf_op jit(solution)/shard_map/sum_over_all/pallas_call | solution.py:852
  677.0 9.7 %copy.129 = f32[256,4,1536]{2,1,0:T(4,128)} copy(f32[256,4,1536]{2,0,1:T(8,128)} %fusion.7) | data formatting | bytes 12582912
  686.8 5.1 fusion.101
  (323 shorter events, 228.7 us)
Async XLA Ops:
  7.2 127.3 %all-gather.6.cloned.1.call-start = ((), (), s32[]{:S(2)}) async-start(), calls=%async_computation.4 | async-start | bytes 10616832 | tf_op jit(solution)/shard_map/all_gather | solution.py:915
  10.3 212.8 %all-gather.8.cloned.1.call-start = ((), (), s32[]{:S(2)}) async-start(), calls=%async_computation.5 | async-start | bytes 10616832 | tf_op jit(solution)/shard_map/all_gather | solution.py:915
  14.7 272.0 %all-gather.4.cloned.1.call-start = ((), (), s32[]{:S(2)}) async-start(), calls=%async_computation.3 | async-start | bytes 10616832 | tf_op jit(solution)/shard_map/all_gather | solution.py:915
  17.3 413.5 %reduce-scatter.4.cloned.1.call-start = ((), (), s32[]{:S(2)}) async-start(), calls=%async_computation.6 | async-start | bytes 10616832 | tf_op jit(solution)/shard_map/reduce_scatter | solution.py:1009
  19.8 137.7 %collective-permute-start.11 = (bf16[4,128,1536]{2,1,0:T(8,128)(2,1)}, bf16[4,128,1536]{2,1,0:T(8,128)(2,1)}, u32[]{:S(2)}, u32[]{:S(2)}) collective-permute-start(bf16[4,128,1536]{2,1,0:T(8,128)(2,1)} %get-tuple-element.263.first_ref), channel_id=1, source_target_pairs={{0,1},{1,0},{2,3},{3,2},{4,5},{5,4},{6,7},{7,6},{8,9},{9,8},{10,11... | collective-permute-start | bytes 4718600 | tf_op jit(solution)/shard_map/ppermute | solution.py:909
  22.7 108.7 %collective-permute-start.6 = (bf16[4,128,1536]{2,1,0:T(8,128)(2,1)}, bf16[4,128,1536]{2,1,0:T(8,128)(2,1)S(1)}, u32[]{:S(2)}, u32[]{:S(2)}) collective-permute-start(bf16[4,128,1536]{2,1,0:T(8,128)(2,1)} %get-tuple-element.263.first_ref), channel_id=1, source_target_pairs={{0,2},{2,0},{1,3},{3,1},{4,6},{6,4},{5,7},{7,5},{8,10},{10,8},{9,1... | collective-permute-start | bytes 4718600 | tf_op jit(solution)/shard_map/ppermute | solution.py:912
  24.3 108.7 %collective-permute-start.8 = (bf16[4,128,1536]{2,1,0:T(8,128)(2,1)}, bf16[4,128,1536]{2,1,0:T(8,128)(2,1)}, u32[]{:S(2)}, u32[]{:S(2)}) collective-permute-start(bf16[4,128,1536]{2,1,0:T(8,128)(2,1)} %get-tuple-element.262.second_ref), channel_id=1, source_target_pairs={{0,1},{1,0},{2,3},{3,2},{4,5},{5,4},{6,7},{7,6},{8,9},{9,8},{10,11... | collective-permute-start | bytes 4718600 | tf_op jit(solution)/shard_map/ppermute | solution.py:909
  24.8 144.9 %collective-permute-start.10 = (bf16[4,128,1536]{2,1,0:T(8,128)(2,1)}, bf16[4,128,1536]{2,1,0:T(8,128)(2,1)}, u32[]{:S(2)}, u32[]{:S(2)}) collective-permute-start(bf16[4,128,1536]{2,1,0:T(8,128)(2,1)} %get-tuple-element.262.second_ref), channel_id=1, source_target_pairs={{0,2},{2,0},{1,3},{3,1},{4,6},{6,4},{5,7},{7,5},{8,10},{10,8},{9,1... | collective-permute-start | bytes 4718600 | tf_op jit(solution)/shard_map/ppermute | solution.py:912
  26.7 68.7 %collective-permute-start.3 = (bf16[4,16,1536]{2,1,0:T(8,128)(2,1)}, bf16[4,16,1536]{2,1,0:T(8,128)(2,1)}, u32[]{:S(2)}, u32[]{:S(2)}) collective-permute-start(bf16[4,16,1536]{2,1,0:T(8,128)(2,1)} %get-tuple-element.250), channel_id=1, source_target_pairs={{0,1},{1,0},{2,3},{3,2},{4,5},{5,4},{6,7},{7,6},{8,9},{9,8},{10,11... | collective-permute-start | bytes 589832 | tf_op jit(solution)/shard_map/ppermute | solution.py:940
  95.4 6.1 collective-permute-start
  101.5 5.9 collective-permute-start.4
  107.4 7.1 collective-permute-start.1
  114.5 8.2 %collective-permute-start.5 = (bf16[4,16,1536]{2,1,0:T(8,128)(2,1)}, bf16[4,16,1536]{2,1,0:T(8,128)(2,1)S(1)}, u32[]{:S(2)}, u32[]{:S(2)}) collective-permute-start(bf16[4,16,1536]{2,1,0:T(8,128)(2,1)} %get-tuple-element.250), channel_id=1, source_target_pairs={{0,3},{3,0},{1,2},{2,1},{4,7},{7,4},{5,6},{6,5},{8,11},{11,8},{9,1... | collective-permute-start | bytes 589832 | tf_op jit(solution)/shard_map/ppermute | solution.py:940
  122.7 8.7 %collective-permute-start.2 = (bf16[4,16,1536]{2,1,0:T(8,128)(2,1)S(1)}, bf16[4,16,1536]{2,1,0:T(8,128)(2,1)S(1)}, u32[]{:S(2)}, u32[]{:S(2)}) collective-permute-start(bf16[4,16,1536]{2,1,0:T(8,128)(2,1)S(1)} %get-tuple-element.248), channel_id=1, source_target_pairs={{0,3},{3,0},{1,2},{2,1},{4,7},{7,4},{5,6},{6,5},{8,11},{11,8},{9,1... | collective-permute-start | bytes 589832 | tf_op jit(solution)/shard_map/ppermute | solution.py:940
  131.4 160.5 %copy-start.14 = (bf16[4,64,1536]{2,1,0:T(8,128)(2,1)}, bf16[4,64,1536]{2,1,0:T(8,128)(2,1)S(1)}, u32[]{:S(2)}) copy-start(bf16[4,64,1536]{2,1,0:T(8,128)(2,1)S(1)} %constant_dynamic-update-slice_fusion.4) | copy-start | bytes 2359300
  131.5 50.5 %collective-permute-start.7 = (bf16[4,128,1536]{2,1,0:T(8,128)(2,1)S(1)}, bf16[4,128,1536]{2,1,0:T(8,128)(2,1)}, u32[]{:S(2)}, u32[]{:S(2)}) collective-permute-start(bf16[4,128,1536]{2,1,0:T(8,128)(2,1)S(1)} %collective-permute-done.6.first_ref), channel_id=1, source_target_pairs={{0,1},{1,0},{2,3},{3,2},{4,5},{5,4},{6,7},{7,6},{8,9},{9,8},{10,11... | collective-permute-start | bytes 4718600 | tf_op jit(solution)/shard_map/ppermute | solution.py:909
  133.0 49.0 %collective-permute-start.9 = (bf16[4,128,1536]{2,1,0:T(8,128)(2,1)}, bf16[4,128,1536]{2,1,0:T(8,128)(2,1)}, u32[]{:S(2)}, u32[]{:S(2)}) collective-permute-start(bf16[4,128,1536]{2,1,0:T(8,128)(2,1)} %collective-permute-done.8.second_ref), channel_id=1, source_target_pairs={{0,2},{2,0},{1,3},{3,1},{4,6},{6,4},{5,7},{7,5},{8,10},{10,8},{9,1... | collective-permute-start | bytes 4718600 | tf_op jit(solution)/shard_map/ppermute | solution.py:912
  307.8 281.3 %reduce-scatter.6.cloned.1.call-start = ((), (), s32[]{:S(2)}) async-start(), calls=%async_computation.7 | async-start | bytes 15925248 | tf_op jit(solution)/shard_map/reduce_scatter | solution.py:1009
  312.8 105.6 %collective-permute-start.12 = (bf16[4,16,1536]{2,1,0:T(8,128)(2,1)S(1)}, bf16[4,16,1536]{2,1,0:T(8,128)(2,1)S(1)}, u32[]{:S(2)}, u32[]{:S(2)}) collective-permute-start(bf16[4,16,1536]{2,1,0:T(8,128)(2,1)S(1)} %get-tuple-element.276), channel_id=1, source_target_pairs={{0,1},{1,0},{2,3},{3,2},{4,5},{5,4},{6,7},{7,6},{8,9},{9,8},{10,11... | collective-permute-start | bytes 589832 | tf_op jit(solution)/shard_map/ppermute | solution.py:981
  314.4 104.0 %collective-permute-start.13 = (bf16[4,16,1536]{2,1,0:T(8,128)(2,1)S(1)}, bf16[4,16,1536]{2,1,0:T(8,128)(2,1)S(1)}, u32[]{:S(2)}, u32[]{:S(2)}) collective-permute-start(bf16[4,16,1536]{2,1,0:T(8,128)(2,1)S(1)} %get-tuple-element.278), channel_id=1, source_target_pairs={{0,2},{2,0},{1,3},{3,1},{4,6},{6,4},{5,7},{7,5},{8,10},{10,8},{9,1... | collective-permute-start | bytes 589832 | tf_op jit(solution)/shard_map/ppermute | solution.py:981
  315.9 102.5 %collective-permute-start.14 = (bf16[4,16,1536]{2,1,0:T(8,128)(2,1)S(1)}, bf16[4,16,1536]{2,1,0:T(8,128)(2,1)S(1)}, u32[]{:S(2)}, u32[]{:S(2)}) collective-permute-start(bf16[4,16,1536]{2,1,0:T(8,128)(2,1)S(1)} %get-tuple-element.277), channel_id=1, source_target_pairs={{0,3},{3,0},{1,2},{2,1},{4,7},{7,4},{5,6},{6,5},{8,11},{11,8},{9,1... | collective-permute-start | bytes 589832 | tf_op jit(solution)/shard_map/ppermute | solution.py:981
  362.9 25.9 %copy-start.38 = (bf16[256,384]{1,0:T(8,128)(2,1)S(1)}, bf16[256,384]{1,0:T(8,128)(2,1)}, u32[]{:S(2)}) copy-start(bf16[256,384]{1,0:T(8,128)(2,1)} %attend.3) | copy-start | bytes 589828
  363.0 25.9 %copy-start.46 = (bf16[4,64,1536]{2,1,0:T(8,128)(2,1)S(1)}, bf16[4,64,1536]{2,1,0:T(8,128)(2,1)}, u32[]{:S(2)}) copy-start(bf16[4,64,1536]{2,1,0:T(8,128)(2,1)} %get-tuple-element.98) | copy-start | bytes 2359300
  430.8 220.6 %reduce-scatter.8.cloned.1.call-start = ((), (), s32[]{:S(2)}) async-start(), calls=%async_computation.8 | async-start | bytes 5308416 | tf_op jit(solution)/shard_map/reduce_scatter | solution.py:1009
  434.7 80.5 %copy-start.25 = (bf16[1536,768]{1,0:T(8,128)(2,1)}, bf16[1536,768]{1,0:T(8,128)(2,1)S(1)}, u32[]{:S(2)}) copy-start(bf16[1536,768]{1,0:T(8,128)(2,1)S(1)} %get-tuple-element.259) | copy-start | bytes 7077892
  519.1 37.6 %collective-permute-start.17 = (bf16[4,128,1536]{2,1,0:T(8,128)(2,1)}, bf16[4,128,1536]{2,1,0:T(8,128)(2,1)}, u32[]{:S(2)}, u32[]{:S(2)}) collective-permute-start(bf16[4,128,1536]{2,1,0:T(8,128)(2,1)} %bitcast.54), channel_id=1, source_target_pairs={{0,1},{1,0},{2,3},{3,2},{4,5},{5,4},{6,7},{7,6},{8,9},{9,8},{10,11... | collective-permute-start | bytes 4718600 | tf_op jit(solution)/shard_map/ppermute | solution.py:909
  520.6 37.7 %collective-permute-start.18 = (bf16[4,128,1536]{2,1,0:T(8,128)(2,1)}, bf16[4,128,1536]{2,1,0:T(8,128)(2,1)}, u32[]{:S(2)}, u32[]{:S(2)}) collective-permute-start(bf16[4,128,1536]{2,1,0:T(8,128)(2,1)} %bitcast.56), channel_id=1, source_target_pairs={{0,2},{2,0},{1,3},{3,1},{4,6},{6,4},{5,7},{7,5},{8,10},{10,8},{9,1... | collective-permute-start | bytes 4718600 | tf_op jit(solution)/shard_map/ppermute | solution.py:912
  522.0 66.7 %collective-permute-start.15 = (bf16[4,128,1536]{2,1,0:T(8,128)(2,1)}, bf16[4,128,1536]{2,1,0:T(8,128)(2,1)}, u32[]{:S(2)}, u32[]{:S(2)}) collective-permute-start(bf16[4,128,1536]{2,1,0:T(8,128)(2,1)} %bitcast.50), channel_id=1, source_target_pairs={{0,1},{1,0},{2,3},{3,2},{4,5},{5,4},{6,7},{7,6},{8,9},{9,8},{10,11... | collective-permute-start | bytes 4718600 | tf_op jit(solution)/shard_map/ppermute | solution.py:909
  522.6 66.5 %collective-permute-start.16 = (bf16[4,128,1536]{2,1,0:T(8,128)(2,1)}, bf16[4,128,1536]{2,1,0:T(8,128)(2,1)}, u32[]{:S(2)}, u32[]{:S(2)}) collective-permute-start(bf16[4,128,1536]{2,1,0:T(8,128)(2,1)} %bitcast.52), channel_id=1, source_target_pairs={{0,2},{2,0},{1,3},{3,1},{4,6},{6,4},{5,7},{7,5},{8,10},{10,8},{9,1... | collective-permute-start | bytes 4718600 | tf_op jit(solution)/shard_map/ppermute | solution.py:912
  550.0 39.1 %copy-start.1 = (bf16[256,4,1536]{2,1,0:T(4,128)(2,1)S(1)}, bf16[256,4,1536]{2,1,0:T(4,128)(2,1)}, u32[]{:S(2)}) copy-start(bf16[256,4,1536]{2,1,0:T(4,128)(2,1)} %param.19) | copy-start | bytes 9437188
  597.8 36.0 %collective-permute-start.20 = (bf16[4,128,1536]{2,1,0:T(8,128)(2,1)}, bf16[4,128,1536]{2,1,0:T(8,128)(2,1)}, u32[]{:S(2)}, u32[]{:S(2)}) collective-permute-start(bf16[4,128,1536]{2,1,0:T(8,128)(2,1)} %add.253), channel_id=1, source_target_pairs={{0,2},{2,0},{1,3},{3,1},{4,6},{6,4},{5,7},{7,5},{8,10},{10,8},{9,1... | collective-permute-start | bytes 4718600 | tf_op jit(solution)/shard_map/ppermute | solution.py:912
  602.5 35.7 %collective-permute-start.19 = (bf16[4,128,1536]{2,1,0:T(8,128)(2,1)}, bf16[4,128,1536]{2,1,0:T(8,128)(2,1)}, u32[]{:S(2)}, u32[]{:S(2)}) collective-permute-start(bf16[4,128,1536]{2,1,0:T(8,128)(2,1)} %add.252), channel_id=1, source_target_pairs={{0,1},{1,0},{2,3},{3,2},{4,5},{5,4},{6,7},{7,6},{8,9},{9,8},{10,11... | collective-permute-start | bytes 4718600 | tf_op jit(solution)/shard_map/ppermute | solution.py:909
  (70 other events, 494.0 us)
Sparse Core Ops, SparseCore 0:
  10.4 93.4 all-gather.5
  106.1 89.1 all-gather.7
  197.5 89.1 all-gather.3
  307.9 97.9 reduce-scatter.3
  430.9 142.5 reduce-scatter.5
  589.3 54.0 reduce-scatter.7

commit v3 on v2

--- a/solution.py
+++ b/solution.py
@@ -48,19 +48,19 @@
 
 
 def gather_slots(rows):
-    return lax.all_gather(rows, "heads", axis=1, tiled=True)
+    return lax.all_gather(rows, HEADS, axis=1, tiled=True)
 
 
 def scatter_slots(terms):
-    return lax.psum_scatter(terms, "heads", scatter_dimension=1, tiled=True)
+    return lax.psum_scatter(terms, HEADS, scatter_dimension=1, tiled=True)
 
 
 def gather_slopes(rows):
-    return lax.all_gather(rows, "heads", axis=1, tiled=True)
+    return lax.all_gather(rows, HEADS, axis=1, tiled=True)
 
 
 def scatter_slopes(terms):
-    return lax.psum_scatter(terms, "heads", scatter_dimension=1, tiled=True)
+    return lax.psum_scatter(terms, HEADS, scatter_dimension=1, tiled=True)
 
 
 def both_scores(query, media_pair, latent_pair, live, scale):
@@ -162,7 +162,7 @@
     gain_first,
     gain_second,
 ):
-    heads_count = lax.axis_size("heads")
+    heads_count = lax.axis_size(HEADS)
     layers, _, row_share, head_columns = inward.shape
     local_positions, videos, width = media.shape
     positions = local_positions * heads_count
@@ -171,10 +171,10 @@
     scale = HD ** (-0.5)
     live = (jnp.arange(positions, dtype=jnp.int32) // PATCHES)[None, :] < frame_count[:, None]
     inward_columns, outward_rows, widen_columns, narrow_rows = (
-        lax.all_gather(inward.astype(jnp.bfloat16), "rows", axis=2, tiled=True),
-        lax.all_gather(outward.astype(jnp.bfloat16), "rows", axis=2, tiled=True),
-        lax.all_gather(widen.astype(jnp.bfloat16), "rows", axis=1, tiled=True),
-        lax.all_gather(narrow.astype(jnp.bfloat16), "rows", axis=2, tiled=True),
+        lax.all_gather(inward.astype(jnp.bfloat16), ROWS, axis=2, tiled=True),
+        lax.all_gather(outward.astype(jnp.bfloat16), ROWS, axis=2, tiled=True),
+        lax.all_gather(widen.astype(jnp.bfloat16), ROWS, axis=1, tiled=True),
+        lax.all_gather(narrow.astype(jnp.bfloat16), ROWS, axis=2, tiled=True),
     )
     media_rows = media.astype(jnp.float32)
     latent = latents
@@ -189,7 +189,7 @@
         pair_columns = inward_columns[layer, 1:3]
         media_pair = jnp.einsum(
             "pvd,tdc->tpvc",
-            lax.all_gather(media_norm, "heads", axis=0, tiled=True),
+            lax.all_gather(media_norm, HEADS, axis=0, tiled=True),
             pair_columns,
             preferred_element_type=jnp.float32,
         ).astype(jnp.bfloat16)
@@ -303,7 +303,7 @@
         pair_slope = media_slopes.reshape(2, positions, videos, head_columns)
         media_columns = jnp.einsum(
             "pvd,tpvc->tdc",
-            lax.all_gather(media_norm, "heads", axis=0, tiled=True),
+            lax.all_gather(media_norm, HEADS, axis=0, tiled=True),
             pair_slope,
             preferred_element_type=jnp.float32,
         )
@@ -313,7 +313,7 @@
             jnp.einsum(
                 "tpvc,tdc->pvd", pair_slope, pair_columns, preferred_element_type=jnp.float32
             ),
-            "heads",
+            HEADS,
             scatter_dimension=0,
             tiled=True,
         )
@@ -329,14 +329,14 @@
             jnp.stack((gain_media, shift_media, gain_latent, shift_latent, gain_feed, shift_feed))
         )
     inward_grad, outward_grad, widen_grad, narrow_grad = (
-        lax.psum_scatter(jnp.stack(inward_parts[::-1]), "rows", scatter_dimension=2, tiled=True),
-        lax.psum_scatter(jnp.stack(outward_parts[::-1]), "rows", scatter_dimension=2, tiled=True),
-        lax.psum_scatter(jnp.stack(widen_parts[::-1]), "rows", scatter_dimension=1, tiled=True),
-        lax.psum_scatter(jnp.stack(narrow_parts[::-1]), "rows", scatter_dimension=2, tiled=True),
+        lax.psum_scatter(jnp.stack(inward_parts[::-1]), ROWS, scatter_dimension=2, tiled=True),
+        lax.psum_scatter(jnp.stack(outward_parts[::-1]), ROWS, scatter_dimension=2, tiled=True),
+        lax.psum_scatter(jnp.stack(widen_parts[::-1]), ROWS, scatter_dimension=1, tiled=True),
+        lax.psum_scatter(jnp.stack(narrow_parts[::-1]), ROWS, scatter_dimension=2, tiled=True),
     )
     squares = jnp.sum(inward_grad * inward_grad) + jnp.sum(outward_grad * outward_grad)
     squares = squares + jnp.sum(widen_grad * widen_grad) + jnp.sum(narrow_grad * narrow_grad)
-    gain_total, square_total = lax.psum((jnp.stack(gain_parts[::-1]), squares), ("rows", "heads"))
+    gain_total, square_total = lax.psum((jnp.stack(gain_parts[::-1]), squares), (ROWS, HEADS))
     gradient_norm = jnp.sqrt(square_total + jnp.sum(gain_total * gain_total))
     factor = CLIP_LEVEL / jnp.maximum(gradient_norm, CLIP_LEVEL)
     table = (
@@ -360,7 +360,8 @@
 
 BF = jnp.bfloat16
 F32 = jnp.float32
-VMEM_LIMIT = 60 * 1024 * 1024
+MIB = 1024 * 1024
+HEADS, ROWS = "heads", "rows"
 NT = (((1,), (1,)), ((), ()))
 TN = (((0,), (0,)), ((), ()))
 X_SWAP = ((0, 1), (1, 0), (2, 3), (3, 2))
@@ -377,19 +378,94 @@
     return lax.dot_general(left, right, dims, preferred_element_type=F32).astype(out)
 
 
-def media_kernel(first_ref, second_ref, gain_ref, weight_ref, *rest):
-    keys_ref, hat_ref, rows_ref = rest[-3:]
-    half, layer = pl.program_id(0), pl.program_id(1)
-
+def greet(count):
+    me = lax.axis_index(HEADS)
+    barrier = pltpu.get_barrier_semaphore()
+    for step in range(1, count):
+        pl.semaphore_signal(barrier, inc=1, device_id={HEADS: (me + step) % count})
+    pl.semaphore_wait(barrier, count - 1)
+    return me
+
+
+def own_rows(ref, place, share):
+    return ref.at[:, pl.ds(pl.multiple_of(place * share, share), share), :]
+
+
+def start_gather(me, count, share, own_ref, full_ref, send_sem, recv_sem):
+    copies = []
+    for step in range(1, count):
+        copy = pltpu.make_async_remote_copy(
+            src_ref=own_ref,
+            dst_ref=own_rows(full_ref, me, share),
+            send_sem=send_sem.at[step - 1],
+            recv_sem=recv_sem.at[step - 1],
+            device_id={HEADS: (me + step) % count},
+        )
+        copy.start()
+        copies.append(copy)
+    return copies
+
+
+def beside(me):
+    return me + 1 - 2 * (me % 2), me + 2 - 4 * (me // 2)
+
+
+def gather_kernel(count, own_ref, norm_ref, near_ref, full_ref, send_sem, recv_sem, norm_send, norm_recv):
+    me = greet(count)
+    beside_x, beside_y = beside(me)
+    share = norm_ref.shape[1]
+    copies = start_gather(me, count, share, norm_ref, full_ref, norm_send, norm_recv)
+    for at, (half, slot, peer) in enumerate(
+        ((1, 1, beside_x), (0, 2, beside_y), (0, 0, beside_x), (1, 3, beside_y))
+    ):
+        copy = pltpu.make_async_remote_copy(
+            src_ref=own_ref.at[half],
+            dst_ref=near_ref.at[slot],
+            send_sem=send_sem.at[at],
+            recv_sem=recv_sem.at[at],
+            device_id={HEADS: peer},
+        )
+        copy.start()
+        copies.append(copy)
+    full_ref[:, pl.ds(pl.multiple_of(me * share, share), share), :] = norm_ref[...]
+    for copy in copies:
+        copy.wait()
+
+
+def gather_near(own, norm, count):
+    videos, share, width = norm.shape
+    any_spec = pl.BlockSpec(memory_space=pl.ANY)
+    return pl.pallas_call(
+        functools.partial(gather_kernel, count),
+        out_shape=(
+            jax.ShapeDtypeStruct((4, *own.shape[1:]), BF),
+            jax.ShapeDtypeStruct((videos, share * count, width), BF),
+        ),
+        in_specs=[any_spec, vmem_spec()],
+        out_specs=(any_spec, vmem_spec()),
+        scratch_shapes=[pltpu.SemaphoreType.DMA((4,))] * 2 + [pltpu.SemaphoreType.DMA((count - 1,))] * 2,
+        compiler_params=pltpu.CompilerParams(
+            collective_id=1, has_side_effects=True, vmem_limit_bytes=60 * MIB
+        ),
+        cost_estimate=pl.CostEstimate(flops=0, bytes_accessed=250 * 1000 * 1000, transcendentals=0),
+        name="gather_near",
+    )(own, norm)
+
+
+def media_rows(half, layer, chunk_ref, gain_ref, weight_ref, keys_ref, hat_ref, rows_ref, other_ref=None):
     @pl.when(layer == 0)
     def _():
-        @pl.when(half == 0)
-        def _():
-            rows_ref[...] = first_ref[...].astype(F32).reshape(rows_ref.shape)
-
-        @pl.when(half == 1)
-        def _():
-            rows_ref[...] = second_ref[...].astype(F32).reshape(rows_ref.shape)
+        if other_ref is None:
+            rows_ref[...] = chunk_ref[0].astype(F32).reshape(rows_ref.shape)
+        else:
+
+            @pl.when(half < 2)
+            def _():
+                rows_ref[...] = chunk_ref[0].astype(F32).reshape(rows_ref.shape)
+
+            @pl.when(half >= 2)
+            def _():
+                rows_ref[...] = other_ref[0].astype(F32).reshape(rows_ref.shape)
 
         rows = rows_ref[...]
         centred = rows - jnp.mean(rows, axis=-1, keepdims=True)
@@ -404,42 +480,157 @@
     keys_ref[...] = jnp.dot(normed, weight_ref[...], preferred_element_type=F32).astype(BF).reshape(keys_ref.shape)
 
 
-def media_part(first, second, gains, weight, group, earlier):
-    videos, patches, width = first.shape
-    columns = weight.shape[1]
-    kinds = (
-        jax.ShapeDtypeStruct((8, videos, patches, columns), BF),
-        jax.ShapeDtypeStruct((8, videos, patches, width), BF),
-    )
-    whole = pl.BlockSpec((videos, patches, width), lambda i, j: (0, 0, 0))
-    in_specs = [
-        whole,
-        whole,
-        pl.BlockSpec(gains.shape, lambda i, j: (0, 0, 0)),
-        pl.BlockSpec((width, columns // 2), lambda i, j: (0, j)),
-    ]
-    aliases = {}
-    if earlier:
-        in_specs += [pl.BlockSpec(memory_space=pl.ANY)] * 2
-        aliases = {4: 0, 5: 1}
+def near_kernel(
+    count, own_ref, near_ref, gain_ref, weight_ref, source_ref, keys_ref, hat_ref, far_ref, rows_ref, send_sem, recv_sem
+):
+    half, layer = pl.program_id(0), pl.program_id(1)
+    me = lax.axis_index(HEADS)
+    beside_x, beside_y = beside(me)
+
+    def relays():
+        return [
+            pltpu.make_async_remote_copy(
+                src_ref=source_ref.at[slot],
+                dst_ref=far_ref.at[at],
+                send_sem=send_sem.at[at],
+                recv_sem=recv_sem.at[at],
+                device_id={HEADS: peer},
+            )
+            for at, (slot, peer) in enumerate(((2, beside_x), (1, beside_y)))
+        ]
+
+    @pl.when((half == 0) & (layer == 0))
+    def _():
+        barrier = pltpu.get_barrier_semaphore()
+        for peer in (beside_x, beside_y):
+            pl.semaphore_signal(barrier, inc=1, device_id={HEADS: peer})
+        pl.semaphore_wait(barrier, 2)
+        for copy in relays():
+            copy.start()
+
+    media_rows(half, layer, own_ref, gain_ref, weight_ref, keys_ref, hat_ref, rows_ref, near_ref)
+
+    @pl.when((half == 5) & (layer == 1))
+    def _():
+        for copy in relays():
+            copy.wait()
+
+
+def media_near(own, near, gains, weight, columns, count):
+    _, videos, patches, width = own.shape
     rows = videos * patches
+    any_spec = pl.BlockSpec(memory_space=pl.ANY)
     return pl.pallas_call(
-        media_kernel,
+        functools.partial(near_kernel, count),
+        grid=(6, 2),
+        out_shape=(
+            jax.ShapeDtypeStruct((8, videos, patches, columns), BF),
+            jax.ShapeDtypeStruct((8, videos, patches, width), BF),
+            jax.ShapeDtypeStruct(own.shape, BF),
+        ),
+        in_specs=[
+            pl.BlockSpec((1, videos, patches, width), lambda i, j: (jnp.minimum(i, 1), 0, 0, 0)),
+            pl.BlockSpec((1, videos, patches, width), lambda i, j: (jnp.maximum(i - 2, 0), 0, 0, 0)),
+            pl.BlockSpec(gains.shape, lambda i, j: (0, 0, 0)),
+            pl.BlockSpec((width, columns // 2), lambda i, j: (0, j)),
+            any_spec,
+        ],
+        out_specs=(
+            pl.BlockSpec((1, videos, patches, columns // 2), lambda i, j: (i, 0, 0, j)),
+            pl.BlockSpec((1, videos, patches, width), lambda i, j: (i, 0, 0, 0)),
+            any_spec,
+        ),
+        scratch_shapes=[
+            pltpu.VMEM((rows, width), F32),
+            pltpu.SemaphoreType.DMA((2,)),
+            pltpu.SemaphoreType.DMA((2,)),
+        ],
+        compiler_params=pltpu.CompilerParams(
+            collective_id=6, has_side_effects=True, vmem_limit_bytes=60 * MIB
+        ),
+        cost_estimate=pl.CostEstimate(
+            flops=12 * rows * width * columns, bytes_accessed=24 * rows * width, transcendentals=0
+        ),
+        name="media_near",
+    )(own, near, gains, weight, near)
+
+
+def far_kernel(
+    count, chunk_ref, gain_ref, weight_ref, slope_ref, keys_in, hat_in, keys_ref, hat_ref, full_ref, rows_ref, *sems
+):
+    half, layer = pl.program_id(0), pl.program_id(1)
+    send_sem, recv_sem, own_sem = sems
+    me = lax.axis_index(HEADS)
+    share = slope_ref.shape[1]
+
+    def copies():
+        return [
+            pltpu.make_async_remote_copy(
+                src_ref=slope_ref,
+                dst_ref=own_rows(full_ref, me, share),
+                send_sem=send_sem.at[step - 1],
+                recv_sem=recv_sem.at[step - 1],
+                device_id={HEADS: (me + step) % count},
+            )
+            for step in range(1, count)
+        ] + [pltpu.make_async_copy(slope_ref, own_rows(full_ref, me, share), own_sem)]
+
+    @pl.when((half == 0) & (layer == 0))
+    def _():
+        greet(count)
+        for copy in copies():
+            copy.start()
+
+    media_rows(half, layer, chunk_ref, gain_ref, weight_ref, keys_ref, hat_ref, rows_ref)
+
+    @pl.when((half == 1) & (layer == 1))
+    def _():
+        for copy in copies():
+            copy.wait()
+
+
+def media_far(far, gains, weight, slope, keys, hat, count):
+    _, videos, patches, width = far.shape
+    columns = keys.shape[3]
+    rows = videos * patches
+    share = slope.shape[1]
+    any_spec = pl.BlockSpec(memory_space=pl.ANY)
+    return pl.pallas_call(
+        functools.partial(far_kernel, count),
         grid=(2, 2),
-        out_shape=kinds,
-        in_specs=in_specs,
+        out_shape=(
+            jax.ShapeDtypeStruct(keys.shape, BF),
+            jax.ShapeDtypeStruct(hat.shape, BF),
+            jax.ShapeDtypeStruct((videos, share * count, width), BF),
+        ),
+        in_specs=[
+            pl.BlockSpec((1, videos, patches, width), lambda i, j: (i, 0, 0, 0)),
+            pl.BlockSpec(gains.shape, lambda i, j: (0, 0, 0)),
+            pl.BlockSpec((width, columns // 2), lambda i, j: (0, j)),
+            any_spec,
+            any_spec,
+            any_spec,
+        ],
         out_specs=(
-            pl.BlockSpec((1, videos, patches, columns // 2), lambda i, j: (2 * group + i, 0, 0, j)),
-            pl.BlockSpec((1, videos, patches, width), lambda i, j: (2 * group + i, 0, 0, 0)),
-        ),
-        scratch_shapes=[pltpu.VMEM((rows, width), F32)],
-        input_output_aliases=aliases,
-        compiler_params=pltpu.CompilerParams(vmem_limit_bytes=VMEM_LIMIT),
+            pl.BlockSpec((1, videos, patches, columns // 2), lambda i, j: (6 + i, 0, 0, j)),
+            pl.BlockSpec((1, videos, patches, width), lambda i, j: (6 + i, 0, 0, 0)),
+            any_spec,
+        ),
+        scratch_shapes=[
+            pltpu.VMEM((rows, width), F32),
+            pltpu.SemaphoreType.DMA((count - 1,)),
+            pltpu.SemaphoreType.DMA((count - 1,)),
+            pltpu.SemaphoreType.DMA,
+        ],
+        input_output_aliases={4: 0, 5: 1},
+        compiler_params=pltpu.CompilerParams(
+            collective_id=8, has_side_effects=True, vmem_limit_bytes=60 * MIB
+        ),
         cost_estimate=pl.CostEstimate(
             flops=4 * rows * width * columns, bytes_accessed=8 * rows * width, transcendentals=0
         ),
-        name="media_part",
-    )(first, second, gains, weight, *earlier)
+        name="media_far",
+    )(far, gains, weight, slope, keys, hat)
 
 
 def head_mask(rows, columns, head):
@@ -507,7 +698,7 @@
             pl.BlockSpec((slots, 1, patches, columns), lambda v: (0, v, 0, 2 * layer + 1)),
         ],
         out_specs=row_block,
-        compiler_params=pltpu.CompilerParams(vmem_limit_bytes=VMEM_LIMIT),
+        compiler_params=pltpu.CompilerParams(vmem_limit_bytes=28 * MIB),
         cost_estimate=pl.CostEstimate(
             flops=8 * slots * patches * videos * count * 2 * columns,
             bytes_accessed=4 * slots * videos * patches * columns,
@@ -603,7 +794,7 @@
             pl.BlockSpec((slots, 1, patches, 2 * columns), lambda v: (0, v, 0, layer)),
         ),
         input_output_aliases=aliases,
-        compiler_params=pltpu.CompilerParams(vmem_limit_bytes=VMEM_LIMIT),
+        compiler_params=pltpu.CompilerParams(vmem_limit_bytes=60 * MIB),
         cost_estimate=pl.CostEstimate(
             flops=20 * slots * patches * videos * count * 2 * columns,
             bytes_accessed=8 * slots * videos * patches * columns,
@@ -615,17 +806,18 @@
 
 def product_pair_kernel(first_ref, second_ref, third_ref, fourth_ref, *rest):
     out_ref = rest[-1]
-
-    @pl.when(pl.program_id(0) == 0)
+    kind = pl.program_id(0) - (len(rest) - 1)
+
+    @pl.when(kind == 0)
     def _():
         out_ref[...] = mm(first_ref[...], second_ref[...], TN)
 
-    @pl.when(pl.program_id(0) == 1)
+    @pl.when(kind == 1)
     def _():
         out_ref[...] = mm(third_ref[...], fourth_ref[...], TN)
 
     if len(rest) > 1:
-        @pl.when(pl.program_id(0) == 2)
+        @pl.when(kind < 0)
         def _():
             out_ref[...] = rest[0][...]
 
@@ -634,52 +826,29 @@
     rows, width, columns = first.shape[0], first.shape[1], second.shape[1]
     cut = columns // 3
     left = pl.BlockSpec((rows, width), lambda i, j: (0, 0))
+    first_kind = len(extra)
+
+    def at(i, j, kind):
+        return jnp.where(i == kind, j, jnp.where(i < kind, 0, 2))
+
     return pl.pallas_call(
         product_pair_kernel,
         grid=(2 + len(extra), 3),
         out_shape=jax.ShapeDtypeStruct((width, (2 + len(extra)) * columns), BF),
         in_specs=[
             left,
-            pl.BlockSpec((rows, cut), lambda i, j: (0, jnp.where(i == 0, j, 2))),
+            pl.BlockSpec((rows, cut), lambda i, j: (0, at(i, j, first_kind))),
             left,
-            pl.BlockSpec((rows, cut), lambda i, j: (0, jnp.where(i == 0, 0, jnp.where(i == 1, j, 2)))),
+            pl.BlockSpec((rows, cut), lambda i, j: (0, at(i, j, first_kind + 1))),
         ]
-        + [pl.BlockSpec((width, cut), lambda i, j: (0, jnp.where(i == 2, j, 0)))] * len(extra),
+        + [pl.BlockSpec((width, cut), lambda i, j: (0, at(i, j, 0)))] * len(extra),
         out_specs=pl.BlockSpec((width, cut), lambda i, j: (0, 3 * i + j)),
-        compiler_params=pltpu.CompilerParams(vmem_limit_bytes=VMEM_LIMIT),
+        compiler_params=pltpu.CompilerParams(vmem_limit_bytes=60 * MIB),
         cost_estimate=pl.CostEstimate(
             flops=4 * rows * width * columns, bytes_accessed=8 * width * columns, transcendentals=0
         ),
         name="feed_gradients",
     )(first, second, third, fourth, *extra)
-
-
-def greet(count):
-    me = lax.axis_index("heads")
-    barrier = pltpu.get_barrier_semaphore()
-    for step in range(1, count):
-        pl.semaphore_signal(barrier, inc=1, device_id={"heads": (me + step) % count})
-    pl.semaphore_wait(barrier, count - 1)
-    return me
-
-
-def own_rows(ref, place, share):
-    return ref.at[:, pl.ds(pl.multiple_of(place * share, share), share), :]
-
-
-def start_gather(me, count, share, own_ref, full_ref, send_sem, recv_sem):
-    copies = []
-    for step in range(1, count):
-        copy = pltpu.make_async_remote_copy(
-            src_ref=own_ref,
-            dst_ref=own_rows(full_ref, me, share),
-            send_sem=send_sem.at[step - 1],
-            recv_sem=recv_sem.at[step - 1],
-            device_id={"heads": (me + step) % count},
-        )
-        copy.start()
-        copies.append(copy)
-    return copies
 
 
 def start_scatter(me, count, share, part_ref, landed_ref, send_sem, recv_sem):
@@ -691,7 +860,7 @@
             dst_ref=landed_ref.at[step - 1],
             send_sem=send_sem.at[step - 1],
             recv_sem=recv_sem.at[step - 1],
-            device_id={"heads": peer},
+            device_id={HEADS: peer},
         )
         copy.start()
         copies.append(copy)
@@ -739,7 +908,7 @@
         ]
         + [pltpu.SemaphoreType.DMA((count - 1,))] * 4,
         compiler_params=pltpu.CompilerParams(
-            collective_id=3 if last else 2, has_side_effects=True, vmem_limit_bytes=VMEM_LIMIT
+            collective_id=3 if last else 2, has_side_effects=True, vmem_limit_bytes=14 * MIB
         ),
         cost_estimate=pl.CostEstimate(flops=0, bytes_accessed=75 * 1000 * 1000, transcendentals=0),
         name="forward_exchange",
@@ -799,7 +968,7 @@
         ]
         + [pltpu.SemaphoreType.DMA((count - 1,))] * 4,
         compiler_params=pltpu.CompilerParams(
-            collective_id=5 if last else 4, has_side_effects=True, vmem_limit_bytes=VMEM_LIMIT
+            collective_id=5 if last else 4, has_side_effects=True, vmem_limit_bytes=14 * MIB
         ),
         cost_estimate=pl.CostEstimate(flops=0, bytes_accessed=75 * 1000 * 1000, transcendentals=0),
         name="backward_exchange",
@@ -808,12 +977,12 @@
 
 
 def sum_kernel(heads, rows, term_ref, out_ref, plane_ref, line_ref, part_ref, *sems):
-    me_head, me_row = lax.axis_index("heads"), lax.axis_index("rows")
+    me_head, me_row = lax.axis_index(HEADS), lax.axis_index(ROWS)
     barrier = pltpu.get_barrier_semaphore()
     for step in range(1, heads):
-        pl.semaphore_signal(barrier, inc=1, device_id={"heads": (me_head + step) % heads})
+        pl.semaphore_signal(barrier, inc=1, device_id={HEADS: (me_head + step) % heads})
     for step in range(1, rows):
-        pl.semaphore_signal(barrier, inc=1, device_id={"rows": (me_row + step) % rows})
+        pl.semaphore_signal(barrier, inc=1, device_id={ROWS: (me_row + step) % rows})
     pl.semaphore_wait(barrier, heads - 1 + rows - 1)
 
     def spread(axis, me, count, source_of, slots_ref, own, send, recv):
@@ -840,11 +1009,11 @@
         return total
 
     mine = term_ref[pl.ds(me_head, 1)][0]
-    spread("heads", me_head, heads, lambda peer: term_ref.at[peer], plane_ref, mine, *sems[0:2])
+    spread(HEADS, me_head, heads, lambda peer: term_ref.at[peer], plane_ref, mine, *sems[0:2])
     part_ref[0] = added(plane_ref, heads)
-    spread("rows", me_row, rows, lambda peer: part_ref.at[0], line_ref, part_ref[0], *sems[2:4])
+    spread(ROWS, me_row, rows, lambda peer: part_ref.at[0], line_ref, part_ref[0], *sems[2:4])
     part_ref[1] = added(line_ref, rows)
-    spread("heads", me_head, heads, lambda peer: part_ref.at[1], out_ref, part_ref[1], *sems[4:6])
+    spread(HEADS, me_head, heads, lambda peer: part_ref.at[1], out_ref, part_ref[1], *sems[4:6])
 
 
 def sum_fast(term, heads, rows, identity):
@@ -866,11 +1035,359 @@
             pltpu.SemaphoreType.DMA((heads - 1,)),
         ],
         compiler_params=pltpu.CompilerParams(
-            collective_id=identity, has_side_effects=True, vmem_limit_bytes=VMEM_LIMIT
+            collective_id=identity, has_side_effects=True, vmem_limit_bytes=8 * MIB
         ),
         cost_estimate=pl.CostEstimate(flops=0, bytes_accessed=40 * 1000 * 1000, transcendentals=0),
         name="sum_over_all",
     )(term)
+
+
+def last_kernel(
+    chips,
+    heads,
+    part_ref,
+    to_x_ref,
+    to_y_ref,
+    slots_ref,
+    final_ref,
+    final_rest_ref,
+    rows_ref,
+    rest_ref,
+    gain_ref,
+    out_ref,
+    from_x_ref,
+    from_y_ref,
+    new_ref,
+    sums_ref,
+    final_out_ref,
+    mine_ref,
+    other_ref,
+    down_ref,
+    up_ref,
+    landed_ref,
+    final_landed_ref,
+    near_sem,
+    slot_send,
+    slot_recv,
+    final_send,
+    final_recv,
+    down_send,
+    down_recv,
+    up_send,
+    up_recv,
+):
+    head, place = lax.axis_index(HEADS), lax.axis_index(ROWS)
+    z, core = place // 2, place % 2
+    sibling, above, below = place + 1 - 2 * core, place + 2, place - 2
+    beside_x, beside_y = head + 1 - 2 * (head % 2), (head + 2) % heads
+    has_above, has_below = z < chips - 1, z > 0
+    depth = out_ref.shape[0]
+    pieces = down_send.shape[1]
+    cut = depth // pieces
+
+    barrier = pltpu.get_barrier_semaphore()
+    for step in range(1, heads):
+        pl.semaphore_signal(barrier, inc=1, device_id={HEADS: (head + step) % heads})
+    pl.semaphore_signal(barrier, inc=1, device_id={ROWS: sibling})
+
+    for step in (2, 2 * chips - 2):
+        pl.semaphore_signal(barrier, inc=1, device_id={ROWS: (place + step) % (2 * chips)})
+    pl.semaphore_wait(barrier, heads + 2)
+
+    share = rest_ref.shape[1]
+    slots = start_scatter(head, heads, share, slots_ref, landed_ref, slot_send, slot_recv)
+    finals = start_scatter(head, heads, share, final_ref, final_landed_ref, final_send, final_recv)
+    over = pltpu.make_async_remote_copy(
+        src_ref=part_ref.at[:, 1 - core],
+        dst_ref=other_ref,
+        send_sem=near_sem.at[0],
+        recv_sem=near_sem.at[1],
+        device_id={ROWS: sibling},
+    )
+    over.start()
+    keep = pltpu.make_async_copy(part_ref.at[:, core], mine_ref, near_sem.at[2])
+    keep.start()
+    media_x = pltpu.make_async_remote_copy(
+        src_ref=to_x_ref,
+        dst_ref=from_x_ref,
+        send_sem=near_sem.at[3],
+        recv_sem=near_sem.at[4],
+        device_id={HEADS: beside_x},
+    )
+    media_y = pltpu.make_async_remote_copy(
+        src_ref=to_y_ref,
+        dst_ref=from_y_ref,
+        send_sem=near_sem.at[5],
+        recv_sem=near_sem.at[6],
+        device_id={HEADS: beside_y},
+    )
+    media_x.start()
+    media_y.start()
+    keep.wait()
+    over.wait()
+    for chip in range(chips):
+
+        def add_rows(at, carry, chip=chip):
+            lines = pl.ds(pl.multiple_of(at * 16, 16), 16)
+            mine_ref[chip, lines] = (
+                mine_ref[chip, lines].astype(F32) + other_ref[chip, lines].astype(F32)
+            ).astype(BF)
+            return carry
+
+        lax.fori_loop(0, depth // 16, add_rows, 0)
+
+    def chain(step, piece, down):
+        landed, send, recv = (down_ref, down_send, down_recv) if down else (up_ref, up_send, up_recv)
+        owner = z - chips + step if down else z + chips - step
+        lines = pl.ds(piece * cut, cut)
+        return pltpu.make_async_remote_copy(
+            src_ref=mine_ref.at[owner, lines],
+            dst_ref=landed.at[step - 1, lines],
+            send_sem=send.at[step - 1, piece],
+            recv_sem=recv.at[step - 1, piece],
+            device_id={ROWS: below if down else above},
+        )
+
+    def take(step, piece, down, owner):
+        landed, recv = (down_ref, down_recv) if down else (up_ref, up_recv)
+        lines = pl.ds(piece * cut, cut)
+        arrival = pltpu.make_async_remote_copy(
+            src_ref=mine_ref.at[z, lines],
+            dst_ref=landed.at[step - 1, lines],
+            send_sem=recv.at[step - 1, piece],
+            recv_sem=recv.at[step - 1, piece],
+            device_id={ROWS: sibling},
+        )
+        arrival.wait_recv()
+        mine_ref[owner, lines] = (
+            mine_ref[owner, lines].astype(F32) + landed[step - 1, lines].astype(F32)
+        ).astype(BF)
+
+    for step in range(1, chips):
+        for piece in range(pieces):
+            for down in (True, False):
+                sends = (z >= chips - step) if down else (z <= step - 1)
+                takes = sends & (has_above if down else has_below)
+                owner = z - chips + step if down else z + chips - step
+
+                if step > 1:
+
+                    @pl.when(takes)
+                    def _():
+                        take(step - 1, piece, down, owner)
+
+                @pl.when(sends)
+                def _():
+                    chain(step, piece, down).start()
+
+    rows = rows_ref[...]
+    centred = rows - jnp.mean(rows, axis=-1, keepdims=True)
+    scale = lax.rsqrt(jnp.mean(centred * centred, axis=-1, keepdims=True) + EPS_NORM)
+    hat = centred * scale
+    own_slots = pl.ds(pl.multiple_of(head * share, share), share)
+    final = final_rest_ref[...] + final_ref[:, own_slots, :].astype(F32)
+    for at, copy in enumerate(finals):
+        copy.wait_recv()
+        final = final + final_landed_ref[at].astype(F32)
+    final_out_ref[...] = final
+    slope = slots_ref[:, own_slots, :].astype(F32)
+    for at, copy in enumerate(slots):
+        copy.wait_recv()
+        slope = slope + landed_ref[at].astype(F32)
+    hat_slope = slope * gain_ref[0]
+    back = hat_slope - jnp.mean(hat_slope, axis=-1, keepdims=True)
+    back = back - hat * jnp.mean(hat_slope * hat, axis=-1, keepdims=True)
+    new_ref[...] = rest_ref[...] + back * scale
+    sums_ref[0:1] = jnp.sum(jnp.sum(slope * hat, axis=0), axis=0, keepdims=True)
+    sums_ref[1:2] = jnp.sum(jnp.sum(slope, axis=0), axis=0, keepdims=True)
+
+    for piece in range(pieces):
+
+        @pl.when(has_above)
+        def _():
+            take(chips - 1, piece, True, z)
+
+        @pl.when(has_below)
+        def _():
+            take(chips - 1, piece, False, z)
+
+    out_ref[...] = mine_ref[z]
+    for step in range(1, chips):
+        for piece in range(pieces):
+
+            @pl.when(z >= chips - step)
+            def _():
+                chain(step, piece, True).wait_send()
+
+            @pl.when(z <= step - 1)
+            def _():
+                chain(step, piece, False).wait_send()
+
+    for copy in slots + finals:
+        copy.wait_send()
+    media_x.wait()
+    media_y.wait()
+
+
+def last_step(partial, to_x, to_y, slots, final, final_rest, rows, rest, gain, heads, chips):
+    depth, columns = partial.shape[0] // (2 * chips), partial.shape[1]
+    videos, share, width = rest.shape
+    pieces = 4
+    any_spec = pl.BlockSpec(memory_space=pl.ANY)
+    block = pltpu.VMEM((chips, depth, columns), BF)
+    steps = pltpu.VMEM((chips - 1, depth, columns), BF)
+    chain_sem = pltpu.SemaphoreType.DMA((chips - 1, pieces))
+    slot_sem = pltpu.SemaphoreType.DMA((heads - 1,))
+    return pl.pallas_call(
+        functools.partial(last_kernel, chips, heads),
+        out_shape=(
+            jax.ShapeDtypeStruct((depth, columns), BF),
+            jax.ShapeDtypeStruct(to_x.shape, BF),
+            jax.ShapeDtypeStruct(to_y.shape, BF),
+            jax.ShapeDtypeStruct(rest.shape, F32),
+            jax.ShapeDtypeStruct((2, width), F32),
+            jax.ShapeDtypeStruct(rest.shape, F32),
+        ),
+        in_specs=[any_spec] * 3 + [vmem_spec()] * 6,
+        out_specs=(vmem_spec(), any_spec, any_spec, vmem_spec(), vmem_spec(), vmem_spec()),
+        scratch_shapes=[
+            block,
+            block,
+            steps,
+            steps,
+            pltpu.VMEM((heads - 1, videos, share, width), BF),
+            pltpu.VMEM((heads - 1, videos, share, width), BF),
+            pltpu.SemaphoreType.DMA((7,)),
+            slot_sem,
+            slot_sem,
+            slot_sem,
+            slot_sem,
+            chain_sem,
+            chain_sem,
+            chain_sem,
+            chain_sem,
+        ],
+        compiler_params=pltpu.CompilerParams(
+            collective_id=7, has_side_effects=True, vmem_limit_bytes=60 * MIB
+        ),
+        cost_estimate=pl.CostEstimate(flops=0, bytes_accessed=160 * 1000 * 1000, transcendentals=0),
+        name="last_step",
+    )(partial.reshape(chips, 2, depth, columns), to_x, to_y, slots, final, final_rest, rows, rest, gain)
+
+
+def media_back_kernel(*refs):
+    first, second, out_ref = refs[:4], refs[4:8], refs[-1]
+
+    def write(own_ref, *terms):
+        rows = own_ref[...].astype(F32)
+        centred = rows - jnp.mean(rows, axis=-1, keepdims=True)
+        spread = lax.rsqrt(jnp.mean(centred * centred, axis=-1, keepdims=True) + EPS_NORM)
+        hat = centred * spread
+        total = functools.reduce(jnp.add, [term[...].astype(F32) for term in terms])
+        total = total - jnp.mean(total, axis=-1, keepdims=True) - hat * jnp.mean(total * hat, axis=-1, keepdims=True)
+        total = total * spread
+        for video in range(rows.shape[0]):
+            out_ref[:, video, :] = total[video]
+
+    @pl.when(pl.program_id(0) == 0)
+    def _():
+        write(*first)
+
+    @pl.when(pl.program_id(0) == 1)
+    def _():
+        write(*second)
+
+
+def media_back(first, second):
+    videos, rows, width = first[0].shape
+    cut = 32
+    steps = rows // cut
+    specs = [pl.BlockSpec((videos, cut, width), lambda i, j: (0, jnp.where(i == 0, j, steps - 1), 0))] * 4
+    specs += [pl.BlockSpec((videos, cut, width), lambda i, j: (0, jnp.where(i == 1, j, 0), 0))] * 4
+    return pl.pallas_call(
+        media_back_kernel,
+        grid=(2, steps),
+        out_shape=jax.ShapeDtypeStruct((2 * rows, videos, width), F32),
+        in_specs=specs,
+        out_specs=pl.BlockSpec((cut, videos, width), lambda i, j: (steps * i + j, 0, 0)),
+        compiler_params=pltpu.CompilerParams(vmem_limit_bytes=60 * MIB),
+        cost_estimate=pl.CostEstimate(flops=0, bytes_accessed=30 * 1000 * 1000, transcendentals=0),
+        name="media_back",
+    )(*first, *second)
+
+
+def adam_kernel(rates, begins, factor_ref, *refs):
+    kinds, step = len(rates), pl.program_id(0)
+    layers = (len(refs) // kinds) - 7
+    factor = factor_ref[0, 0]
+    ins = [refs[at * (3 + layers) : (at + 1) * (3 + layers)] for at in range(kinds)]
+    outs = [refs[kinds * (3 + layers) + 4 * at :][:4] for at in range(kinds)]
+    for kind in range(kinds):
+        steps = (begins[kind + 1] - begins[kind]) // layers
+        weight_ref, first_ref, second_ref = ins[kind][:3]
+        mean_ref, square_ref, next_ref, copy_ref = outs[kind]
+        columns = weight_ref.shape[3]
+        for layer in range(layers):
+            begin = begins[kind] + layer * steps
+
+            @pl.when((step >= begin) & (step < begin + steps))
+            def _():
+                for part in range(weight_ref.shape[1]):
+                    grad = ins[kind][3 + layer][:, part * columns : (part + 1) * columns]
+                    mean, square, weight = adam_step(
+                        weight_ref[0, part],
+                        first_ref[0, part],
+                        second_ref[0, part],
+                        grad.astype(F32) * factor,
+                        rates[kind],
+                        WEIGHT_DECAY,
+                    )
+                    mean_ref[0, part] = mean
+                    square_ref[0, part] = square
+                    next_ref[0, part] = weight
+                    copy_ref[0, part] = weight.astype(BF)
+
+
+def adam_fast(kinds, factor):
+    layers = kinds[0][0].shape[0]
+    begins = [0]
+    for weight, _, _, _, cut, _ in kinds:
+        begins.append(begins[-1] + layers * (weight.shape[2] // cut))
+    operands, in_specs, out_specs, out_shape = [], [], [], []
+    for kind, (weight, first, second, grads, cut, _) in enumerate(kinds):
+        _, parts, rows, columns = weight.shape
+        steps = rows // cut
+        begin, end = begins[kind], begins[kind + 1]
+
+        def place(i, begin=begin, end=end, steps=steps):
+            at = jnp.clip(i, begin, end - 1) - begin
+            return (at // steps, 0, at % steps, 0)
+
+        spec = pl.BlockSpec((1, parts, cut, columns), place)
+        operands += [weight, first, second]
+        in_specs += [spec] * 3
+        for layer, (grad, base) in enumerate(grads):
+
+            def grad_place(i, begin=begin + layer * steps, steps=steps, base=base):
+                return (jnp.clip(i, begin, begin + steps - 1) - begin, base)
+
+            operands.append(grad)
+            in_specs.append(pl.BlockSpec((cut, parts * columns), grad_place))
+        wide = jax.ShapeDtypeStruct(weight.shape, F32)
+        out_specs += [spec] * 4
+        out_shape += [wide, wide, wide, jax.ShapeDtypeStruct(weight.shape, BF)]
+    size = sum(kind[0].size for kind in kinds)
+    made = pl.pallas_call(
+        functools.partial(adam_kernel, [kind[-1] for kind in kinds], begins),
+        grid=(begins[-1],),
+        out_shape=tuple(out_shape),
+        in_specs=[pl.BlockSpec(memory_space=pltpu.SMEM)] + in_specs,
+        out_specs=tuple(out_specs),
+        compiler_params=pltpu.CompilerParams(vmem_limit_bytes=60 * MIB),
+        cost_estimate=pl.CostEstimate(flops=20 * size, bytes_accessed=28 * size, transcendentals=size),
+        name="adam",
+    )(factor, *operands)
+    return [made[4 * at : 4 * at + 4] for at in range(len(kinds))]
 
 
 def flat(rows):
@@ -898,21 +1415,21 @@
     gain_first,
     gain_second,
 ):
-    heads_count, rows_count = lax.axis_size("heads"), lax.axis_size("rows")
-    me = lax.axis_index("heads")
+    heads_count, rows_count = lax.axis_size(HEADS), lax.axis_size(ROWS)
+    me = lax.axis_index(HEADS)
     layers, _, row_share, head_columns = inward.shape
     local_positions, videos, width = media.shape
     latent_count = latents.shape[1] * heads_count
     scale = HD ** (-0.5)
 
     def swap_x(rows):
-        return lax.ppermute(rows, "heads", X_SWAP)
+        return lax.ppermute(rows, HEADS, X_SWAP)
 
     def swap_y(rows):
-        return lax.ppermute(rows, "heads", Y_SWAP)
+        return lax.ppermute(rows, HEADS, Y_SWAP)
 
     def gather_rows(rows):
-        return lax.all_gather(rows, "rows", axis=0, tiled=True)
+        return lax.all_gather(rows, ROWS, axis=0, tiled=True)
 
     outward_t, narrow_t = (jnp.swapaxes(outward, 1, 2), jnp.swapaxes(narrow, 1, 2))
     columns, units = head_columns, widen.shape[2]
@@ -929,36 +1446,22 @@
     query_full = [first_set[:, begin + l * columns : begin + (l + 1) * columns] for l in range(layers)]
     begin = begin + layers * columns
     out_full = [first_set[:, begin + l * columns : begin + (l + 1) * columns] for l in range(layers)]
-    widen_full, narrow_full = [], []
-    for layer in range(layers):
-        later = gather_rows(jnp.concatenate((widen[layer].astype(BF), narrow_t[layer].astype(BF)), axis=1))
-        widen_full.append(later[:, :units])
-        narrow_full.append(later[:, units:])
     share = latents.shape[1]
-    moved = [(normed, slope_rows)]
-    for swap in (X_SWAP, Y_SWAP, FAR_SWAP):
-        moved.append(tuple(lax.ppermute(rows, "heads", swap) for rows in (normed, slope_rows)))
-    gathered = []
-    for at in range(2):
-        full = jnp.zeros((videos, latent_count, width), BF)
-        for group in range(heads_count):
-            full = lax.dynamic_update_slice(full, moved[group][at], (0, (me ^ group) * share, 0))
-        gathered.append(full)
-    latent_norm, feed_slope = gathered
-
-    own = jnp.swapaxes(media, 0, 1).reshape(videos, 2, local_positions // 2, width)
-    own = (own[:, 0], own[:, 1])
-    from_x = (swap_x(own[0]), swap_x(own[1]))
-    from_y = (swap_y(own[0]), swap_y(own[1]))
-    from_far = (swap_x(from_y[0]), swap_y(from_x[1]))
+    own = jnp.swapaxes(media.reshape(2, local_positions // 2, videos, width), 1, 2)
+    later_sets = [
+        jnp.concatenate((widen[layer].astype(BF), narrow_t[layer].astype(BF)), axis=1) for layer in range(layers)
+    ]
+    own, *later_sets = lax.optimization_barrier((own, *later_sets))
+    later_sets = [gather_rows(rows) for rows in later_sets]
+    widen_full = [rows[:, :units] for rows in later_sets]
+    narrow_full = [rows[:, units:] for rows in later_sets]
+
     frames = jnp.stack([2 * (me ^ group) + half for group in range(4) for half in range(2)])
     live = (frames[None, :] < frame_count[:, None]).astype(jnp.int32)
-    made = ()
     media_gains = norm_gains[:, 0:2]
-    for group, parts in enumerate((own, from_x, from_y, from_far)):
-        made = media_part(parts[0], parts[1], media_gains, pair_weights, group, made)
-    keys, media_hat = made
-
+    near, latent_norm = gather_near(own, normed, heads_count)
+    keys, media_hat, far = media_near(own, near, media_gains, first_set, 2 * layers * columns, heads_count)
+    keys, media_hat, feed_slope = media_far(far, media_gains, first_set, slope_rows, keys, media_hat, heads_count)
     kept = []
     for layer in range(layers):
         query_weight, out_weight = query_full[layer], out_full[layer]
@@ -975,10 +1478,7 @@
         gain = norm_gains[0 if last else layer + 1, 2:4]
         kept.append((latent, middle, latent_norm, query, latent_pair, mixed, feed_norm, hidden_pre, hidden))
         if last:
-            latent = middle
-            for group, swap in enumerate((None, X_SWAP, Y_SWAP, FAR_SWAP)):
-                term = lax.dynamic_slice_in_dim(part, (me ^ group) * share, share, axis=1)
-                latent = latent + (lax.ppermute(term, "heads", swap) if swap else term).astype(F32)
+            final_part, final_rest = part, middle
         else:
             latent, latent_norm = forward_exchange(part, middle, gain, heads_count)
 
@@ -1006,7 +1506,7 @@
     def scatter_rows(gradient):
         if summed:
             gradient, _ = lax.optimization_barrier((gradient, summed[-1]))
-        summed.append(lax.psum_scatter(gradient, "rows", scatter_dimension=0, tiled=True))
+        summed.append(lax.psum_scatter(gradient, ROWS, scatter_dimension=0, tiled=True))
         return summed[-1]
 
     for layer in reversed(range(layers)):
@@ -1033,11 +1533,12 @@
         part = (mm(query_slope, query_weight, NT, F32) + mm(latent_slopes, pair_weight, NT, F32)).astype(BF)
         part = part.reshape(videos, latent_count, width)
         last = layer == 0
-        slope, latent_sums, feed_slope = backward_exchange(
-            part, latent_in, middle_slope, norm_gains[layer, 2:4], heads_count, last
-        )
-        if last:
-            media_slopes, slope = lax.optimization_barrier((media_slopes, slope))
+        if not last:
+            slope, latent_sums, feed_slope = backward_exchange(
+                part, latent_in, middle_slope, norm_gains[layer, 2:4], heads_count
+            )
+        else:
+            last_part = part
             far = [hat_slope(media_slopes, 3, half) for half in range(2)]
             media_slopes, *far = lax.optimization_barrier((media_slopes, *far))
             over_x, over_y = swap_x(far[0]), swap_y(far[1])
@@ -1060,41 +1561,37 @@
         media_sums = jnp.stack(
             (jnp.sum(wide * hat_grad, axis=1), jnp.sum(wide * slope_sum[None, :], axis=1))
         )
-        inward_grad = jnp.concatenate((out_grad, query_grad, pair_grad), axis=1)
+        inward_grad = jnp.concatenate((query_grad, pair_grad, out_grad), axis=1)
         if last:
-            inward_grad, over_x, over_y, in_x[0], in_y[1] = lax.optimization_barrier(
-                (inward_grad, over_x, over_y, in_x[0], in_y[1])
-            )
-            shares.append(scatter_rows(inward_grad))
+            near = [near[0] + over_y, near[1] + over_x]
+            last_grad, *near = lax.optimization_barrier((inward_grad, *near))
         else:
-            inward_grad, latent = lax.optimization_barrier((inward_grad, latent))
             waiting = [inward_grad]
-        gain_parts[layer] = jnp.concatenate((media_sums, latent_sums, feed_sums), axis=0)
-
-    back = [hat_slope(media_slopes, 0, half).astype(F32) for half in range(2)]
-    in_x[1] = swap_x(near[0] + over_y)
-    in_y[0] = swap_y(near[1] + over_x)
+        gain_parts[layer] = [media_sums, None if last else latent_sums, feed_sums]
+
+    back = [hat_slope(media_slopes, 0, half) for half in range(2)]
+    last_grad, *back = lax.optimization_barrier((last_grad, *back))
+    share_out, in_x[1], in_y[0], slope, gain_parts[0][1], latent = last_step(
+        last_grad, *near, last_part, final_part, final_rest, latents, middle_slope, norm_gains[0, 2:4], heads_count, rows_count // 2
+    )
+    media_slope = media_back(*[(own[half], back[half], in_x[half], in_y[half]) for half in range(2)])
 
     def square_sum(rows):
         wide = rows.astype(F32)
         return jnp.sum(wide * wide)
 
+    shares.append(share_out)
     early = sum(square_sum(piece) for piece in shares[:-1])
-    in_x[1], in_y[0], early = lax.optimization_barrier((in_x[1], in_y[0], early))
-    rows = jnp.stack(own, axis=1).astype(F32)
-    total = jnp.stack(back, axis=1) + jnp.stack(in_x, axis=1).astype(F32) + jnp.stack(in_y, axis=1).astype(F32)
-    centred = rows - jnp.mean(rows, axis=-1, keepdims=True)
-    spread = lax.rsqrt(jnp.mean(centred * centred, axis=-1, keepdims=True) + EPS_NORM)
-    hat = centred * spread
-    total = total - jnp.mean(total, axis=-1, keepdims=True) - hat * jnp.mean(total * hat, axis=-1, keepdims=True)
-    media_slope = (total * spread).reshape(videos, local_positions, width)
-    media_slope = jnp.swapaxes(media_slope, 0, 1)
-
-    media_slope, shares[-1] = lax.optimization_barrier((media_slope, shares[-1]))
-    gain_term = jnp.concatenate(gain_parts, axis=0).reshape(heads_count, -1, 128)
+    gain_term = jnp.concatenate([rows for parts in gain_parts for rows in parts], axis=0).reshape(heads_count, -1, 128)
     lines = gain_term.shape[1]
     squares = jnp.full((heads_count, 8 - lines % 8, 128), early + square_sum(shares[-1]), F32)
-    totals = sum_fast(jnp.concatenate((gain_term, squares), axis=1), heads_count, rows_count, 6)
+    totals = sum_fast(jnp.concatenate((gain_term, squares), axis=1), heads_count, rows_count, 9)
+    gain_total = totals[:, :lines].reshape(layers, 6, width)
+    square_total = totals[0, lines, 0]
+    gain_total = totals[:, :lines].reshape(layers, 6, width)
+    square_total = totals[0, lines, 0]
+    gain_total = totals[:, :lines].reshape(layers, 6, width)
+    square_total = totals[0, lines, 0]
     gain_total = totals[:, :lines].reshape(layers, 6, width)
     square_total = totals[0, lines, 0]
     feed_parts = [piece[:, : 2 * units] for piece in shares[-2::-1]]
@@ -1102,24 +1599,43 @@
     gradient_norm = jnp.sqrt(square_total + jnp.sum(gain_total * gain_total))
     factor = CLIP_LEVEL / jnp.maximum(gradient_norm, CLIP_LEVEL)
 
-    def wide_part(parts, begin, end):
-        return jnp.stack([piece[:, begin:end] for piece in parts]).astype(F32)
-
-    inward_grad = jnp.stack(
-        [wide_part(inward_parts, (1 + t) * columns, (2 + t) * columns) for t in range(3)], axis=1
-    )
-    table = (
-        (inward, inward_first, inward_second, inward_grad, RATE_INWARD),
-        (outward, outward_first, outward_second, jnp.swapaxes(wide_part(inward_parts, 0, columns), 1, 2), RATE_OUTWARD),
-        (widen, widen_first, widen_second, wide_part(feed_parts, units, None), RATE_WIDEN),
-        (narrow, narrow_first, narrow_second, jnp.swapaxes(wide_part(feed_parts, 0, units), 1, 2), RATE_NARROW),
-    )
-    results = [latent, slope, media_slope, gradient_norm]
-    for weight, first, second, gradient, rate in table:
-        mean_new, square_new, weight_new = adam_step(
-            weight, first, second, gradient * factor, rate, WEIGHT_DECAY
-        )
-        results = results + [mean_new, square_new, weight_new, weight_new.astype(BF)]
+    factor_cell = factor.reshape(1, 1)
+    early_share, middle_share, late_share = shares
+    depth = widen.shape[1]
+
+    def turned(*arrays):
+        return [jnp.swapaxes(rows, 1, 2)[:, None] for rows in arrays]
+
+    def turn_back(arrays):
+        return [jnp.swapaxes(rows[:, 0], 1, 2) for rows in arrays]
+
+    inward_made, outward_made, widen_made, narrow_made = adam_fast(
+        (
+            (
+                *(inward, inward_first, inward_second),
+                [(late_share, 0), (middle_share, 0)],
+                *(depth // 2, RATE_INWARD),
+            ),
+            (
+                *turned(outward, outward_first, outward_second),
+                [(late_share, 3), (middle_share, 3)],
+                *(depth, RATE_OUTWARD),
+            ),
+            (
+                *[rows[:, None] for rows in (widen, widen_first, widen_second)],
+                [(middle_share, 1 + 4 * columns // units), (early_share, 1)],
+                *(depth // 2, RATE_WIDEN),
+            ),
+            (
+                *turned(narrow, narrow_first, narrow_second),
+                [(middle_share, 4 * columns // units), (early_share, 0)],
+                *(depth // 2, RATE_NARROW),
+            ),
+        ),
+        factor_cell,
+    )
+    results = [latent, slope, media_slope, gradient_norm, *inward_made, *turn_back(outward_made)]
+    results += [rows[:, 0] for rows in widen_made] + turn_back(narrow_made)
     mean_new, square_new, weight_new = adam_step(
         norm_gains, gain_first, gain_second, gain_total * factor, RATE_GAINS, 0.0
     )
@@ -1129,52 +1645,52 @@
 
 def solution(mesh):
     placed = (
-        P("heads", "rows", None),
-        P("rows", "heads", None),
-        P("rows"),
-        P("rows", "heads", None),
-        P(None, None, "rows", "heads"),
-        P(None, None, "rows", "heads"),
-        P(None, None, "rows", "heads"),
-        P(None, "heads", "rows"),
-        P(None, "heads", "rows"),
-        P(None, "heads", "rows"),
-        P(None, "rows", "heads"),
-        P(None, "rows", "heads"),
-        P(None, "rows", "heads"),
-        P(None, "heads", "rows"),
-        P(None, "heads", "rows"),
-        P(None, "heads", "rows"),
+        P(HEADS, ROWS, None),
+        P(ROWS, HEADS, None),
+        P(ROWS),
+        P(ROWS, HEADS, None),
+        P(None, None, ROWS, HEADS),
+        P(None, None, ROWS, HEADS),
+        P(None, None, ROWS, HEADS),
+        P(None, HEADS, ROWS),
+        P(None, HEADS, ROWS),
+        P(None, HEADS, ROWS),
+        P(None, ROWS, HEADS),
+        P(None, ROWS, HEADS),
+        P(None, ROWS, HEADS),
+        P(None, HEADS, ROWS),
+        P(None, HEADS, ROWS),
+        P(None, HEADS, ROWS),
         P(),
         P(),
         P(),
     )
-    local = local_fast if (mesh.shape["rows"], mesh.shape["heads"]) == (8, 4) else local_plain
+    local = local_fast if (mesh.shape[ROWS], mesh.shape[HEADS]) == (8, 4) else local_plain
     return jax.shard_map(
         local,
         mesh=mesh,
         in_specs=placed,
         out_specs=(
-            P("rows", "heads", None),
-            P("rows", "heads", None),
-            P("heads", "rows", None),
+            P(ROWS, HEADS, None),
+            P(ROWS, HEADS, None),
+            P(HEADS, ROWS, None),
             P(),
-            P(None, None, "rows", "heads"),
-            P(None, None, "rows", "heads"),
-            P(None, None, "rows", "heads"),
-            P(None, None, "rows", "heads"),
-            P(None, "heads", "rows"),
-            P(None, "heads", "rows"),
-            P(None, "heads", "rows"),
-            P(None, "heads", "rows"),
-            P(None, "rows", "heads"),
-            P(None, "rows", "heads"),
-            P(None, "rows", "heads"),
-            P(None, "rows", "heads"),
-            P(None, "heads", "rows"),
-            P(None, "heads", "rows"),
-            P(None, "heads", "rows"),
-            P(None, "heads", "rows"),
+            P(None, None, ROWS, HEADS),
+            P(None, None, ROWS, HEADS),
+            P(None, None, ROWS, HEADS),
+            P(None, None, ROWS, HEADS),
+            P(None, HEADS, ROWS),
+            P(None, HEADS, ROWS),
+            P(None, HEADS, ROWS),
+            P(None, HEADS, ROWS),
+            P(None, ROWS, HEADS),
+            P(None, ROWS, HEADS),
+            P(None, ROWS, HEADS),
+            P(None, ROWS, HEADS),
+            P(None, HEADS, ROWS),
+            P(None, HEADS, ROWS),
+            P(None, HEADS, ROWS),
+            P(None, HEADS, ROWS),
             P(),
             P(),
             P(),

time: 719 us -> 680 us (0.946)
  Pallas kernels: 267 us -> 429 us
  waiting for transfers between devices: 148 us -> 22.3 us
  other arithmetic: 65.1 us -> 31.9 us
  starting transfers between devices: 32.2 us -> 4.25 us
  matrix products: 137 us -> 126 us
    pallas_call x4 -> x6, Pallas kernels: 49 us -> 231 us  [the longest x1 82.8 us: gather_near(): pl.pallas_call(functools.partial(gather_kernel, count), out_shape=(jax.Sh...]
    ppermute x21 -> x4, waiting for transfers between devices: 145 us -> 0.01 us  [the longest x2 0.01 us: swap_x(): return lax.ppermute(rows, HEADS, X_SWAP)]
    ppermute x21 -> x4, starting transfers between devices: 31.9 us -> 4.05 us  [the longest x2 2.08 us: swap_x(): return lax.ppermute(rows, HEADS, X_SWAP)]
    pallas_call x4 -> x3, Pallas kernels: 90.3 us -> 67.2 us  [backward_exchange(): pl.pallas_call(functools.partial(backward_kernel, count, last), out_shape...]
    all_gather x3, waiting for transfers between devices: 2.76 us -> 21.5 us  [gather_rows(): return lax.all_gather(rows, ROWS, axis=0, tiled=True)]
    convert_element_type x4 -> x2, other arithmetic: 14.4 us -> 1.53 us  [the longest x1 0.83 us: local_fast(): normed = layer_norm(latent, norm_gains[0, 2], norm_gains[0, 3]).astype(BF)]
    dot_general x36, matrix products: 137 us -> 126 us  [mm(): lax.dot_general(left, right, dims, preferred_element_type=F32).astype(out)]
    reduce_sum x4 -> x0, other arithmetic: 8.38 us -> none  [the longest x1 4.48 us: local_fast(): jnp.mean(total, axis=-1, keepdims=True)]
  transfers between devices with their start and end apart: 27 -> 9, of which waited for: 13 -> 1; matrix products, arithmetic and copies ran while one was open for 27% -> 23% of each run, Pallas kernels for 34% -> 57%
where the time goes in v3:
time: 680 us; the launch traced here: 674 us
  Pallas kernels  429 us (63%)
  matrix products  126 us (19%)
  local copies, waits for them, and re-layouts  40.9 us (6%)
  other arithmetic  31.9 us (5%)
  waiting for transfers between devices  22.3 us (3%)
  between operations  19.5 us (3%)
    dot_general x36, matrix products, mm(): lax.dot_general(left, right, dims, preferred_element_type=F32).astype(out)  126 us
    pallas_call x1, Pallas kernels, gather_near(): pl.pallas_call(functools.partial(gather_kernel, count), out_shape=(jax.Sh...  82.8 us
    pallas_call x3, Pallas kernels, backward_exchange(): pl.pallas_call(functools.partial(backward_kernel, count, last), out_shape...  67.2 us
    pallas_call x3, Pallas kernels, forward_exchange(): pl.pallas_call(functools.partial(forward_kernel, count, last), out_shape=...  61.7 us
    pallas_call x1, Pallas kernels, last_step(): pl.pallas_call(functools.partial(last_kernel, chips, heads), out_shape=(j...  57.1 us
    pallas_call x1, Pallas kernels, media_near(): pl.pallas_call(functools.partial(near_kernel, count), grid=(6, 2), out_sh...  41.5 us
    unnamed x155, local copies, waits for them, and re-layouts  25.5 us
    pallas_call x2, Pallas kernels, attend_back_fast(): pl.pallas_call(functools.partial(attend_back_kernel, scale=scale), grid=(...  23.7 us
  transfers between devices with their start and end apart: 9, of which 1 were waited for; matrix products, arithmetic and copies ran while one was open for 23% of the time, Pallas kernels for 57%

profile of v3, /device:TPU:0, one launch (start us, length us, event | category | flops | bytes accessed | tf_op | source)
XLA Modules:
  0.0 674.5 jit_solution(4415448022045465551)
XLA Ops:
  23.9 82.8 %gather_near.1 = (bf16[4,4,128,1536]{3,2,1,0:T(8,128)(2,1)}, bf16[4,64,1536]{2,1,0:T(8,128)(2,1)}) custom-call(bf16[2,4,128,1536]{3,2,1,0:T(8,128)(2,1)} %bitcast.240, bf16[4,16,1536]{2,1,0:T(8,128)(2,1)} %add_convert_fusion.norm_ref), custom_call_target="tpu_custom_call" | custom-call | bytes 250000000 | tf_op jit(solution)/shard_map/gather_near/pallas_call | solution.py:438
  112.1 41.5 %media_near.1 = (bf16[8,4,128,1536]{3,2,1,0:T(8,128)(2,1)}, bf16[8,4,128,1536]{3,2,1,0:T(8,128)(2,1)}, bf16[2,4,128,1536]{3,2,1,0:T(8,128)(2,1)}) custom-call(bf16[2,4,128,1536]{3,2,1,0:T(8,128)(2,1)} %bitcast.241, bf16[4,4,128,1536]{3,2,1,0:T(8,128)(2,1)} %get-tuple-element.100.near_ref.source_ref, f32[2,2,1536]{2,1,0:T(2,128)} %slice.230.gain_ref, ...), custom_call_target="tpu_custom_call" | custom-call | flops 14495514624 | bytes 18874368 | tf_op jit(solution)/shard_map/media_near/pallas_call | solution.py:523
  153.6 15.0 %media_far.1 = (bf16[8,4,128,1536]{3,2,1,0:T(8,128)(2,1)}, bf16[8,4,128,1536]{3,2,1,0:T(8,128)(2,1)}, bf16[4,64,1536]{2,1,0:T(8,128)(2,1)}) custom-call(bf16[2,4,128,1536]{3,2,1,0:T(8,128)(2,1)} %get-tuple-element.101.chunk_ref, f32[2,2,1536]{2,1,0:T(2,128)} %slice.230.gain_ref, ...), custom_call_target="tpu_custom_call", output_to_operand_aliasing={{0}: (4, {}), {1}: (5, {})} | custom-call | flops 4831838208 | bytes 6291456 | tf_op jit(solution)/shard_map/media_far/pallas_call | solution.py:598
  168.6 4.7 copy-done
  173.4 6.0 attend.2
  181.4 20.6 %forward_exchange.3 = (f32[4,16,1536]{2,1,0:T(8,128)S(1)}, bf16[4,64,1536]{2,1,0:T(8,128)(2,1)S(1)}) custom-call(bf16[4,64,1536]{2,1,0:T(8,128)(2,1)S(1)} %bitcast.235, f32[4,16,1536]{2,1,0:T(8,128)S(1)} %copy-done.1, f32[2,1536]{1,0:T(2,128)S(1)} %get-tuple-element.252.gain_ref), custom_call_target="tpu_custom_call" | custom-call | bytes 75000000 | tf_op jit(solution)/shard_map/forward_exchange/pallas_call | solution.py:900
  202.0 5.7 multiply_convert_fusion.1
  207.8 4.3 fusion.37
  212.1 20.7 %forward_exchange.4 = (f32[4,16,1536]{2,1,0:T(8,128)S(1)}, bf16[4,64,1536]{2,1,0:T(8,128)(2,1)S(1)}) custom-call(bf16[4,64,1536]{2,1,0:T(8,128)(2,1)S(1)} %bitcast.233, f32[4,16,1536]{2,1,0:T(8,128)S(1)} %get-tuple-element.107.rest_ref.rows_ref, f32[2,1536]{1,0:T(2,128)S(1)} %copy-done.17), custom_call_target="tpu_custom_call" | custom-call | bytes 75000000 | tf_op jit(solution)/shard_map/forward_exchange/pallas_call | solution.py:900
  237.3 6.5 attend.3
  245.7 20.4 %forward_exchange.5 = (f32[4,16,1536]{2,1,0:T(8,128)S(1)}, bf16[4,64,1536]{2,1,0:T(8,128)(2,1)S(1)}) custom-call(bf16[4,64,1536]{2,1,0:T(8,128)(2,1)S(1)} %bitcast.234, f32[4,16,1536]{2,1,0:T(8,128)S(1)} %get-tuple-element.111.rest_ref.rows_ref, f32[2,1536]{1,0:T(2,128)S(1)} %copy-done.19), custom_call_target="tpu_custom_call" | custom-call | bytes 75000000 | tf_op jit(solution)/shard_map/forward_exchange/pallas_call | solution.py:900
  266.2 21.5 %all-gather.8.cloned.1.call-done = bf16[1536,3072]{1,0:T(8,128)(2,1)} async-done(((bf16[192,3072]{1,0:T(8,128)(2,1)}), bf16[1536,3072]{1,0:T(8,128)(2,1)}) %all-gather.8.cloned.1.call-update) | async-done | bytes 9437200 | tf_op jit(solution)/shard_map/all_gather | solution.py:1432
  287.7 5.0 multiply_convert_fusion
  296.5 8.1 %feed_gradients.2 = bf16[1536,3072]{1,0:T(8,128)(2,1)} custom-call(bf16[256,1536]{1,0:T(8,128)(2,1)} %bitcast.269, bf16[256,1536]{1,0:T(8,128)(2,1)} %get-tuple-element.257.second_ref, bf16[256,1536]{1,0:T(8,128)(2,1)} %bitcast.226, bf16[256,1536]{1,0:T(8,128)(2,1)} %fusion.59.fourth_ref), custom_call_target="tpu_custom_call" | custom-call | flops 2415919104 | bytes 18874368 | tf_op jit(solution)/shard_map/feed_gradients/pallas_call | solution.py:834
  304.5 4.6 fusion.43
  311.0 23.6 %backward_exchange.3 = (f32[4,16,1536]{2,1,0:T(8,128)S(1)}, f32[2,1536]{1,0:T(2,128)S(1)}, bf16[4,64,1536]{2,1,0:T(8,128)(2,1)S(1)}) custom-call(bf16[4,64,1536]{2,1,0:T(8,128)(2,1)S(1)} %bitcast.232, f32[4,16,1536]{2,1,0:T(8,128)S(1)} %get-tuple-element.114.rows_ref.final_rest_ref, f32[4,16,1536]{2,1,0:T(8,128)S(1)} %copy-done.5, f32[2,1536]{1,0:T(2,128)S(1)} %copy-done.20), custom_call_target="tpu_custom_call" | custom-call | bytes 75000000 | tf_op jit(solution)/shard_map/backward_exchange/pallas_call | solution.py:960
  337.9 11.8 %attend_back.2 = (bf16[256,384]{1,0:T(8,128)(2,1)}, bf16[256,768]{1,0:T(8,128)(2,1)}, bf16[8,4,128,1536]{3,2,1,0:T(8,128)(2,1)}) custom-call(s32[4,8]{1,0:T(4,128)} %copy-done.21, bf16[256,384]{1,0:T(8,128)(2,1)} %copy-done.7, bf16[256,768]{1,0:T(8,128)(2,1)} %copy-done.3, bf16[256,768]{1,0:T(8,128)(2,1)} %copy-done.3, ...), custom_call_target="tpu_custom_call" | custom-call | flops 4026531840 | bytes 12582912 | tf_op jit(solution)/shard_map/attend_back/pallas_call | solution.py:782
  354.5 21.9 %backward_exchange.4 = (f32[4,16,1536]{2,1,0:T(8,128)S(1)}, f32[2,1536]{1,0:T(2,128)S(1)}, bf16[4,64,1536]{2,1,0:T(8,128)(2,1)S(1)}) custom-call(bf16[4,64,1536]{2,1,0:T(8,128)(2,1)S(1)} %bitcast.220, f32[4,16,1536]{2,1,0:T(8,128)S(1)} %get-tuple-element.111.rest_ref.rows_ref, f32[4,16,1536]{2,1,0:T(8,128)S(1)} %copy-done.16, f32[2,1536]{1,0:T(2,128)S(1)} %copy-done.18), custom_call_target="tpu_custom_call" | custom-call | bytes 75000000 | tf_op jit(solution)/shard_map/backward_exchange/pallas_call | solution.py:960
  377.6 4.3 convert_reduce_fusion.1
  382.0 12.7 %fusion.2 = f32[1536,768,1,1]{1,0,3,2:T(8,128)S(1)} fusion(bf16[8,4,128,1536]{3,2,1,0:T(8,128)(2,1)} %get-tuple-element.120, bf16[8,4,128,1536]{3,2,1,0:T(8,128)(2,1)S(1)} %copy-done.22), kind=kOutput, calls=%fused_computation.10 | convolution fusion | flops 9663676416 | bytes 23592960 | tf_op jit(solution)/shard_map/dot_general | solution.py:378
  405.6 12.0 %feed_gradients.3 = bf16[1536,4608]{1,0:T(8,128)(2,1)} custom-call(bf16[256,1536]{1,0:T(8,128)(2,1)} %bitcast.224, bf16[256,1536]{1,0:T(8,128)(2,1)} %copy-done.42, bf16[256,1536]{1,0:T(8,128)(2,1)} %bitcast.222, bf16[256,1536]{1,0:T(8,128)(2,1)} %fusion.52.fourth_ref, bf16[1536,1536]{1,0:T(8,128)(2,1)} %pad_maximum_fusion.rest_0_), custom_call_target="tpu_custom_call" | custom-call | flops 2415919104 | bytes 18874368 | tf_op jit(solution)/shard_map/feed_gradients/pallas_call | solution.py:834
  425.2 21.8 %backward_exchange.5 = (f32[4,16,1536]{2,1,0:T(8,128)S(1)}, f32[2,1536]{1,0:T(2,128)S(1)}, bf16[4,64,1536]{2,1,0:T(8,128)(2,1)S(1)}) custom-call(bf16[4,64,1536]{2,1,0:T(8,128)(2,1)S(1)} %bitcast.231, f32[4,16,1536]{2,1,0:T(8,128)S(1)} %get-tuple-element.107.rest_ref.rows_ref, f32[4,16,1536]{2,1,0:T(8,128)S(1)} %get-tuple-element.123.rest_ref, ...), custom_call_target="tpu_custom_call" | custom-call | bytes 75000000 | tf_op jit(solution)/shard_map/backward_exchange/pallas_call | solution.py:960
  450.3 11.9 %attend_back.3 = (bf16[256,384]{1,0:T(8,128)(2,1)}, bf16[256,768]{1,0:T(8,128)(2,1)}, bf16[8,4,128,1536]{3,2,1,0:T(8,128)(2,1)}) custom-call(s32[4,8]{1,0:T(4,128)} %copy-done.21, bf16[256,384]{1,0:T(8,128)(2,1)} %copy-done.6, bf16[256,768]{1,0:T(8,128)(2,1)} %copy-done.2, bf16[256,768]{1,0:T(8,128)(2,1)} %copy-done.2, ...), custom_call_target="tpu_custom_call", output_to_operand_aliasing={{2}: (7, {})} | custom-call | flops 4026531840 | bytes 12582912 | tf_op jit(solution)/shard_map/attend_back/pallas_call | solution.py:782
  477.9 3.8 convolution_convert_fusion.4
  490.7 4.0 convolution_convert_fusion.3
  496.1 18.3 %fusion.9 = (f32[1536]{0:T(1024)S(1)}, f32[1536]{0:T(1024)S(1)}, f32[1536]{0:T(1024)S(1)}, f32[1536]{0:T(1024)S(1)}, f32[1536,768,1,1]{1,0,3,2:T(8,128)}) fusion(f32[768]{0:T(1024)S(1)} %convert_reduce_fusion.1, bf16[1536,3072]{1,0:T(8,128)(2,1)S(1)} %bitcast.239, f32[768]{0:T(1024)S(1)} %convert_reduce_fusion, f32[1536,768,1,1]{1,0,3,2:T(8,128)} %copy-done.27, ...), kind=kOutput, calls=%fused_computation.17 | convolution fusion | flops 9675466752 | bytes 33060864 | tf_op jit(solution)/shard_map/dot_general | solution.py:378
  519.7 4.8 fusion.40
  528.0 4.1 convolution_convert_fusion
  546.0 57.1 %last_step.1 = (bf16[192,1536]{1,0:T(8,128)(2,1)}, bf16[4,128,1536]{2,1,0:T(8,128)(2,1)}, bf16[4,128,1536]{2,1,0:T(8,128)(2,1)}, f32[4,16,1536]{2,1,0:T(8,128)},...) custom-call(bf16[4,2,192,1536]{3,2,1,0:T(8,128)(2,1)} %bitcast.243, bf16[4,128,1536]{2,1,0:T(8,128)(2,1)} %add.123.to_x_ref, ...), custom_call_target="tpu_custom_call" | custom-call | bytes 160000000 | tf_op jit(solution)/shard_map/last_step/pallas_call | solution.py:1241
  605.1 11.9 %media_back.1 = f32[256,4,1536]{2,1,0:T(4,128)} custom-call(bf16[4,128,1536]{2,1,0:T(8,128)(2,1)} %get-tuple-element.244.refs_0_, bf16[4,128,1536]{2,1,0:T(8,128)(2,1)} %bitcast.258, bf16[4,128,1536]{2,1,0:T(8,128)(2,1)} %copy-done.38, bf16[4,128,1536]{2,1,0:T(8,128)(2,1)} %get-tuple-element.144.refs_3_, bf16[4,128,1536]{2,1,0:T(8,128)(2,1)} %get-tuple-element.243.refs_4_, ...), custom_call_target="tpu_custom_call" | custom-call | bytes 30000000 | tf_op jit(solution)/shard_map/media_back/pallas_call | solution.py:1307
  624.1 12.7 %sum_over_all.1 = f32[4,40,128]{2,1,0:T(8,128)S(1)} custom-call(f32[4,40,128]{2,1,0:T(8,128)S(1)} %concatenate.31.term_ref), custom_call_target="tpu_custom_call" | custom-call | bytes 40000000 | tf_op jit(solution)/shard_map/sum_over_all/pallas_call | solution.py:1021
  642.1 23.0 %adam.1 = (f32[2,3,192,384]{3,2,1,0:T(8,128)}, f32[2,3,192,384]{3,2,1,0:T(8,128)}, f32[2,3,192,384]{3,2,1,0:T(8,128)}, bf16[2,3,192,384]{3,2,1,0:T(8,128)(2,1)},...) custom-call(f32[1,1]{1,0:T(1,128)} %bitcast.70.factor_ref, ...), custom_call_target="tpu_custom_call" | custom-call | flops 35389440 | bytes 49545216 | tf_op jit(solution)/shard_map/adam/pallas_call | solution.py:1380
  (252 shorter events, 127.9 us)
Async XLA Ops:
  7.2 100.3 %all-gather.4.cloned.1.call-start = ((), (), s32[]{:S(2)}) async-start(), calls=%async_computation.2 | async-start | bytes 10616832 | tf_op jit(solution)/shard_map/all_gather | solution.py:1432
  11.3 190.7 %all-gather.6.cloned.1.call-start = ((), (), s32[]{:S(2)}) async-start(), calls=%async_computation.3 | async-start | bytes 10616832 | tf_op jit(solution)/shard_map/all_gather | solution.py:1432
  19.9 267.8 %all-gather.8.cloned.1.call-start = ((), (), s32[]{:S(2)}) async-start(), calls=%async_computation.4 | async-start | bytes 10616832 | tf_op jit(solution)/shard_map/all_gather | solution.py:1432
  20.6 400.8 %reduce-scatter.3.cloned.1.call-start = ((), (), s32[]{:S(2)}) async-start(), calls=%async_computation.5 | async-start | bytes 10616832 | tf_op jit(solution)/shard_map/reduce_scatter | solution.py:1509
  22.1 84.7 %copy-start.56 = (s32[4]{0:T(128)S(1)}, s32[4]{0:T(128)}, u32[]{:S(2)}) copy-start(s32[4]{0:T(128)} %param.21) | copy-start | bytes 52
  106.8 130.4 %copy-start.21 = (s32[4,8]{1,0:T(4,128)}, s32[4,8]{1,0:T(4,128)S(1)}, u32[]{:S(2)}) copy-start(s32[4,8]{1,0:T(4,128)S(1)} %compare_convert_fusion.live_ref) | copy-start | bytes 388
  109.6 59.0 %copy-start.6 = (bf16[256,384]{1,0:T(8,128)(2,1)}, bf16[256,384]{1,0:T(8,128)(2,1)S(1)}, u32[]{:S(2)}) copy-start(bf16[256,384]{1,0:T(8,128)(2,1)S(1)} %convolution_convert_fusion.19.query_ref) | copy-start | bytes 589828
  112.1 56.5 %copy-start.2 = (bf16[256,768]{1,0:T(8,128)(2,1)}, bf16[256,768]{1,0:T(8,128)(2,1)S(1)}, u32[]{:S(2)}) copy-start(bf16[256,768]{1,0:T(8,128)(2,1)S(1)} %convolution_convert_fusion.15.latent_key_ref.latent_value_ref) | copy-start | bytes 1179652
  179.4 28.3 %copy-start.8 = (bf16[256,384]{1,0:T(8,128)(2,1)}, bf16[256,384]{1,0:T(8,128)(2,1)S(1)}, u32[]{:S(2)}) copy-start(bf16[256,384]{1,0:T(8,128)(2,1)S(1)} %attend.2) | copy-start | bytes 589828
  202.0 35.2 %slice-start = ((s8[12582912]{0:T(1024)(128)(4,1)}), s8[4194304]{0:T(1024)(128)(4,1)S(1)}, s32[]{:S(2)}) async-start(s8[12582912]{0:T(1024)(128)(4,1)} %bitcast.214), calls=%async_computation.7 | async-start | bytes 8388608
  202.0 35.2 %slice-start.1 = ((s8[12582912]{0:T(1024)(128)(4,1)}), s8[4194304]{0:T(1024)(128)(4,1)S(1)}, s32[]{:S(2)}) async-start(s8[12582912]{0:T(1024)(128)(4,1)} %bitcast.214), calls=%async_computation.8 | async-start | bytes 8388608
  207.7 29.5 %slice-start.2 = ((s8[12582912]{0:T(1024)(128)(4,1)}), s8[4194304]{0:T(1024)(128)(4,1)S(1)}, s32[]{:S(2)}) async-start(s8[12582912]{0:T(1024)(128)(4,1)} %bitcast.214), calls=%async_computation.9 | async-start | bytes 8388608
  266.2 26.6 %copy-start.12 = (bf16[4,64,1536]{2,1,0:T(8,128)(2,1)}, bf16[4,64,1536]{2,1,0:T(8,128)(2,1)S(1)}, u32[]{:S(2)}) copy-start(bf16[4,64,1536]{2,1,0:T(8,128)(2,1)S(1)} %get-tuple-element.112) | copy-start | bytes 2359300
  266.2 43.1 %copy-start.4 = (f32[4,16,1536]{2,1,0:T(8,128)}, f32[4,16,1536]{2,1,0:T(8,128)S(1)}, u32[]{:S(2)}) copy-start(f32[4,16,1536]{2,1,0:T(8,128)S(1)} %get-tuple-element.114.rows_ref.final_rest_ref) | copy-start | bytes 1179652
  309.2 309.9 %reduce-scatter.5.cloned.1.call-start = ((), (), s32[]{:S(2)}) async-start(), calls=%async_computation.6 | async-start | bytes 15925248 | tf_op jit(solution)/shard_map/reduce_scatter | solution.py:1509
  351.8 25.2 %copy-start.48 = (bf16[256,384]{1,0:T(8,128)(2,1)S(1)}, bf16[256,384]{1,0:T(8,128)(2,1)}, u32[]{:S(2)}) copy-start(bf16[256,384]{1,0:T(8,128)(2,1)} %get-tuple-element.116) | copy-start | bytes 589828
  351.8 30.2 %copy-start.22 = (bf16[8,4,128,1536]{3,2,1,0:T(8,128)(2,1)S(1)}, bf16[8,4,128,1536]{3,2,1,0:T(8,128)(2,1)}, u32[]{:S(2)}) copy-start(bf16[8,4,128,1536]{3,2,1,0:T(8,128)(2,1)} %get-tuple-element.121.rest_0_) | copy-start | bytes 37748740
  376.4 23.3 %copy-start.11 = (bf16[4,64,1536]{2,1,0:T(8,128)(2,1)}, bf16[4,64,1536]{2,1,0:T(8,128)(2,1)S(1)}, u32[]{:S(2)}) copy-start(bf16[4,64,1536]{2,1,0:T(8,128)(2,1)S(1)} %get-tuple-element.119) | copy-start | bytes 2359300
  467.2 23.5 %copy-start.32 = (bf16[1536,768]{1,0:T(8,128)(2,1)}, bf16[1536,768]{1,0:T(8,128)(2,1)S(1)}, u32[]{:S(2)}) copy-start(bf16[1536,768]{1,0:T(8,128)(2,1)S(1)} %get-tuple-element.241) | copy-start | bytes 7077892
  467.2 23.5 %copy-start.34 = (bf16[1536,768]{1,0:T(8,128)(2,1)}, bf16[1536,768]{1,0:T(8,128)(2,1)S(1)}, u32[]{:S(2)}) copy-start(bf16[1536,768]{1,0:T(8,128)(2,1)S(1)} %get-tuple-element.242) | copy-start | bytes 7077892
  474.8 65.2 %collective-permute-start = (bf16[4,128,1536]{2,1,0:T(8,128)(2,1)}, bf16[4,128,1536]{2,1,0:T(8,128)(2,1)}, u32[]{:S(2)}, u32[]{:S(2)}) collective-permute-start(bf16[4,128,1536]{2,1,0:T(8,128)(2,1)} %bitcast.46), channel_id=1, source_target_pairs={{0,2},{2,0},{1,3},{3,1},{4,6},{6,4},{5,7},{7,5},{8,10},{10,8},{9,1... | collective-permute-start | bytes 4718600 | tf_op jit(solution)/shard_map/ppermute | solution.py:1429
  475.5 67.6 %collective-permute-start.1 = (bf16[4,128,1536]{2,1,0:T(8,128)(2,1)}, bf16[4,128,1536]{2,1,0:T(8,128)(2,1)}, u32[]{:S(2)}, u32[]{:S(2)}) collective-permute-start(bf16[4,128,1536]{2,1,0:T(8,128)(2,1)} %bitcast.44), channel_id=1, source_target_pairs={{0,1},{1,0},{2,3},{3,2},{4,5},{5,4},{6,7},{7,6},{8,9},{9,8},{10,11... | collective-permute-start | bytes 4718600 | tf_op jit(solution)/shard_map/ppermute | solution.py:1426
  485.4 118.6 %collective-permute-start.2 = (bf16[4,128,1536]{2,1,0:T(8,128)(2,1)}, bf16[4,128,1536]{2,1,0:T(8,128)(2,1)S(1)}, u32[]{:S(2)}, u32[]{:S(2)}) collective-permute-start(bf16[4,128,1536]{2,1,0:T(8,128)(2,1)} %bitcast.48), channel_id=1, source_target_pairs={{0,1},{1,0},{2,3},{3,2},{4,5},{5,4},{6,7},{7,6},{8,9},{9,8},{10,11... | collective-permute-start | bytes 4718600 | tf_op jit(solution)/shard_map/ppermute | solution.py:1426
  485.4 118.6 %collective-permute-start.3 = (bf16[4,128,1536]{2,1,0:T(8,128)(2,1)}, bf16[4,128,1536]{2,1,0:T(8,128)(2,1)}, u32[]{:S(2)}, u32[]{:S(2)}) collective-permute-start(bf16[4,128,1536]{2,1,0:T(8,128)(2,1)} %bitcast.50), channel_id=1, source_target_pairs={{0,2},{2,0},{1,3},{3,1},{4,6},{6,4},{5,7},{7,5},{8,10},{10,8},{9,1... | collective-permute-start | bytes 4718600 | tf_op jit(solution)/shard_map/ppermute | solution.py:1429
  496.1 18.4 %copy-start.9 = (bf16[256,384]{1,0:T(8,128)(2,1)S(1)}, bf16[256,384]{1,0:T(8,128)(2,1)}, u32[]{:S(2)}) copy-start(bf16[256,384]{1,0:T(8,128)(2,1)} %copy-done.8) | copy-start | bytes 589828
  496.1 20.7 %copy-start.55 = (f32[1536]{0:T(1024)S(1)}, f32[1536]{0:T(1024)}, u32[]{:S(2)}) copy-start(f32[1536]{0:T(1024)} %get-tuple-element.224) | copy-start | bytes 18436
  605.1 12.8 %copy-start.23 = (bf16[192,3072]{1,0:T(8,128)(2,1)S(1)}, bf16[192,3072]{1,0:T(8,128)(2,1)}, u32[]{:S(2)}) copy-start(bf16[192,3072]{1,0:T(8,128)(2,1)} %reduce-scatter.3.cloned.1.call-done.refs_14_.refs_19_) | copy-start | bytes 3538948
  617.0 22.9 %copy-start.50 = (f32[2,6,1536]{2,0,1:T(2,128)S(1)}, f32[2,6,1536]{2,0,1:T(2,128)}, u32[]{:S(2)}) copy-start(f32[2,6,1536]{2,0,1:T(2,128)} %param.35) | copy-start | bytes 221188
  617.0 22.9 %copy-start.53 = (f32[2,6,1536]{2,0,1:T(2,128)S(1)}, f32[2,6,1536]{2,0,1:T(2,128)}, u32[]{:S(2)}) copy-start(f32[2,6,1536]{2,0,1:T(2,128)} %param.37) | copy-start | bytes 221188
  617.0 22.9 %copy-start.54 = (f32[2,6,1536]{2,0,1:T(2,128)S(1)}, f32[2,6,1536]{2,0,1:T(2,128)}, u32[]{:S(2)}) copy-start(f32[2,6,1536]{2,0,1:T(2,128)} %param.36) | copy-start | bytes 221188
  642.1 23.0 %copy-start.52 = (f32[4,16,1536]{2,1,0:T(8,128)S(1)}, f32[4,16,1536]{2,1,0:T(8,128)}, u32[]{:S(2)}) copy-start(f32[4,16,1536]{2,1,0:T(8,128)} %get-tuple-element.286) | copy-start | bytes 1179652
  642.1 23.8 %copy-start.51 = (f32[4,16,1536]{2,1,0:T(8,128)S(1)}, f32[4,16,1536]{2,1,0:T(8,128)}, u32[]{:S(2)}) copy-start(f32[4,16,1536]{2,1,0:T(8,128)} %get-tuple-element.287) | copy-start | bytes 1179652
  (48 other events, 201.7 us)
Sparse Core Ops, SparseCore 0:
  11.4 93.4 all-gather.3
  107.1 89.1 all-gather.5
  198.5 89.1 all-gather.7
  309.3 97.9 reduce-scatter.2
  421.6 146.0 reduce-scatter.4

commit v4 on v3

--- a/solution.py
+++ b/solution.py
@@ -711,7 +711,7 @@
 def attend_back_kernel(
     live_ref, query_ref, latent_key_ref, latent_value_ref, key_ref, value_ref, slope_ref, *rest, scale
 ):
-    query_slope_ref, latent_slope_ref, media_slope_ref = rest[-3:]
+    query_slope_ref, latent_slope_ref, media_slope_ref, sums_ref = rest[-4:]
     video = pl.program_id(0)
     slots, patches = key_ref.shape[0], key_ref.shape[2]
     pairs = slots // 2
@@ -745,6 +745,7 @@
         [jnp.sum(a * b, axis=0, keepdims=True) for a, b in zip(shares, share_slopes)],
     )
     query_slope = jnp.zeros((rows, columns), F32)
+    key_sum, value_sum = jnp.zeros((1, columns), F32), jnp.zeros((1, columns), F32)
     for at in range(pairs + 1):
         keys = keys_of(key_ref, at) if at < pairs else latent_key_ref[...]
         score_slope = (shares[at] * (share_slopes[at] - row_total)).astype(BF)
@@ -754,11 +755,15 @@
             score_slope, keys, TN, preferred_element_type=F32
         )
         if at < pairs:
+            key_sum = key_sum + jnp.sum(key_slope.astype(F32), axis=0, keepdims=True)
+            value_sum = value_sum + jnp.sum(value_slope.astype(F32), axis=0, keepdims=True)
             media_slope_ref[2 * at : 2 * at + 2, 0, :, :columns] = key_slope.reshape(2, patches, columns)
             media_slope_ref[2 * at : 2 * at + 2, 0, :, columns:] = value_slope.reshape(2, patches, columns)
         else:
             latent_slope_ref[:, :columns] = key_slope
             latent_slope_ref[:, columns:] = value_slope
+    sums_ref[0, :, :columns] = key_sum
+    sums_ref[0, :, columns:] = value_sum
     query_slope_ref[...] = (gather_heads(query_slope, count) * scale).astype(BF)
 
 
@@ -786,12 +791,14 @@
             jax.ShapeDtypeStruct(query.shape, BF),
             jax.ShapeDtypeStruct(latent_pair.shape, BF),
             jax.ShapeDtypeStruct(keys.shape, BF),
+            jax.ShapeDtypeStruct((videos, 1, 2 * columns), F32),
         ),
         in_specs=in_specs,
         out_specs=(
             row_block,
             pl.BlockSpec((count, 2 * columns), lambda v: (v, 0)),
             pl.BlockSpec((slots, 1, patches, 2 * columns), lambda v: (0, v, 0, layer)),
+            pl.BlockSpec((1, 1, 2 * columns), lambda v: (v, 0, 0)),
         ),
         input_output_aliases=aliases,
         compiler_params=pltpu.CompilerParams(vmem_limit_bytes=60 * MIB),
@@ -804,45 +811,85 @@
     )(live, query, latent_pair, latent_pair, keys, keys, slope, *earlier)
 
 
-def product_pair_kernel(first_ref, second_ref, third_ref, fourth_ref, *rest):
-    out_ref = rest[-1]
-    kind = pl.program_id(0) - (len(rest) - 1)
-
-    @pl.when(kind == 0)
+def product_pair_kernel(begin, first_ref, second_ref, third_ref, fourth_ref, *rest):
+    step = pl.program_id(0)
+    count = len(rest) - 5
+    extra, (out_ref, tile_ref, extra_ref, tile_sem, extra_sem) = rest[:count], rest[count:]
+    cut, half = tile_ref.shape[2], pl.num_programs(0) // 2
+
+    def moves():
+        at = 0
+        for number, ref in enumerate(extra):
+            lines = pl.ds(at, ref.shape[1])
+            yield pltpu.make_async_copy(ref, extra_ref.at[:, lines], extra_sem.at[number])
+            at += ref.shape[1]
+
+    def store(at):
+        lines = pl.ds(pl.multiple_of(begin + at * cut, 128), cut)
+        return pltpu.make_async_copy(tile_ref.at[at % 2], out_ref.at[:, lines], tile_sem.at[at % 2])
+
+    def store_extra():
+        return pltpu.make_async_copy(extra_ref, out_ref.at[:, pl.ds(0, begin)], extra_sem.at[count])
+
+    if count:
+
+        @pl.when(step == 0)
+        def _():
+            for copy in moves():
+                copy.start()
+
+        @pl.when(step == 2)
+        def _():
+            for copy in moves():
+                copy.wait()
+            store_extra().start()
+
+    @pl.when(step >= 2)
     def _():
-        out_ref[...] = mm(first_ref[...], second_ref[...], TN)
-
-    @pl.when(kind == 1)
+        store(step - 2).wait()
+
+    @pl.when(step < half)
     def _():
-        out_ref[...] = mm(third_ref[...], fourth_ref[...], TN)
-
-    if len(rest) > 1:
-        @pl.when(kind < 0)
-        def _():
-            out_ref[...] = rest[0][...]
+        tile_ref[step % 2] = mm(first_ref[...], second_ref[...], TN)
+
+    @pl.when(step >= half)
+    def _():
+        tile_ref[step % 2] = mm(third_ref[...], fourth_ref[...], TN)
+
+    store(step).start()
+
+    @pl.when(step == 2 * half - 1)
+    def _():
+        store(step - 1).wait()
+        store(step).wait()
+        if count:
+            store_extra().wait()
 
 
 def product_pair(first, second, third, fourth, *extra):
     rows, width, columns = first.shape[0], first.shape[1], second.shape[1]
     cut = columns // 3
-    left = pl.BlockSpec((rows, width), lambda i, j: (0, 0))
-    first_kind = len(extra)
-
-    def at(i, j, kind):
-        return jnp.where(i == kind, j, jnp.where(i < kind, 0, 2))
-
+    begin = sum(piece.shape[1] for piece in extra)
+    left = pl.BlockSpec((rows, width), lambda i: (0, 0))
+    any_spec = pl.BlockSpec(memory_space=pl.ANY)
     return pl.pallas_call(
-        product_pair_kernel,
-        grid=(2 + len(extra), 3),
-        out_shape=jax.ShapeDtypeStruct((width, (2 + len(extra)) * columns), BF),
+        functools.partial(product_pair_kernel, begin),
+        grid=(6,),
+        out_shape=jax.ShapeDtypeStruct((width, begin + 2 * columns), BF),
         in_specs=[
             left,
-            pl.BlockSpec((rows, cut), lambda i, j: (0, at(i, j, first_kind))),
+            pl.BlockSpec((rows, cut), lambda i: (0, jnp.minimum(i, 2))),
             left,
-            pl.BlockSpec((rows, cut), lambda i, j: (0, at(i, j, first_kind + 1))),
+            pl.BlockSpec((rows, cut), lambda i: (0, jnp.maximum(i - 3, 0))),
         ]
-        + [pl.BlockSpec((width, cut), lambda i, j: (0, at(i, j, 0)))] * len(extra),
-        out_specs=pl.BlockSpec((width, cut), lambda i, j: (0, 3 * i + j)),
+        + [any_spec] * len(extra),
+        out_specs=any_spec,
+        scratch_shapes=[
+            pltpu.VMEM((2, width, cut), BF),
+            pltpu.VMEM((width, max(begin, 128)), BF),
+            pltpu.SemaphoreType.DMA((2,)),
+            pltpu.SemaphoreType.DMA((4,)),
+        ],
         compiler_params=pltpu.CompilerParams(vmem_limit_bytes=60 * MIB),
         cost_estimate=pl.CostEstimate(
             flops=4 * rows * width * columns, bytes_accessed=8 * width * columns, transcendentals=0
@@ -976,13 +1023,28 @@
     return got if not last else (*got, None)
 
 
-def sum_kernel(heads, rows, term_ref, out_ref, plane_ref, line_ref, part_ref, *sems):
+def sum_kernel(heads, rows, lines, term_in, *refs):
+    shares, (out_ref, term_ref, plane_ref, line_ref, part_ref), sems = refs[:3], refs[3:8], refs[8:]
     me_head, me_row = lax.axis_index(HEADS), lax.axis_index(ROWS)
     barrier = pltpu.get_barrier_semaphore()
     for step in range(1, heads):
         pl.semaphore_signal(barrier, inc=1, device_id={HEADS: (me_head + step) % heads})
     for step in range(1, rows):
         pl.semaphore_signal(barrier, inc=1, device_id={ROWS: (me_row + step) % rows})
+    term_ref[...] = term_in[...]
+    total = jnp.zeros((16, 384), F32)
+    for share in shares:
+
+        def add_squares(at, total, share=share):
+            line = pl.ds(pl.multiple_of(at * 16, 16), 16)
+            for begin in range(0, share.shape[1], 384):
+                wide = share[line, begin : begin + 384].astype(F32)
+                total = total + wide * wide
+            return total
+
+        total = lax.fori_loop(0, share.shape[0] // 16, add_squares, total)
+    total = jnp.sum(total, axis=0, keepdims=True)
+    term_ref[0, lines : lines + 1] = total[:, :128] + total[:, 128:256] + total[:, 256:]
     pl.semaphore_wait(barrier, heads - 1 + rows - 1)
 
     def spread(axis, me, count, source_of, slots_ref, own, send, recv):
@@ -1016,14 +1078,15 @@
     spread(HEADS, me_head, heads, lambda peer: part_ref.at[1], out_ref, part_ref[1], *sems[4:6])
 
 
-def sum_fast(term, heads, rows, identity):
+def sum_fast(term, shares, lines, heads, rows, identity):
     block = term.shape[1:]
     return pl.pallas_call(
-        functools.partial(sum_kernel, heads, rows),
+        functools.partial(sum_kernel, heads, rows, lines),
         out_shape=jax.ShapeDtypeStruct(term.shape, F32),
-        in_specs=[vmem_spec()],
+        in_specs=[vmem_spec()] * 4,
         out_specs=vmem_spec(),
         scratch_shapes=[
+            pltpu.VMEM(term.shape, F32),
             pltpu.VMEM((heads, *block), F32),
             pltpu.VMEM((rows, *block), F32),
             pltpu.VMEM((2, *block), F32),
@@ -1035,19 +1098,25 @@
             pltpu.SemaphoreType.DMA((heads - 1,)),
         ],
         compiler_params=pltpu.CompilerParams(
-            collective_id=identity, has_side_effects=True, vmem_limit_bytes=8 * MIB
+            collective_id=identity, has_side_effects=True, vmem_limit_bytes=16 * MIB
         ),
         cost_estimate=pl.CostEstimate(flops=0, bytes_accessed=40 * 1000 * 1000, transcendentals=0),
         name="sum_over_all",
-    )(term)
+    )(term, *shares)
 
 
 def last_kernel(
     chips,
     heads,
-    part_ref,
-    to_x_ref,
-    to_y_ref,
+    query_ref,
+    pair_ref,
+    rest_part_ref,
+    near_x_ref,
+    near_y_ref,
+    over_x_ref,
+    over_y_ref,
+    slopes_ref,
+    scaled_ref,
     slots_ref,
     final_ref,
     final_rest_ref,
@@ -1060,13 +1129,21 @@
     new_ref,
     sums_ref,
     final_out_ref,
+    back_ref,
     mine_ref,
     other_ref,
     down_ref,
     up_ref,
     landed_ref,
     final_landed_ref,
+    to_x_ref,
+    to_y_ref,
+    add_x_ref,
+    add_y_ref,
+    weight_ref,
+    chunk_ref,
     near_sem,
+    local_sem,
     slot_send,
     slot_recv,
     final_send,
@@ -1097,34 +1174,67 @@
     share = rest_ref.shape[1]
     slots = start_scatter(head, heads, share, slots_ref, landed_ref, slot_send, slot_recv)
     finals = start_scatter(head, heads, share, final_ref, final_landed_ref, final_send, final_recv)
-    over = pltpu.make_async_remote_copy(
-        src_ref=part_ref.at[:, 1 - core],
-        dst_ref=other_ref,
-        send_sem=near_sem.at[0],
-        recv_sem=near_sem.at[1],
-        device_id={ROWS: sibling},
-    )
-    over.start()
-    keep = pltpu.make_async_copy(part_ref.at[:, core], mine_ref, near_sem.at[2])
-    keep.start()
-    media_x = pltpu.make_async_remote_copy(
-        src_ref=to_x_ref,
-        dst_ref=from_x_ref,
-        send_sem=near_sem.at[3],
-        recv_sem=near_sem.at[4],
-        device_id={HEADS: beside_x},
-    )
-    media_y = pltpu.make_async_remote_copy(
-        src_ref=to_y_ref,
-        dst_ref=from_y_ref,
-        send_sem=near_sem.at[5],
-        recv_sem=near_sem.at[6],
-        device_id={HEADS: beside_y},
-    )
-    media_x.start()
-    media_y.start()
-    keep.wait()
-    over.wait()
+    whole = [query_ref, pair_ref, rest_part_ref]
+    begins = [0]
+    for ref in whole:
+        begins.append(begins[-1] + ref.shape[3])
+    over, keep = [], []
+    for at, ref in enumerate(whole):
+        lines = pl.ds(begins[at], ref.shape[3])
+        copy = pltpu.make_async_remote_copy(
+            src_ref=ref.at[:, 1 - core],
+            dst_ref=other_ref.at[:, :, lines],
+            send_sem=near_sem.at[at],
+            recv_sem=near_sem.at[3 + at],
+            device_id={ROWS: sibling},
+        )
+        copy.start()
+        over.append(copy)
+        copy = pltpu.make_async_copy(ref.at[:, core], mine_ref.at[:, :, lines], local_sem.at[at])
+        copy.start()
+        keep.append(copy)
+    loads = []
+    for at, (source, target) in enumerate(
+        (
+            (near_x_ref, to_x_ref),
+            (over_y_ref, add_x_ref),
+            (near_y_ref, to_y_ref),
+            (over_x_ref, add_y_ref),
+            (scaled_ref, weight_ref),
+            (slopes_ref.at[pl.ds(0, 2)], chunk_ref),
+        )
+    ):
+        loads.append(pltpu.make_async_copy(source, target, local_sem.at[3 + at]))
+        loads[-1].start()
+    medias = []
+    for at, (to_ref, add_ref, from_ref, peer) in enumerate(
+        ((to_x_ref, add_x_ref, from_x_ref, beside_x), (to_y_ref, add_y_ref, from_y_ref, beside_y))
+    ):
+        loads[2 * at].wait()
+        loads[2 * at + 1].wait()
+        for video in range(to_ref.shape[0]):
+
+            def add_slopes(row, carry, to_ref=to_ref, add_ref=add_ref, video=video):
+                lines = pl.ds(pl.multiple_of(row * 16, 16), 16)
+                to_ref[video, lines] = (
+                    to_ref[video, lines].astype(F32) + add_ref[video, lines].astype(F32)
+                ).astype(BF)
+                return carry
+
+            lax.fori_loop(0, to_ref.shape[1] // 16, add_slopes, 0)
+        copy = pltpu.make_async_remote_copy(
+            src_ref=to_ref,
+            dst_ref=from_ref,
+            send_sem=near_sem.at[6 + 2 * at],
+            recv_sem=near_sem.at[7 + 2 * at],
+            device_id={HEADS: peer},
+        )
+        copy.start()
+        medias.append(copy)
+    for copy in keep:
+        copy.wait()
+    for copy in over:
+        copy.wait()
     for chip in range(chips):
 
         def add_rows(at, carry, chip=chip):
@@ -1180,6 +1290,19 @@
                 def _():
                     chain(step, piece, down).start()
 
+    loads[4].wait()
+    loads[5].wait()
+    videos, patches, width = chunk_ref.shape[1:]
+    tile = width // 4
+
+    def own_slopes(at, carry):
+        half = at // 4
+        lines = pl.ds(pl.multiple_of((at % 4) * tile, tile), tile)
+        made = mm(chunk_ref[half].reshape(videos * patches, width), weight_ref[lines], NT)
+        back_ref[half, :, :, lines] = made.reshape(videos, patches, tile)
+        return carry
+
+    lax.fori_loop(0, 8, own_slopes, 0)
     rows = rows_ref[...]
     centred = rows - jnp.mean(rows, axis=-1, keepdims=True)
     scale = lax.rsqrt(jnp.mean(centred * centred, axis=-1, keepdims=True) + EPS_NORM)
@@ -1225,65 +1348,74 @@
 
     for copy in slots + finals:
         copy.wait_send()
-    media_x.wait()
-    media_y.wait()
-
-
-def last_step(partial, to_x, to_y, slots, final, final_rest, rows, rest, gain, heads, chips):
-    depth, columns = partial.shape[0] // (2 * chips), partial.shape[1]
+    for copy in medias:
+        copy.wait()
+
+
+def last_step(parts, near, over, slopes, scaled, slots, final, final_rest, rows, rest, gain, heads, chips):
+    depth, columns = parts[0].shape[0] // (2 * chips), sum(part.shape[1] for part in parts)
     videos, share, width = rest.shape
     pieces = 4
     any_spec = pl.BlockSpec(memory_space=pl.ANY)
     block = pltpu.VMEM((chips, depth, columns), BF)
     steps = pltpu.VMEM((chips - 1, depth, columns), BF)
+    landed = pltpu.VMEM((heads - 1, videos, share, width), BF)
+    chunk = pltpu.VMEM(near[0].shape, BF)
     chain_sem = pltpu.SemaphoreType.DMA((chips - 1, pieces))
     slot_sem = pltpu.SemaphoreType.DMA((heads - 1,))
+    chunk_kind = jax.ShapeDtypeStruct(near[0].shape, BF)
     return pl.pallas_call(
         functools.partial(last_kernel, chips, heads),
         out_shape=(
             jax.ShapeDtypeStruct((depth, columns), BF),
-            jax.ShapeDtypeStruct(to_x.shape, BF),
-            jax.ShapeDtypeStruct(to_y.shape, BF),
+            chunk_kind,
+            chunk_kind,
             jax.ShapeDtypeStruct(rest.shape, F32),
             jax.ShapeDtypeStruct((2, width), F32),
             jax.ShapeDtypeStruct(rest.shape, F32),
-        ),
-        in_specs=[any_spec] * 3 + [vmem_spec()] * 6,
-        out_specs=(vmem_spec(), any_spec, any_spec, vmem_spec(), vmem_spec(), vmem_spec()),
-        scratch_shapes=[
-            block,
-            block,
-            steps,
-            steps,
-            pltpu.VMEM((heads - 1, videos, share, width), BF),
-            pltpu.VMEM((heads - 1, videos, share, width), BF),
-            pltpu.SemaphoreType.DMA((7,)),
-            slot_sem,
-            slot_sem,
-            slot_sem,
-            slot_sem,
-            chain_sem,
-            chain_sem,
-            chain_sem,
-            chain_sem,
-        ],
+            jax.ShapeDtypeStruct((2, *near[0].shape), BF),
+        ),
+        in_specs=[any_spec] * 9 + [vmem_spec()] * 6,
+        out_specs=(vmem_spec(), any_spec, any_spec) + (vmem_spec(),) * 4,
+        scratch_shapes=[block, block, steps, steps, landed, landed]
+        + [chunk] * 4
+        + [
+            pltpu.VMEM(scaled.shape, BF),
+            pltpu.VMEM((2, *near[0].shape), BF),
+            pltpu.SemaphoreType.DMA((10,)),
+            pltpu.SemaphoreType.DMA((9,)),
+        ]
+        + [slot_sem] * 4
+        + [chain_sem] * 4,
         compiler_params=pltpu.CompilerParams(
             collective_id=7, has_side_effects=True, vmem_limit_bytes=60 * MIB
         ),
         cost_estimate=pl.CostEstimate(flops=0, bytes_accessed=160 * 1000 * 1000, transcendentals=0),
         name="last_step",
-    )(partial.reshape(chips, 2, depth, columns), to_x, to_y, slots, final, final_rest, rows, rest, gain)
-
-
-def media_back_kernel(*refs):
-    first, second, out_ref = refs[:4], refs[4:8], refs[-1]
-
-    def write(own_ref, *terms):
-        rows = own_ref[...].astype(F32)
+    )(
+        *[part.reshape(chips, 2, depth, part.shape[1]) for part in parts],
+        *near,
+        *over,
+        slopes,
+        scaled,
+        slots,
+        final,
+        final_rest,
+        rows,
+        rest,
+        gain,
+    )
+
+
+def media_back_kernel(own_ref, back_ref, *refs):
+    first, second, out_ref = refs[:2], refs[2:4], refs[-1]
+
+    def write(*terms):
+        rows = own_ref[0].astype(F32)
         centred = rows - jnp.mean(rows, axis=-1, keepdims=True)
         spread = lax.rsqrt(jnp.mean(centred * centred, axis=-1, keepdims=True) + EPS_NORM)
         hat = centred * spread
-        total = functools.reduce(jnp.add, [term[...].astype(F32) for term in terms])
+        total = functools.reduce(jnp.add, [term[...].astype(F32) for term in terms], back_ref[0].astype(F32))
         total = total - jnp.mean(total, axis=-1, keepdims=True) - hat * jnp.mean(total * hat, axis=-1, keepdims=True)
         total = total * spread
         for video in range(rows.shape[0]):
@@ -1298,22 +1430,23 @@
         write(*second)
 
 
-def media_back(first, second):
-    videos, rows, width = first[0].shape
+def media_back(own, back, in_x, in_y):
+    _, videos, rows, width = own.shape
     cut = 32
     steps = rows // cut
-    specs = [pl.BlockSpec((videos, cut, width), lambda i, j: (0, jnp.where(i == 0, j, steps - 1), 0))] * 4
-    specs += [pl.BlockSpec((videos, cut, width), lambda i, j: (0, jnp.where(i == 1, j, 0), 0))] * 4
+    both = pl.BlockSpec((1, videos, cut, width), lambda i, j: (i, 0, j, 0))
+    specs = [pl.BlockSpec((videos, cut, width), lambda i, j: (0, jnp.where(i == 0, j, steps - 1), 0))] * 2
+    specs += [pl.BlockSpec((videos, cut, width), lambda i, j: (0, jnp.where(i == 1, j, 0), 0))] * 2
     return pl.pallas_call(
         media_back_kernel,
         grid=(2, steps),
         out_shape=jax.ShapeDtypeStruct((2 * rows, videos, width), F32),
-        in_specs=specs,
+        in_specs=[both, both] + specs,
         out_specs=pl.BlockSpec((cut, videos, width), lambda i, j: (steps * i + j, 0, 0)),
         compiler_params=pltpu.CompilerParams(vmem_limit_bytes=60 * MIB),
         cost_estimate=pl.CostEstimate(flops=0, bytes_accessed=30 * 1000 * 1000, transcendentals=0),
         name="media_back",
-    )(*first, *second)
+    )(own, back, in_x[0], in_y[0], in_x[1], in_y[1])
 
 
 def adam_kernel(rates, begins, factor_ref, *refs):
@@ -1334,14 +1467,13 @@
             def _():
                 for part in range(weight_ref.shape[1]):
                     grad = ins[kind][3 + layer][:, part * columns : (part + 1) * columns]
-                    mean, square, weight = adam_step(
-                        weight_ref[0, part],
-                        first_ref[0, part],
-                        second_ref[0, part],
-                        grad.astype(F32) * factor,
-                        rates[kind],
-                        WEIGHT_DECAY,
-                    )
+                    scaled = grad.astype(F32) * factor
+                    mean = BETA_ONE * first_ref[0, part] + (1.0 - BETA_ONE) * scaled
+                    square = BETA_TWO * second_ref[0, part] + (1.0 - BETA_TWO) * scaled * scaled
+                    root = jnp.sqrt(square * (1.0 / (1.0 - BETA_TWO**STEP))) + ADAM_EPS
+                    change = (mean * (1.0 / (1.0 - BETA_ONE**STEP))) / root
+                    weight = weight_ref[0, part]
+                    weight = weight - rates[kind] * (change + WEIGHT_DECAY * weight)
                     mean_ref[0, part] = mean
                     square_ref[0, part] = square
                     next_ref[0, part] = weight
@@ -1462,6 +1594,17 @@
     near, latent_norm = gather_near(own, normed, heads_count)
     keys, media_hat, far = media_near(own, near, media_gains, first_set, 2 * layers * columns, heads_count)
     keys, media_hat, feed_slope = media_far(far, media_gains, first_set, slope_rows, keys, media_hat, heads_count)
+    scaled = jnp.concatenate(
+        [
+            (
+                pair_weights[:, 2 * l * head_columns : 2 * (l + 1) * head_columns].astype(F32)
+                * norm_gains[l, 0][:, None]
+            ).astype(BF)
+            for l in range(layers)
+        ],
+        axis=1,
+    )
+
     kept = []
     for layer in range(layers):
         query_weight, out_weight = query_full[layer], out_full[layer]
@@ -1470,6 +1613,9 @@
         latent_pair = mm(flat(latent_norm), pair_weight)
         mixed = attend_fast(live, query, latent_pair, keys, layer, scale)
         part = mm(mixed, out_weight, NT).reshape(videos, latent_count, width)
+        if layer == layers - 1:
+            gain_rows = [rows.reshape(-1, width) for rows in (norm_gains, gain_first, gain_second)]
+            part, scaled, *gain_rows = lax.optimization_barrier((part, scaled, *gain_rows))
         middle, feed_norm = forward_exchange(part, latent, norm_gains[layer, 4:6], heads_count)
         hidden_pre = mm(flat(feed_norm), widen_full[layer], None, F32)
         hidden = jax.nn.gelu(hidden_pre).astype(BF)
@@ -1486,17 +1632,6 @@
     gain_parts = [None] * layers
     shares, waiting = [], []
     media_slopes = ()
-
-    scaled = jnp.concatenate(
-        [
-            (
-                pair_weights[:, 2 * l * head_columns : 2 * (l + 1) * head_columns].astype(F32)
-                * norm_gains[l, 0][:, None]
-            ).astype(BF)
-            for l in range(layers)
-        ],
-        axis=1,
-    )
 
     def hat_slope(slopes, group, half):
         return mm(flat(slopes[2 * group + half]), scaled, NT).reshape(videos, -1, width)
@@ -1527,7 +1662,7 @@
         branch_slope = flat(branch_slope)
         mixed_slope = mm(branch_slope, out_weight)
         out_grad = mm(branch_slope, mixed, TN)
-        query_slope, latent_slopes, media_slopes = attend_back_fast(
+        query_slope, latent_slopes, media_slopes, slope_sums = attend_back_fast(
             live, query, latent_pair, keys, mixed_slope, layer, scale, (media_slopes,) if layer < layers - 1 else ()
         )
         part = (mm(query_slope, query_weight, NT, F32) + mm(latent_slopes, pair_weight, NT, F32)).astype(BF)
@@ -1550,7 +1685,7 @@
         query_grad = mm(flat(latent_norm), query_slope, TN)
         pair_slope = flat(media_slopes[..., 2 * layer * head_columns : 2 * (layer + 1) * head_columns])
         hat_grad = mm(flat(media_hat), pair_slope, TN, F32)
-        slope_sum = jnp.sum(pair_slope.astype(F32), axis=0)
+        slope_sum = jnp.sum(slope_sums[:, 0], axis=0)
         gain, shift = norm_gains[layer, 0], norm_gains[layer, 1]
         pair_grad = (
             mm(flat(latent_norm), latent_slopes, TN, F32)
@@ -1561,42 +1696,27 @@
         media_sums = jnp.stack(
             (jnp.sum(wide * hat_grad, axis=1), jnp.sum(wide * slope_sum[None, :], axis=1))
         )
-        inward_grad = jnp.concatenate((query_grad, pair_grad, out_grad), axis=1)
+        parts = (query_grad, pair_grad, out_grad)
         if last:
-            near = [near[0] + over_y, near[1] + over_x]
-            last_grad, *near = lax.optimization_barrier((inward_grad, *near))
-        else:
-            waiting = [inward_grad]
+            *parts, over_x, over_y, near[0], near[1] = lax.optimization_barrier((*parts, over_x, over_y, *near))
+        waiting = parts
         gain_parts[layer] = [media_sums, None if last else latent_sums, feed_sums]
 
-    back = [hat_slope(media_slopes, 0, half) for half in range(2)]
-    last_grad, *back = lax.optimization_barrier((last_grad, *back))
-    share_out, in_x[1], in_y[0], slope, gain_parts[0][1], latent = last_step(
-        last_grad, *near, last_part, final_part, final_rest, latents, middle_slope, norm_gains[0, 2:4], heads_count, rows_count // 2
-    )
-    media_slope = media_back(*[(own[half], back[half], in_x[half], in_y[half]) for half in range(2)])
-
-    def square_sum(rows):
-        wide = rows.astype(F32)
-        return jnp.sum(wide * wide)
+    share_out, in_x[1], in_y[0], slope, gain_parts[0][1], latent, back = last_step(
+        *(parts, near, (over_x, over_y), media_slopes, scaled),
+        *(last_part, final_part, final_rest, latents, middle_slope, norm_gains[0, 2:4]),
+        *(heads_count, rows_count // 2),
+    )
+    media_slope = media_back(own, back, in_x, in_y)
 
     shares.append(share_out)
-    early = sum(square_sum(piece) for piece in shares[:-1])
     gain_term = jnp.concatenate([rows for parts in gain_parts for rows in parts], axis=0).reshape(heads_count, -1, 128)
     lines = gain_term.shape[1]
-    squares = jnp.full((heads_count, 8 - lines % 8, 128), early + square_sum(shares[-1]), F32)
-    totals = sum_fast(jnp.concatenate((gain_term, squares), axis=1), heads_count, rows_count, 9)
+    gain_term = jnp.pad(gain_term, ((0, 0), (0, 8 - lines % 8), (0, 0)))
+    totals = sum_fast(gain_term, shares, lines, heads_count, rows_count, 9)
     gain_total = totals[:, :lines].reshape(layers, 6, width)
-    square_total = totals[0, lines, 0]
-    gain_total = totals[:, :lines].reshape(layers, 6, width)
-    square_total = totals[0, lines, 0]
-    gain_total = totals[:, :lines].reshape(layers, 6, width)
-    square_total = totals[0, lines, 0]
-    gain_total = totals[:, :lines].reshape(layers, 6, width)
-    square_total = totals[0, lines, 0]
-    feed_parts = [piece[:, : 2 * units] for piece in shares[-2::-1]]
-    inward_parts = [shares[-1]] + [piece[:, 2 * units :] for piece in shares[-2:0:-1]]
-    gradient_norm = jnp.sqrt(square_total + jnp.sum(gain_total * gain_total))
+    square_total = jnp.sum(totals[0, lines]) + jnp.sum(totals[:, :lines] * totals[:, :lines])
+    gradient_norm = jnp.sqrt(square_total)
     factor = CLIP_LEVEL / jnp.maximum(gradient_norm, CLIP_LEVEL)
 
     factor_cell = factor.reshape(1, 1)
@@ -1636,10 +1756,8 @@
     )
     results = [latent, slope, media_slope, gradient_norm, *inward_made, *turn_back(outward_made)]
     results += [rows[:, 0] for rows in widen_made] + turn_back(narrow_made)
-    mean_new, square_new, weight_new = adam_step(
-        norm_gains, gain_first, gain_second, gain_total * factor, RATE_GAINS, 0.0
-    )
-    results = results + [mean_new, square_new, weight_new, gain_total[:, 4:6]]
+    made = adam_step(*gain_rows, gain_total.reshape(-1, width) * factor, RATE_GAINS, 0.0)
+    results = results + [rows.reshape(norm_gains.shape) for rows in made] + [gain_total[:, 4:6]]
     return tuple(results)
 
 

time: 680 us -> 667 us (0.981)
  Pallas kernels: 429 us -> 448 us
  other arithmetic: 31.9 us -> 12.9 us
  local copies, waits for them, and re-layouts: 40.9 us -> 33.5 us
    pallas_call x1, Pallas kernels: 57.1 us -> 72.9 us  [last_step(): pl.pallas_call(functools.partial(last_kernel, chips, heads), out_shape=(j...]
    reduce_sum x5 -> x3, other arithmetic: 10.8 us -> 2.11 us  [the longest x2 1.51 us: local_fast(): slope_sum = jnp.sum(slope_sums[:, 0], axis=0)]
    unnamed x155 -> x163, local copies, waits for them, and re-layouts: 25.5 us -> 22.8 us
    dot_general x36 -> x34, matrix products: 126 us -> 128 us  [mm(): lax.dot_general(left, right, dims, preferred_element_type=F32).astype(out)]
  transfers between devices with their start and end apart: 9 -> 9, of which waited for: 1 -> 1; matrix products, arithmetic and copies ran while one was open for 23% -> 20% of each run, Pallas kernels for 57% -> 61%
where the time goes in v4:
time: 667 us; the launch traced here: 662 us
  Pallas kernels  448 us (67%)
  matrix products  128 us (19%)
  local copies, waits for them, and re-layouts  33.5 us (5%)
  between operations  17.7 us (3%)
  waiting for transfers between devices  17.2 us (3%)
  other arithmetic  12.9 us (2%)
    dot_general x34, matrix products, mm(): lax.dot_general(left, right, dims, preferred_element_type=F32).astype(out)  128 us
    pallas_call x1, Pallas kernels, gather_near(): pl.pallas_call(functools.partial(gather_kernel, count), out_shape=(jax.Sh...  82.8 us
    pallas_call x1, Pallas kernels, last_step(): pl.pallas_call(functools.partial(last_kernel, chips, heads), out_shape=(j...  72.9 us
    pallas_call x3, Pallas kernels, backward_exchange(): pl.pallas_call(functools.partial(backward_kernel, count, last), out_shape...  67.7 us
    pallas_call x3, Pallas kernels, forward_exchange(): pl.pallas_call(functools.partial(forward_kernel, count, last), out_shape=...  61.7 us
    pallas_call x1, Pallas kernels, media_near(): pl.pallas_call(functools.partial(near_kernel, count), grid=(6, 2), out_sh...  41.6 us
    pallas_call x2, Pallas kernels, attend_back_fast(): pl.pallas_call(functools.partial(attend_back_kernel, scale=scale), grid=(...  24.1 us
    pallas_call x1, Pallas kernels, adam_fast(): pl.pallas_call(functools.partial(adam_kernel, [kind[-1] for kind in kinds...  23 us
  transfers between devices with their start and end apart: 9, of which 1 were waited for; matrix products, arithmetic and copies ran while one was open for 20% of the time, Pallas kernels for 61%

profile of v4, /device:TPU:0, one launch (start us, length us, event | category | flops | bytes accessed | tf_op | source)
XLA Modules:
  0.0 661.7 jit_solution(15321448879358283260)
XLA Ops:
  25.9 82.8 %gather_near.1 = (bf16[4,4,128,1536]{3,2,1,0:T(8,128)(2,1)}, bf16[4,64,1536]{2,1,0:T(8,128)(2,1)}) custom-call(bf16[2,4,128,1536]{3,2,1,0:T(8,128)(2,1)} %bitcast.239, bf16[4,16,1536]{2,1,0:T(8,128)(2,1)} %add_convert_fusion.norm_ref), custom_call_target="tpu_custom_call" | custom-call | bytes 250000000 | tf_op jit(solution)/shard_map/gather_near/pallas_call | solution.py:438
  114.4 41.6 %media_near.1 = (bf16[8,4,128,1536]{3,2,1,0:T(8,128)(2,1)}, bf16[8,4,128,1536]{3,2,1,0:T(8,128)(2,1)}, bf16[2,4,128,1536]{3,2,1,0:T(8,128)(2,1)}) custom-call(bf16[2,4,128,1536]{3,2,1,0:T(8,128)(2,1)} %bitcast.240, bf16[4,4,128,1536]{3,2,1,0:T(8,128)(2,1)} %get-tuple-element.109.near_ref.source_ref, f32[2,2,1536]{2,1,0:T(2,128)} %slice.216.gain_ref, ...), custom_call_target="tpu_custom_call" | custom-call | flops 14495514624 | bytes 18874368 | tf_op jit(solution)/shard_map/media_near/pallas_call | solution.py:523
  156.0 15.3 %media_far.1 = (bf16[8,4,128,1536]{3,2,1,0:T(8,128)(2,1)}, bf16[8,4,128,1536]{3,2,1,0:T(8,128)(2,1)}, bf16[4,64,1536]{2,1,0:T(8,128)(2,1)}) custom-call(bf16[2,4,128,1536]{3,2,1,0:T(8,128)(2,1)} %get-tuple-element.110.chunk_ref, f32[2,2,1536]{2,1,0:T(2,128)} %slice.216.gain_ref, ...), custom_call_target="tpu_custom_call", output_to_operand_aliasing={{0}: (4, {}), {1}: (5, {})} | custom-call | flops 4831838208 | bytes 6291456 | tf_op jit(solution)/shard_map/media_far/pallas_call | solution.py:598
  171.4 4.6 copy-done
  176.0 6.0 attend.2
  184.0 20.6 %forward_exchange.3 = (f32[4,16,1536]{2,1,0:T(8,128)S(1)}, bf16[4,64,1536]{2,1,0:T(8,128)(2,1)S(1)}) custom-call(bf16[4,64,1536]{2,1,0:T(8,128)(2,1)S(1)} %bitcast.232, f32[4,16,1536]{2,1,0:T(8,128)S(1)} %copy-done.3, f32[2,1536]{1,0:T(2,128)S(1)} %get-tuple-element.242.gain_ref), custom_call_target="tpu_custom_call" | custom-call | bytes 75000000 | tf_op jit(solution)/shard_map/forward_exchange/pallas_call | solution.py:947
  204.6 6.1 multiply_convert_fusion.1
  210.7 4.2 fusion.37
  214.9 20.8 %forward_exchange.4 = (f32[4,16,1536]{2,1,0:T(8,128)S(1)}, bf16[4,64,1536]{2,1,0:T(8,128)(2,1)S(1)}) custom-call(bf16[4,64,1536]{2,1,0:T(8,128)(2,1)S(1)} %bitcast.231, f32[4,16,1536]{2,1,0:T(8,128)S(1)} %get-tuple-element.116.rest_ref.rows_ref, f32[2,1536]{1,0:T(2,128)S(1)} %copy-done.22), custom_call_target="tpu_custom_call" | custom-call | bytes 75000000 | tf_op jit(solution)/shard_map/forward_exchange/pallas_call | solution.py:947
  240.4 6.3 attend.3
  250.9 20.4 %forward_exchange.5 = (f32[4,16,1536]{2,1,0:T(8,128)S(1)}, bf16[4,64,1536]{2,1,0:T(8,128)(2,1)S(1)}) custom-call(bf16[4,64,1536]{2,1,0:T(8,128)(2,1)S(1)} %bitcast.230, f32[4,16,1536]{2,1,0:T(8,128)S(1)} %get-tuple-element.121.rest_ref.rows_ref, f32[2,1536]{1,0:T(2,128)S(1)} %copy-done.24), custom_call_target="tpu_custom_call" | custom-call | bytes 75000000 | tf_op jit(solution)/shard_map/forward_exchange/pallas_call | solution.py:947
  271.4 16.4 %all-gather.8.cloned.1.call-done = bf16[1536,3072]{1,0:T(8,128)(2,1)} async-done(((bf16[192,3072]{1,0:T(8,128)(2,1)}), bf16[1536,3072]{1,0:T(8,128)(2,1)}) %all-gather.8.cloned.1.call-update) | async-done | bytes 9437200 | tf_op jit(solution)/shard_map/all_gather | solution.py:1564
  287.7 5.0 multiply_convert_fusion
  296.5 7.9 %feed_gradients.2 = bf16[1536,3072]{1,0:T(8,128)(2,1)} custom-call(bf16[256,1536]{1,0:T(8,128)(2,1)} %bitcast.268, bf16[256,1536]{1,0:T(8,128)(2,1)} %get-tuple-element.247.second_ref, bf16[256,1536]{1,0:T(8,128)(2,1)} %bitcast.223, bf16[256,1536]{1,0:T(8,128)(2,1)} %fusion.59.fourth_ref), custom_call_target="tpu_custom_call" | custom-call | flops 2415919104 | bytes 18874368 | tf_op jit(solution)/shard_map/feed_gradients/pallas_call | solution.py:875
  304.3 4.7 fusion.43
  310.2 23.5 %backward_exchange.3 = (f32[4,16,1536]{2,1,0:T(8,128)S(1)}, f32[2,1536]{1,0:T(2,128)S(1)}, bf16[4,64,1536]{2,1,0:T(8,128)(2,1)S(1)}) custom-call(bf16[4,64,1536]{2,1,0:T(8,128)(2,1)S(1)} %bitcast.229, f32[4,16,1536]{2,1,0:T(8,128)S(1)} %get-tuple-element.124.rows_ref.final_rest_ref, f32[4,16,1536]{2,1,0:T(8,128)S(1)} %copy-done.8, f32[2,1536]{1,0:T(2,128)S(1)} %copy-done.24), custom_call_target="tpu_custom_call" | custom-call | bytes 75000000 | tf_op jit(solution)/shard_map/backward_exchange/pallas_call | solution.py:1007
  337.1 12.3 %attend_back.2 = (bf16[256,384]{1,0:T(8,128)(2,1)}, bf16[256,768]{1,0:T(8,128)(2,1)}, bf16[8,4,128,1536]{3,2,1,0:T(8,128)(2,1)}, f32[4,1,768]{2,1,0:T(1,128)}) custom-call(s32[4,8]{1,0:T(4,128)} %copy-done.25, bf16[256,384]{1,0:T(8,128)(2,1)} %copy-done.10, bf16[256,768]{1,0:T(8,128)(2,1)} %copy-done.5, bf16[256,768]{1,0:T(8,128)(2,1)} %copy-done.5, ...), custom_call_target="tpu_custom_call" | custom-call | flops 4026531840 | bytes 12582912 | tf_op jit(solution)/shard_map/attend_back/pallas_call | solution.py:787
  354.8 21.8 %backward_exchange.4 = (f32[4,16,1536]{2,1,0:T(8,128)S(1)}, f32[2,1536]{1,0:T(2,128)S(1)}, bf16[4,64,1536]{2,1,0:T(8,128)(2,1)S(1)}) custom-call(bf16[4,64,1536]{2,1,0:T(8,128)(2,1)S(1)} %bitcast.217, f32[4,16,1536]{2,1,0:T(8,128)S(1)} %get-tuple-element.121.rest_ref.rows_ref, f32[4,16,1536]{2,1,0:T(8,128)S(1)} %copy-done.21, f32[2,1536]{1,0:T(2,128)S(1)} %copy-done.23), custom_call_target="tpu_custom_call" | custom-call | bytes 75000000 | tf_op jit(solution)/shard_map/backward_exchange/pallas_call | solution.py:1007
  380.6 14.3 %fusion.2 = f32[1536,768,1,1]{1,0,3,2:T(8,128)S(1)} fusion(bf16[8,4,128,1536]{3,2,1,0:T(8,128)(2,1)} %get-tuple-element.130, bf16[8,4,128,1536]{3,2,1,0:T(8,128)(2,1)} %get-tuple-element.131.rest_0_), kind=kOutput, calls=%fused_computation.8 | convolution fusion | flops 9663676416 | bytes 23592960 | tf_op jit(solution)/shard_map/dot_general | solution.py:378
  401.0 10.6 %feed_gradients.3 = bf16[1536,4608]{1,0:T(8,128)(2,1)} custom-call(bf16[256,1536]{1,0:T(8,128)(2,1)} %bitcast.221, bf16[256,1536]{1,0:T(8,128)(2,1)} %copy-done.38, bf16[256,1536]{1,0:T(8,128)(2,1)} %bitcast.219, bf16[256,1536]{1,0:T(8,128)(2,1)} %fusion.52.fourth_ref, bf16[1536,384]{1,0:T(8,128)(2,1)} %convolution_convert_fusion.9.rest_0_, ...), custom_call_target="tpu_custom_call" | custom-call | flops 2415919104 | bytes 18874368 | tf_op jit(solution)/shard_map/feed_gradients/pallas_call | solution.py:875
  411.7 3.8 fusion.34
  416.5 22.3 %backward_exchange.5 = (f32[4,16,1536]{2,1,0:T(8,128)S(1)}, f32[2,1536]{1,0:T(2,128)S(1)}, bf16[4,64,1536]{2,1,0:T(8,128)(2,1)S(1)}) custom-call(bf16[4,64,1536]{2,1,0:T(8,128)(2,1)S(1)} %bitcast.228, f32[4,16,1536]{2,1,0:T(8,128)S(1)} %get-tuple-element.116.rest_ref.rows_ref, f32[4,16,1536]{2,1,0:T(8,128)S(1)} %copy-done.19, ...), custom_call_target="tpu_custom_call" | custom-call | bytes 75000000 | tf_op jit(solution)/shard_map/backward_exchange/pallas_call | solution.py:1007
  442.1 11.8 %attend_back.3 = (bf16[256,384]{1,0:T(8,128)(2,1)}, bf16[256,768]{1,0:T(8,128)(2,1)}, bf16[8,4,128,1536]{3,2,1,0:T(8,128)(2,1)}, f32[4,1,768]{2,1,0:T(1,128)}) custom-call(s32[4,8]{1,0:T(4,128)} %copy-done.25, bf16[256,384]{1,0:T(8,128)(2,1)} %copy-done.9, bf16[256,768]{1,0:T(8,128)(2,1)} %copy-done.4, ...), custom_call_target="tpu_custom_call", output_to_operand_aliasing={{2}: (7, {})} | custom-call | flops 4026531840 | bytes 12582912 | tf_op jit(solution)/shard_map/attend_back/pallas_call | solution.py:787
  456.9 6.4 convolution_convert_fusion.4
  463.4 3.8 convolution_convert_fusion.5
  482.8 3.8 convolution_convert_fusion.1
  487.3 18.4 %fusion.9 = (f32[1536]{0:T(1024)S(1)}, f32[1536]{0:T(1024)S(1)}, f32[1536]{0:T(1024)S(1)}, f32[1536]{0:T(1024)S(1)}, f32[1536,768,1,1]{1,0,3,2:T(8,128)}) fusion(f32[768]{0:T(1024)S(1)} %reduce_sum.92, bf16[1536,3072]{1,0:T(8,128)(2,1)S(1)} %bitcast.238, f32[768]{0:T(1024)S(1)} %reduce_sum.93, f32[1536,768,1,1]{1,0,3,2:T(8,128)} %copy-done.28, ...), kind=kOutput, calls=%fused_computation.15 | convolution fusion | flops 9675466752 | bytes 33060864 | tf_op jit(solution)/shard_map/dot_general | solution.py:378
  514.3 4.8 fusion.40
  520.3 72.9 %last_step.1 = (bf16[192,1536]{1,0:T(8,128)(2,1)}, bf16[4,128,1536]{2,1,0:T(8,128)(2,1)}, bf16[4,128,1536]{2,1,0:T(8,128)(2,1)}, f32[4,16,1536]{2,1,0:T(8,128)},...) custom-call(bf16[4,2,192,384]{3,2,1,0:T(8,128)(2,1)} %bitcast.248, ...), custom_call_target="tpu_custom_call" | custom-call | bytes 160000000 | tf_op jit(solution)/shard_map/last_step/pallas_call | solution.py:1367
  594.1 12.0 %media_back.1 = f32[256,4,1536]{2,1,0:T(4,128)} custom-call(bf16[2,4,128,1536]{3,2,1,0:T(8,128)(2,1)} %bitcast.241, bf16[2,4,128,1536]{3,2,1,0:T(8,128)(2,1)} %get-tuple-element.158.back_ref, bf16[4,128,1536]{2,1,0:T(8,128)(2,1)} %collective-permute-done.2.refs_0_, bf16[4,128,1536]{2,1,0:T(8,128)(2,1)} %get-tuple-element.160.refs_1_, ...), custom_call_target="tpu_custom_call" | custom-call | bytes 30000000 | tf_op jit(solution)/shard_map/media_back/pallas_call | solution.py:1440
  607.6 16.1 %sum_over_all.1 = f32[4,40,128]{2,1,0:T(8,128)S(1)} custom-call(f32[4,40,128]{2,1,0:T(8,128)S(1)} %pad.4.term_in, bf16[192,3072]{1,0:T(8,128)(2,1)S(1)} %copy-done.2, bf16[192,4608]{1,0:T(8,128)(2,1)S(1)} %copy-done.1, bf16[192,1536]{1,0:T(8,128)(2,1)S(1)} %copy-done.6), custom_call_target="tpu_custom_call" | custom-call | bytes 40000000 | tf_op jit(solution)/shard_map/sum_over_all/pallas_call | solution.py:1083
  629.2 23.0 %adam.1 = (f32[2,3,192,384]{3,2,1,0:T(8,128)}, f32[2,3,192,384]{3,2,1,0:T(8,128)}, f32[2,3,192,384]{3,2,1,0:T(8,128)}, bf16[2,3,192,384]{3,2,1,0:T(8,128)(2,1)},...) custom-call(f32[1,1]{1,0:T(1,128)} %bitcast.65.factor_ref, ...), custom_call_target="tpu_custom_call" | custom-call | flops 35389440 | bytes 49545216 | tf_op jit(solution)/shard_map/adam/pallas_call | solution.py:1512
  (260 shorter events, 99.7 us)
Async XLA Ops:
  7.2 102.4 %all-gather.4.cloned.1.call-start = ((), (), s32[]{:S(2)}) async-start(), calls=%async_computation.2 | async-start | bytes 10616832 | tf_op jit(solution)/shard_map/all_gather | solution.py:1564
  11.3 193.4 %all-gather.6.cloned.1.call-start = ((), (), s32[]{:S(2)}) async-start(), calls=%async_computation.3 | async-start | bytes 10616832 | tf_op jit(solution)/shard_map/all_gather | solution.py:1564
  20.0 267.8 %all-gather.8.cloned.1.call-start = ((), (), s32[]{:S(2)}) async-start(), calls=%async_computation.4 | async-start | bytes 10616832 | tf_op jit(solution)/shard_map/all_gather | solution.py:1564
  20.7 394.8 %reduce-scatter.3.cloned.1.call-start = ((), (), s32[]{:S(2)}) async-start(), calls=%async_computation.5 | async-start | bytes 10616832 | tf_op jit(solution)/shard_map/reduce_scatter | solution.py:1644
  25.9 82.9 %copy-start.54 = (s32[4]{0:T(128)S(1)}, s32[4]{0:T(128)}, u32[]{:S(2)}) copy-start(s32[4]{0:T(128)} %param.21) | copy-start | bytes 52
  108.9 131.4 %copy-start.25 = (s32[4,8]{1,0:T(4,128)}, s32[4,8]{1,0:T(4,128)S(1)}, u32[]{:S(2)}) copy-start(s32[4,8]{1,0:T(4,128)S(1)} %compare_convert_fusion.live_ref) | copy-start | bytes 388
  111.6 59.7 %copy-start.9 = (bf16[256,384]{1,0:T(8,128)(2,1)}, bf16[256,384]{1,0:T(8,128)(2,1)S(1)}, u32[]{:S(2)}) copy-start(bf16[256,384]{1,0:T(8,128)(2,1)S(1)} %convolution_convert_fusion.17.query_ref) | copy-start | bytes 589828
  114.4 56.9 %copy-start.4 = (bf16[256,768]{1,0:T(8,128)(2,1)}, bf16[256,768]{1,0:T(8,128)(2,1)S(1)}, u32[]{:S(2)}) copy-start(bf16[256,768]{1,0:T(8,128)(2,1)S(1)} %convolution_convert_fusion.13.latent_key_ref.latent_value_ref) | copy-start | bytes 1179652
  182.0 22.5 %copy-start.11 = (bf16[256,384]{1,0:T(8,128)(2,1)}, bf16[256,384]{1,0:T(8,128)(2,1)S(1)}, u32[]{:S(2)}) copy-start(bf16[256,384]{1,0:T(8,128)(2,1)S(1)} %attend.2) | copy-start | bytes 589828
  204.6 35.7 %slice-start = ((s8[12582912]{0:T(1024)(128)(4,1)}), s8[4194304]{0:T(1024)(128)(4,1)S(1)}, s32[]{:S(2)}) async-start(s8[12582912]{0:T(1024)(128)(4,1)} %bitcast.211), calls=%async_computation.7 | async-start | bytes 8388608
  204.6 35.7 %slice-start.1 = ((s8[12582912]{0:T(1024)(128)(4,1)}), s8[4194304]{0:T(1024)(128)(4,1)S(1)}, s32[]{:S(2)}) async-start(s8[12582912]{0:T(1024)(128)(4,1)} %bitcast.211), calls=%async_computation.8 | async-start | bytes 8388608
  210.7 29.6 %slice-start.2 = ((s8[12582912]{0:T(1024)(128)(4,1)}), s8[4194304]{0:T(1024)(128)(4,1)S(1)}, s32[]{:S(2)}) async-start(s8[12582912]{0:T(1024)(128)(4,1)} %bitcast.211), calls=%async_computation.9 | async-start | bytes 8388608
  271.3 21.4 %copy-start.15 = (bf16[4,64,1536]{2,1,0:T(8,128)(2,1)}, bf16[4,64,1536]{2,1,0:T(8,128)(2,1)S(1)}, u32[]{:S(2)}) copy-start(bf16[4,64,1536]{2,1,0:T(8,128)(2,1)S(1)} %get-tuple-element.122) | copy-start | bytes 2359300
  271.3 37.7 %copy-start.7 = (f32[4,16,1536]{2,1,0:T(8,128)}, f32[4,16,1536]{2,1,0:T(8,128)S(1)}, u32[]{:S(2)}) copy-start(f32[4,16,1536]{2,1,0:T(8,128)S(1)} %get-tuple-element.124.rows_ref.final_rest_ref) | copy-start | bytes 1179652
  309.0 297.1 %reduce-scatter.5.cloned.1.call-start = ((), (), s32[]{:S(2)}) async-start(), calls=%async_computation.6 | async-start | bytes 15925248 | tf_op jit(solution)/shard_map/reduce_scatter | solution.py:1644
  354.8 24.2 %copy-start.44 = (bf16[256,384]{1,0:T(8,128)(2,1)S(1)}, bf16[256,384]{1,0:T(8,128)(2,1)}, u32[]{:S(2)}) copy-start(bf16[256,384]{1,0:T(8,128)(2,1)} %get-tuple-element.126) | copy-start | bytes 589828
  377.4 20.6 %copy-start.14 = (bf16[4,64,1536]{2,1,0:T(8,128)(2,1)}, bf16[4,64,1536]{2,1,0:T(8,128)(2,1)S(1)}, u32[]{:S(2)}) copy-start(bf16[4,64,1536]{2,1,0:T(8,128)(2,1)S(1)} %get-tuple-element.129) | copy-start | bytes 2359300
  377.4 20.6 %slice-start.14 = ((s8[9437184]{0:T(1024)(128)(4,1)}), s8[4194304]{0:T(1024)(128)(4,1)S(1)}, s32[]{:S(2)}) async-start(s8[9437184]{0:T(1024)(128)(4,1)} %bitcast.273), calls=%async_computation.21 | async-start | bytes 8388608
  380.6 14.4 %copy-start.36 = (bf16[256,768]{1,0:T(8,128)(2,1)S(1)}, bf16[256,768]{1,0:T(8,128)(2,1)}, u32[]{:S(2)}) copy-start(bf16[256,768]{1,0:T(8,128)(2,1)} %get-tuple-element.127) | copy-start | bytes 1179652
  380.6 17.3 %slice-start.15 = ((s8[9437184]{0:T(1024)(128)(4,1)}), s8[4194304]{0:T(1024)(128)(4,1)S(1)}, s32[]{:S(2)}) async-start(s8[9437184]{0:T(1024)(128)(4,1)} %bitcast.273), calls=%async_computation.22 | async-start | bytes 8388608
  380.6 17.3 %slice-start.16 = ((s8[9437184]{0:T(1024)(128)(4,1)}), s8[1048576]{0:T(1024)(128)(4,1)S(1)}, s32[]{:S(2)}) async-start(s8[9437184]{0:T(1024)(128)(4,1)} %bitcast.273), calls=%async_computation.23 | async-start | bytes 2097152
  456.9 12.3 %slice-start.3 = ((s8[12582912]{0:T(1024)(128)(4,1)}), s8[4194304]{0:T(1024)(128)(4,1)S(1)}, s32[]{:S(2)}) async-start(s8[12582912]{0:T(1024)(128)(4,1)} %bitcast.233), calls=%async_computation.10 | async-start | bytes 8388608
  467.1 52.0 %collective-permute-start = (bf16[4,128,1536]{2,1,0:T(8,128)(2,1)}, bf16[4,128,1536]{2,1,0:T(8,128)(2,1)S(1)}, u32[]{:S(2)}, u32[]{:S(2)}) collective-permute-start(bf16[4,128,1536]{2,1,0:T(8,128)(2,1)} %bitcast.44), channel_id=1, source_target_pairs={{0,1},{1,0},{2,3},{3,2},{4,5},{5,4},{6,7},{7,6},{8,9},{9,8},{10,11... | collective-permute-start | bytes 4718600 | tf_op jit(solution)/shard_map/ppermute | solution.py:1558
  468.7 50.5 %collective-permute-start.1 = (bf16[4,128,1536]{2,1,0:T(8,128)(2,1)}, bf16[4,128,1536]{2,1,0:T(8,128)(2,1)}, u32[]{:S(2)}, u32[]{:S(2)}) collective-permute-start(bf16[4,128,1536]{2,1,0:T(8,128)(2,1)} %bitcast.46), channel_id=1, source_target_pairs={{0,2},{2,0},{1,3},{3,1},{4,6},{6,4},{5,7},{7,5},{8,10},{10,8},{9,1... | collective-permute-start | bytes 4718600 | tf_op jit(solution)/shard_map/ppermute | solution.py:1561
  476.9 117.2 %collective-permute-start.2 = (bf16[4,128,1536]{2,1,0:T(8,128)(2,1)}, bf16[4,128,1536]{2,1,0:T(8,128)(2,1)}, u32[]{:S(2)}, u32[]{:S(2)}) collective-permute-start(bf16[4,128,1536]{2,1,0:T(8,128)(2,1)} %bitcast.48), channel_id=1, source_target_pairs={{0,1},{1,0},{2,3},{3,2},{4,5},{5,4},{6,7},{7,6},{8,9},{9,8},{10,11... | collective-permute-start | bytes 4718600 | tf_op jit(solution)/shard_map/ppermute | solution.py:1558
  477.4 116.7 %collective-permute-start.3 = (bf16[4,128,1536]{2,1,0:T(8,128)(2,1)}, bf16[4,128,1536]{2,1,0:T(8,128)(2,1)}, u32[]{:S(2)}, u32[]{:S(2)}) collective-permute-start(bf16[4,128,1536]{2,1,0:T(8,128)(2,1)} %bitcast.50), channel_id=1, source_target_pairs={{0,2},{2,0},{1,3},{3,1},{4,6},{6,4},{5,7},{7,5},{8,10},{10,8},{9,1... | collective-permute-start | bytes 4718600 | tf_op jit(solution)/shard_map/ppermute | solution.py:1561
  487.3 18.4 %copy-start.12 = (bf16[256,384]{1,0:T(8,128)(2,1)S(1)}, bf16[256,384]{1,0:T(8,128)(2,1)}, u32[]{:S(2)}) copy-start(bf16[256,384]{1,0:T(8,128)(2,1)} %copy-done.11) | copy-start | bytes 589828
  607.6 18.8 %copy-start.47 = (f32[12,1536]{1,0:T(8,128)S(1)}, f32[12,1536]{1,0:T(8,128)}, u32[]{:S(2)}) copy-start(f32[12,1536]{1,0:T(8,128)} %reshape.207) | copy-start | bytes 221188
  607.6 18.8 %copy-start.48 = (f32[12,1536]{1,0:T(8,128)S(1)}, f32[12,1536]{1,0:T(8,128)}, u32[]{:S(2)}) copy-start(f32[12,1536]{1,0:T(8,128)} %reshape.208) | copy-start | bytes 221188
  607.6 18.8 %copy-start.49 = (f32[12,1536]{1,0:T(8,128)S(1)}, f32[12,1536]{1,0:T(8,128)}, u32[]{:S(2)}) copy-start(f32[12,1536]{1,0:T(8,128)} %reshape.209) | copy-start | bytes 221188
  629.2 23.1 %copy-start.46 = (f32[4,16,1536]{2,1,0:T(8,128)S(1)}, f32[4,16,1536]{2,1,0:T(8,128)}, u32[]{:S(2)}) copy-start(f32[4,16,1536]{2,1,0:T(8,128)} %get-tuple-element.276) | copy-start | bytes 1179652
  629.2 23.8 %copy-start.45 = (f32[4,16,1536]{2,1,0:T(8,128)S(1)}, f32[4,16,1536]{2,1,0:T(8,128)}, u32[]{:S(2)}) copy-start(f32[4,16,1536]{2,1,0:T(8,128)} %get-tuple-element.277) | copy-start | bytes 1179652
  (51 other events, 217.0 us)
Sparse Core Ops, SparseCore 0:
  11.4 93.4 all-gather.3
  107.1 89.1 all-gather.5
  198.5 89.1 all-gather.7
  309.2 97.9 reduce-scatter.2
  415.7 166.1 reduce-scatter.4

commit v5 on v4

--- a/solution.py
+++ b/solution.py
@@ -811,85 +811,29 @@
     )(live, query, latent_pair, latent_pair, keys, keys, slope, *earlier)
 
 
-def product_pair_kernel(begin, first_ref, second_ref, third_ref, fourth_ref, *rest):
-    step = pl.program_id(0)
-    count = len(rest) - 5
-    extra, (out_ref, tile_ref, extra_ref, tile_sem, extra_sem) = rest[:count], rest[count:]
-    cut, half = tile_ref.shape[2], pl.num_programs(0) // 2
-
-    def moves():
-        at = 0
-        for number, ref in enumerate(extra):
-            lines = pl.ds(at, ref.shape[1])
-            yield pltpu.make_async_copy(ref, extra_ref.at[:, lines], extra_sem.at[number])
-            at += ref.shape[1]
-
-    def store(at):
-        lines = pl.ds(pl.multiple_of(begin + at * cut, 128), cut)
-        return pltpu.make_async_copy(tile_ref.at[at % 2], out_ref.at[:, lines], tile_sem.at[at % 2])
-
-    def store_extra():
-        return pltpu.make_async_copy(extra_ref, out_ref.at[:, pl.ds(0, begin)], extra_sem.at[count])
-
-    if count:
-
-        @pl.when(step == 0)
-        def _():
-            for copy in moves():
-                copy.start()
-
-        @pl.when(step == 2)
-        def _():
-            for copy in moves():
-                copy.wait()
-            store_extra().start()
-
-    @pl.when(step >= 2)
-    def _():
-        store(step - 2).wait()
-
-    @pl.when(step < half)
-    def _():
-        tile_ref[step % 2] = mm(first_ref[...], second_ref[...], TN)
-
-    @pl.when(step >= half)
-    def _():
-        tile_ref[step % 2] = mm(third_ref[...], fourth_ref[...], TN)
-
-    store(step).start()
-
-    @pl.when(step == 2 * half - 1)
-    def _():
-        store(step - 1).wait()
-        store(step).wait()
-        if count:
-            store_extra().wait()
+def product_pair_kernel(first_ref, second_ref, third_ref, fourth_ref, *rest):
+    out_ref, at = rest[-1], 0
+    for ref in rest[:-1]:
+        out_ref[:, at : at + ref.shape[1]] = ref[...]
+        at += ref.shape[1]
+    units = second_ref.shape[1]
+    out_ref[:, at : at + units] = mm(first_ref[...], second_ref[...], TN)
+    out_ref[:, at + units :] = mm(third_ref[...], fourth_ref[...], TN)
 
 
 def product_pair(first, second, third, fourth, *extra):
     rows, width, columns = first.shape[0], first.shape[1], second.shape[1]
-    cut = columns // 3
-    begin = sum(piece.shape[1] for piece in extra)
-    left = pl.BlockSpec((rows, width), lambda i: (0, 0))
-    any_spec = pl.BlockSpec(memory_space=pl.ANY)
+    cut = width // 6
+    total = sum(piece.shape[1] for piece in extra) + 2 * columns
+    left = pl.BlockSpec((rows, cut), lambda i: (0, i))
+    whole = pl.BlockSpec((rows, columns), lambda i: (0, 0))
     return pl.pallas_call(
-        functools.partial(product_pair_kernel, begin),
+        product_pair_kernel,
         grid=(6,),
-        out_shape=jax.ShapeDtypeStruct((width, begin + 2 * columns), BF),
-        in_specs=[
-            left,
-            pl.BlockSpec((rows, cut), lambda i: (0, jnp.minimum(i, 2))),
-            left,
-            pl.BlockSpec((rows, cut), lambda i: (0, jnp.maximum(i - 3, 0))),
-        ]
-        + [any_spec] * len(extra),
-        out_specs=any_spec,
-        scratch_shapes=[
-            pltpu.VMEM((2, width, cut), BF),
-            pltpu.VMEM((width, max(begin, 128)), BF),
-            pltpu.SemaphoreType.DMA((2,)),
-            pltpu.SemaphoreType.DMA((4,)),
-        ],
+        out_shape=jax.ShapeDtypeStruct((width, total), BF),
+        in_specs=[left, whole, left, whole]
+        + [pl.BlockSpec((cut, piece.shape[1]), lambda i: (i, 0)) for piece in extra],
+        out_specs=pl.BlockSpec((cut, total), lambda i: (i, 0)),
         compiler_params=pltpu.CompilerParams(vmem_limit_bytes=60 * MIB),
         cost_estimate=pl.CostEstimate(
             flops=4 * rows * width * columns, bytes_accessed=8 * width * columns, transcendentals=0
@@ -1432,7 +1376,7 @@
 
 def media_back(own, back, in_x, in_y):
     _, videos, rows, width = own.shape
-    cut = 32
+    cut = 64
     steps = rows // cut
     both = pl.BlockSpec((1, videos, cut, width), lambda i, j: (i, 0, j, 0))
     specs = [pl.BlockSpec((videos, cut, width), lambda i, j: (0, jnp.where(i == 0, j, steps - 1), 0))] * 2
@@ -1734,7 +1678,7 @@
             (
                 *(inward, inward_first, inward_second),
                 [(late_share, 0), (middle_share, 0)],
-                *(depth // 2, RATE_INWARD),
+                *(depth, RATE_INWARD),
             ),
             (
                 *turned(outward, outward_first, outward_second),

time: 667 us -> 665 us (level)
  no operation moved by 1% of the time
where the time goes in v5:
time: 665 us; the launch traced here: 660 us
  Pallas kernels  447 us (67%)
  matrix products  128 us (19%)
  local copies, waits for them, and re-layouts  33.4 us (5%)
  between operations  17.9 us (3%)
  waiting for transfers between devices  16.9 us (3%)
  other arithmetic  12.9 us (2%)
    dot_general x34, matrix products, mm(): lax.dot_general(left, right, dims, preferred_element_type=F32).astype(out)  128 us
    pallas_call x1, Pallas kernels, gather_near(): pl.pallas_call(functools.partial(gather_kernel, count), out_shape=(jax.Sh...  82.8 us
    pallas_call x1, Pallas kernels, last_step(): pl.pallas_call(functools.partial(last_kernel, chips, heads), out_shape=(j...  73.2 us
    pallas_call x3, Pallas kernels, backward_exchange(): pl.pallas_call(functools.partial(backward_kernel, count, last), out_shape...  67.4 us
    pallas_call x3, Pallas kernels, forward_exchange(): pl.pallas_call(functools.partial(forward_kernel, count, last), out_shape=...  61.8 us
    pallas_call x1, Pallas kernels, media_near(): pl.pallas_call(functools.partial(near_kernel, count), grid=(6, 2), out_sh...  41.6 us
    pallas_call x2, Pallas kernels, attend_back_fast(): pl.pallas_call(functools.partial(attend_back_kernel, scale=scale), grid=(...  23.7 us
    unnamed x163, local copies, waits for them, and re-layouts  22.8 us
  transfers between devices with their start and end apart: 9, of which 1 were waited for; matrix products, arithmetic and copies ran while one was open for 20% of the time, Pallas kernels for 61%

profile of v5, /device:TPU:0, one launch (start us, length us, event | category | flops | bytes accessed | tf_op | source)
XLA Modules:
  0.0 660.0 jit_solution(11903613441216692015)
XLA Ops:
  25.9 82.8 %gather_near.1 = (bf16[4,4,128,1536]{3,2,1,0:T(8,128)(2,1)}, bf16[4,64,1536]{2,1,0:T(8,128)(2,1)}) custom-call(bf16[2,4,128,1536]{3,2,1,0:T(8,128)(2,1)} %bitcast.239, bf16[4,16,1536]{2,1,0:T(8,128)(2,1)} %add_convert_fusion.norm_ref), custom_call_target="tpu_custom_call" | custom-call | bytes 250000000 | tf_op jit(solution)/shard_map/gather_near/pallas_call | solution.py:438
  114.4 41.6 %media_near.1 = (bf16[8,4,128,1536]{3,2,1,0:T(8,128)(2,1)}, bf16[8,4,128,1536]{3,2,1,0:T(8,128)(2,1)}, bf16[2,4,128,1536]{3,2,1,0:T(8,128)(2,1)}) custom-call(bf16[2,4,128,1536]{3,2,1,0:T(8,128)(2,1)} %bitcast.240, bf16[4,4,128,1536]{3,2,1,0:T(8,128)(2,1)} %get-tuple-element.109.near_ref.source_ref, f32[2,2,1536]{2,1,0:T(2,128)} %slice.216.gain_ref, ...), custom_call_target="tpu_custom_call" | custom-call | flops 14495514624 | bytes 18874368 | tf_op jit(solution)/shard_map/media_near/pallas_call | solution.py:523
  156.1 15.3 %media_far.1 = (bf16[8,4,128,1536]{3,2,1,0:T(8,128)(2,1)}, bf16[8,4,128,1536]{3,2,1,0:T(8,128)(2,1)}, bf16[4,64,1536]{2,1,0:T(8,128)(2,1)}) custom-call(bf16[2,4,128,1536]{3,2,1,0:T(8,128)(2,1)} %get-tuple-element.110.chunk_ref, f32[2,2,1536]{2,1,0:T(2,128)} %slice.216.gain_ref, ...), custom_call_target="tpu_custom_call", output_to_operand_aliasing={{0}: (4, {}), {1}: (5, {})} | custom-call | flops 4831838208 | bytes 6291456 | tf_op jit(solution)/shard_map/media_far/pallas_call | solution.py:598
  171.4 4.6 copy-done
  176.0 6.0 attend.2
  184.0 20.6 %forward_exchange.3 = (f32[4,16,1536]{2,1,0:T(8,128)S(1)}, bf16[4,64,1536]{2,1,0:T(8,128)(2,1)S(1)}) custom-call(bf16[4,64,1536]{2,1,0:T(8,128)(2,1)S(1)} %bitcast.232, f32[4,16,1536]{2,1,0:T(8,128)S(1)} %copy-done.3, f32[2,1536]{1,0:T(2,128)S(1)} %get-tuple-element.242.gain_ref), custom_call_target="tpu_custom_call" | custom-call | bytes 75000000 | tf_op jit(solution)/shard_map/forward_exchange/pallas_call | solution.py:891
  204.6 6.1 multiply_convert_fusion.1
  210.7 4.2 fusion.37
  214.9 20.8 %forward_exchange.4 = (f32[4,16,1536]{2,1,0:T(8,128)S(1)}, bf16[4,64,1536]{2,1,0:T(8,128)(2,1)S(1)}) custom-call(bf16[4,64,1536]{2,1,0:T(8,128)(2,1)S(1)} %bitcast.231, f32[4,16,1536]{2,1,0:T(8,128)S(1)} %get-tuple-element.116.rest_ref.rows_ref, f32[2,1536]{1,0:T(2,128)S(1)} %copy-done.22), custom_call_target="tpu_custom_call" | custom-call | bytes 75000000 | tf_op jit(solution)/shard_map/forward_exchange/pallas_call | solution.py:891
  240.4 6.5 attend.3
  251.2 20.4 %forward_exchange.5 = (f32[4,16,1536]{2,1,0:T(8,128)S(1)}, bf16[4,64,1536]{2,1,0:T(8,128)(2,1)S(1)}) custom-call(bf16[4,64,1536]{2,1,0:T(8,128)(2,1)S(1)} %bitcast.230, f32[4,16,1536]{2,1,0:T(8,128)S(1)} %get-tuple-element.121.rest_ref.rows_ref, f32[2,1536]{1,0:T(2,128)S(1)} %copy-done.24), custom_call_target="tpu_custom_call" | custom-call | bytes 75000000 | tf_op jit(solution)/shard_map/forward_exchange/pallas_call | solution.py:891
  271.7 16.1 %all-gather.8.cloned.1.call-done = bf16[1536,3072]{1,0:T(8,128)(2,1)} async-done(((bf16[192,3072]{1,0:T(8,128)(2,1)}), bf16[1536,3072]{1,0:T(8,128)(2,1)}) %all-gather.8.cloned.1.call-update) | async-done | bytes 9437200 | tf_op jit(solution)/shard_map/all_gather | solution.py:1508
  287.7 5.0 multiply_convert_fusion
  296.5 8.3 %feed_gradients.2 = bf16[1536,3072]{1,0:T(8,128)(2,1)} custom-call(bf16[256,1536]{1,0:T(8,128)(2,1)} %bitcast.268, bf16[256,1536]{1,0:T(8,128)(2,1)} %get-tuple-element.247.second_ref, bf16[256,1536]{1,0:T(8,128)(2,1)} %bitcast.223, bf16[256,1536]{1,0:T(8,128)(2,1)} %fusion.59.fourth_ref), custom_call_target="tpu_custom_call" | custom-call | flops 2415919104 | bytes 18874368 | tf_op jit(solution)/shard_map/feed_gradients/pallas_call | solution.py:830
  304.7 4.7 fusion.43
  310.6 23.6 %backward_exchange.3 = (f32[4,16,1536]{2,1,0:T(8,128)S(1)}, f32[2,1536]{1,0:T(2,128)S(1)}, bf16[4,64,1536]{2,1,0:T(8,128)(2,1)S(1)}) custom-call(bf16[4,64,1536]{2,1,0:T(8,128)(2,1)S(1)} %bitcast.229, f32[4,16,1536]{2,1,0:T(8,128)S(1)} %get-tuple-element.124.rows_ref.final_rest_ref, f32[4,16,1536]{2,1,0:T(8,128)S(1)} %copy-done.8, f32[2,1536]{1,0:T(2,128)S(1)} %copy-done.24), custom_call_target="tpu_custom_call" | custom-call | bytes 75000000 | tf_op jit(solution)/shard_map/backward_exchange/pallas_call | solution.py:951
  337.5 11.9 %attend_back.2 = (bf16[256,384]{1,0:T(8,128)(2,1)}, bf16[256,768]{1,0:T(8,128)(2,1)}, bf16[8,4,128,1536]{3,2,1,0:T(8,128)(2,1)}, f32[4,1,768]{2,1,0:T(1,128)}) custom-call(s32[4,8]{1,0:T(4,128)} %copy-done.25, bf16[256,384]{1,0:T(8,128)(2,1)} %copy-done.10, bf16[256,768]{1,0:T(8,128)(2,1)} %copy-done.5, bf16[256,768]{1,0:T(8,128)(2,1)} %copy-done.5, ...), custom_call_target="tpu_custom_call" | custom-call | flops 4026531840 | bytes 12582912 | tf_op jit(solution)/shard_map/attend_back/pallas_call | solution.py:787
  354.8 21.8 %backward_exchange.4 = (f32[4,16,1536]{2,1,0:T(8,128)S(1)}, f32[2,1536]{1,0:T(2,128)S(1)}, bf16[4,64,1536]{2,1,0:T(8,128)(2,1)S(1)}) custom-call(bf16[4,64,1536]{2,1,0:T(8,128)(2,1)S(1)} %bitcast.217, f32[4,16,1536]{2,1,0:T(8,128)S(1)} %get-tuple-element.121.rest_ref.rows_ref, f32[4,16,1536]{2,1,0:T(8,128)S(1)} %copy-done.21, f32[2,1536]{1,0:T(2,128)S(1)} %copy-done.23), custom_call_target="tpu_custom_call" | custom-call | bytes 75000000 | tf_op jit(solution)/shard_map/backward_exchange/pallas_call | solution.py:951
  380.6 14.3 %fusion.2 = f32[1536,768,1,1]{1,0,3,2:T(8,128)S(1)} fusion(bf16[8,4,128,1536]{3,2,1,0:T(8,128)(2,1)} %get-tuple-element.130, bf16[8,4,128,1536]{3,2,1,0:T(8,128)(2,1)} %get-tuple-element.131.rest_0_), kind=kOutput, calls=%fused_computation.8 | convolution fusion | flops 9663676416 | bytes 23592960 | tf_op jit(solution)/shard_map/dot_general | solution.py:378
  401.0 10.9 %feed_gradients.3 = bf16[1536,4608]{1,0:T(8,128)(2,1)} custom-call(bf16[256,1536]{1,0:T(8,128)(2,1)} %bitcast.221, bf16[256,1536]{1,0:T(8,128)(2,1)} %copy-done.38, bf16[256,1536]{1,0:T(8,128)(2,1)} %bitcast.219, bf16[256,1536]{1,0:T(8,128)(2,1)} %fusion.52.fourth_ref, bf16[1536,384]{1,0:T(8,128)(2,1)} %convolution_convert_fusion.9.rest_0_, ...), custom_call_target="tpu_custom_call" | custom-call | flops 2415919104 | bytes 18874368 | tf_op jit(solution)/shard_map/feed_gradients/pallas_call | solution.py:830
  416.7 22.1 %backward_exchange.5 = (f32[4,16,1536]{2,1,0:T(8,128)S(1)}, f32[2,1536]{1,0:T(2,128)S(1)}, bf16[4,64,1536]{2,1,0:T(8,128)(2,1)S(1)}) custom-call(bf16[4,64,1536]{2,1,0:T(8,128)(2,1)S(1)} %bitcast.228, f32[4,16,1536]{2,1,0:T(8,128)S(1)} %get-tuple-element.116.rest_ref.rows_ref, f32[4,16,1536]{2,1,0:T(8,128)S(1)} %copy-done.19, ...), custom_call_target="tpu_custom_call" | custom-call | bytes 75000000 | tf_op jit(solution)/shard_map/backward_exchange/pallas_call | solution.py:951
  442.0 11.8 %attend_back.3 = (bf16[256,384]{1,0:T(8,128)(2,1)}, bf16[256,768]{1,0:T(8,128)(2,1)}, bf16[8,4,128,1536]{3,2,1,0:T(8,128)(2,1)}, f32[4,1,768]{2,1,0:T(1,128)}) custom-call(s32[4,8]{1,0:T(4,128)} %copy-done.25, bf16[256,384]{1,0:T(8,128)(2,1)} %copy-done.9, bf16[256,768]{1,0:T(8,128)(2,1)} %copy-done.4, ...), custom_call_target="tpu_custom_call", output_to_operand_aliasing={{2}: (7, {})} | custom-call | flops 4026531840 | bytes 12582912 | tf_op jit(solution)/shard_map/attend_back/pallas_call | solution.py:787
  456.9 6.4 convolution_convert_fusion.4
  463.3 3.8 convolution_convert_fusion.5
  469.5 3.8 convolution_convert_fusion.2
  482.8 3.8 convolution_convert_fusion.1
  487.2 18.4 %fusion.9 = (f32[1536]{0:T(1024)S(1)}, f32[1536]{0:T(1024)S(1)}, f32[1536]{0:T(1024)S(1)}, f32[1536]{0:T(1024)S(1)}, f32[1536,768,1,1]{1,0,3,2:T(8,128)}) fusion(f32[768]{0:T(1024)S(1)} %reduce_sum.92, bf16[1536,3072]{1,0:T(8,128)(2,1)S(1)} %bitcast.238, f32[768]{0:T(1024)S(1)} %reduce_sum.93, f32[1536,768,1,1]{1,0,3,2:T(8,128)} %copy-done.28, ...), kind=kOutput, calls=%fused_computation.15 | convolution fusion | flops 9675466752 | bytes 33060864 | tf_op jit(solution)/shard_map/dot_general | solution.py:378
  514.2 4.8 fusion.40
  520.2 73.2 %last_step.1 = (bf16[192,1536]{1,0:T(8,128)(2,1)}, bf16[4,128,1536]{2,1,0:T(8,128)(2,1)}, bf16[4,128,1536]{2,1,0:T(8,128)(2,1)}, f32[4,16,1536]{2,1,0:T(8,128)},...) custom-call(bf16[4,2,192,384]{3,2,1,0:T(8,128)(2,1)} %bitcast.248, ...), custom_call_target="tpu_custom_call" | custom-call | bytes 160000000 | tf_op jit(solution)/shard_map/last_step/pallas_call | solution.py:1311
  594.3 10.8 %media_back.1 = f32[256,4,1536]{2,1,0:T(4,128)} custom-call(bf16[2,4,128,1536]{3,2,1,0:T(8,128)(2,1)} %bitcast.241, bf16[2,4,128,1536]{3,2,1,0:T(8,128)(2,1)} %get-tuple-element.158.back_ref, bf16[4,128,1536]{2,1,0:T(8,128)(2,1)} %collective-permute-done.2.refs_0_, bf16[4,128,1536]{2,1,0:T(8,128)(2,1)} %get-tuple-element.160.refs_1_, ...), custom_call_target="tpu_custom_call" | custom-call | bytes 30000000 | tf_op jit(solution)/shard_map/media_back/pallas_call | solution.py:1384
  606.6 16.1 %sum_over_all.1 = f32[4,40,128]{2,1,0:T(8,128)S(1)} custom-call(f32[4,40,128]{2,1,0:T(8,128)S(1)} %pad.4.term_in, bf16[192,3072]{1,0:T(8,128)(2,1)S(1)} %copy-done.2, bf16[192,4608]{1,0:T(8,128)(2,1)S(1)} %copy-done.1, bf16[192,1536]{1,0:T(8,128)(2,1)S(1)} %copy-done.6), custom_call_target="tpu_custom_call" | custom-call | bytes 40000000 | tf_op jit(solution)/shard_map/sum_over_all/pallas_call | solution.py:1027
  628.2 22.2 %adam.1 = (f32[2,3,192,384]{3,2,1,0:T(8,128)}, f32[2,3,192,384]{3,2,1,0:T(8,128)}, f32[2,3,192,384]{3,2,1,0:T(8,128)}, bf16[2,3,192,384]{3,2,1,0:T(8,128)(2,1)},...) custom-call(f32[1,1]{1,0:T(1,128)} %bitcast.65.factor_ref, ...), custom_call_target="tpu_custom_call" | custom-call | flops 35389440 | bytes 49545216 | tf_op jit(solution)/shard_map/adam/pallas_call | solution.py:1456
  (260 shorter events, 99.8 us)
Async XLA Ops:
  7.2 102.4 %all-gather.4.cloned.1.call-start = ((), (), s32[]{:S(2)}) async-start(), calls=%async_computation.2 | async-start | bytes 10616832 | tf_op jit(solution)/shard_map/all_gather | solution.py:1508
  11.3 193.4 %all-gather.6.cloned.1.call-start = ((), (), s32[]{:S(2)}) async-start(), calls=%async_computation.3 | async-start | bytes 10616832 | tf_op jit(solution)/shard_map/all_gather | solution.py:1508
  20.0 267.8 %all-gather.8.cloned.1.call-start = ((), (), s32[]{:S(2)}) async-start(), calls=%async_computation.4 | async-start | bytes 10616832 | tf_op jit(solution)/shard_map/all_gather | solution.py:1508
  20.7 395.0 %reduce-scatter.3.cloned.1.call-start = ((), (), s32[]{:S(2)}) async-start(), calls=%async_computation.5 | async-start | bytes 10616832 | tf_op jit(solution)/shard_map/reduce_scatter | solution.py:1588
  25.9 82.9 %copy-start.54 = (s32[4]{0:T(128)S(1)}, s32[4]{0:T(128)}, u32[]{:S(2)}) copy-start(s32[4]{0:T(128)} %param.21) | copy-start | bytes 52
  108.9 131.4 %copy-start.25 = (s32[4,8]{1,0:T(4,128)}, s32[4,8]{1,0:T(4,128)S(1)}, u32[]{:S(2)}) copy-start(s32[4,8]{1,0:T(4,128)S(1)} %compare_convert_fusion.live_ref) | copy-start | bytes 388
  111.6 59.7 %copy-start.9 = (bf16[256,384]{1,0:T(8,128)(2,1)}, bf16[256,384]{1,0:T(8,128)(2,1)S(1)}, u32[]{:S(2)}) copy-start(bf16[256,384]{1,0:T(8,128)(2,1)S(1)} %convolution_convert_fusion.17.query_ref) | copy-start | bytes 589828
  114.4 56.9 %copy-start.4 = (bf16[256,768]{1,0:T(8,128)(2,1)}, bf16[256,768]{1,0:T(8,128)(2,1)S(1)}, u32[]{:S(2)}) copy-start(bf16[256,768]{1,0:T(8,128)(2,1)S(1)} %convolution_convert_fusion.13.latent_key_ref.latent_value_ref) | copy-start | bytes 1179652
  182.0 22.5 %copy-start.11 = (bf16[256,384]{1,0:T(8,128)(2,1)}, bf16[256,384]{1,0:T(8,128)(2,1)S(1)}, u32[]{:S(2)}) copy-start(bf16[256,384]{1,0:T(8,128)(2,1)S(1)} %attend.2) | copy-start | bytes 589828
  204.6 35.7 %slice-start = ((s8[12582912]{0:T(1024)(128)(4,1)}), s8[4194304]{0:T(1024)(128)(4,1)S(1)}, s32[]{:S(2)}) async-start(s8[12582912]{0:T(1024)(128)(4,1)} %bitcast.211), calls=%async_computation.7 | async-start | bytes 8388608
  204.6 35.7 %slice-start.1 = ((s8[12582912]{0:T(1024)(128)(4,1)}), s8[4194304]{0:T(1024)(128)(4,1)S(1)}, s32[]{:S(2)}) async-start(s8[12582912]{0:T(1024)(128)(4,1)} %bitcast.211), calls=%async_computation.8 | async-start | bytes 8388608
  210.7 29.6 %slice-start.2 = ((s8[12582912]{0:T(1024)(128)(4,1)}), s8[4194304]{0:T(1024)(128)(4,1)S(1)}, s32[]{:S(2)}) async-start(s8[12582912]{0:T(1024)(128)(4,1)} %bitcast.211), calls=%async_computation.9 | async-start | bytes 8388608
  271.6 21.1 %copy-start.15 = (bf16[4,64,1536]{2,1,0:T(8,128)(2,1)}, bf16[4,64,1536]{2,1,0:T(8,128)(2,1)S(1)}, u32[]{:S(2)}) copy-start(bf16[4,64,1536]{2,1,0:T(8,128)(2,1)S(1)} %get-tuple-element.122) | copy-start | bytes 2359300
  271.6 37.8 %copy-start.7 = (f32[4,16,1536]{2,1,0:T(8,128)}, f32[4,16,1536]{2,1,0:T(8,128)S(1)}, u32[]{:S(2)}) copy-start(f32[4,16,1536]{2,1,0:T(8,128)S(1)} %get-tuple-element.124.rows_ref.final_rest_ref) | copy-start | bytes 1179652
  309.4 295.7 %reduce-scatter.5.cloned.1.call-start = ((), (), s32[]{:S(2)}) async-start(), calls=%async_computation.6 | async-start | bytes 15925248 | tf_op jit(solution)/shard_map/reduce_scatter | solution.py:1588
  354.8 24.2 %copy-start.44 = (bf16[256,384]{1,0:T(8,128)(2,1)S(1)}, bf16[256,384]{1,0:T(8,128)(2,1)}, u32[]{:S(2)}) copy-start(bf16[256,384]{1,0:T(8,128)(2,1)} %get-tuple-element.126) | copy-start | bytes 589828
  377.4 20.6 %copy-start.14 = (bf16[4,64,1536]{2,1,0:T(8,128)(2,1)}, bf16[4,64,1536]{2,1,0:T(8,128)(2,1)S(1)}, u32[]{:S(2)}) copy-start(bf16[4,64,1536]{2,1,0:T(8,128)(2,1)S(1)} %get-tuple-element.129) | copy-start | bytes 2359300
  377.4 20.6 %slice-start.14 = ((s8[9437184]{0:T(1024)(128)(4,1)}), s8[4194304]{0:T(1024)(128)(4,1)S(1)}, s32[]{:S(2)}) async-start(s8[9437184]{0:T(1024)(128)(4,1)} %bitcast.273), calls=%async_computation.21 | async-start | bytes 8388608
  380.6 14.4 %copy-start.36 = (bf16[256,768]{1,0:T(8,128)(2,1)S(1)}, bf16[256,768]{1,0:T(8,128)(2,1)}, u32[]{:S(2)}) copy-start(bf16[256,768]{1,0:T(8,128)(2,1)} %get-tuple-element.127) | copy-start | bytes 1179652
  380.6 17.3 %slice-start.15 = ((s8[9437184]{0:T(1024)(128)(4,1)}), s8[4194304]{0:T(1024)(128)(4,1)S(1)}, s32[]{:S(2)}) async-start(s8[9437184]{0:T(1024)(128)(4,1)} %bitcast.273), calls=%async_computation.22 | async-start | bytes 8388608
  380.6 17.3 %slice-start.16 = ((s8[9437184]{0:T(1024)(128)(4,1)}), s8[1048576]{0:T(1024)(128)(4,1)S(1)}, s32[]{:S(2)}) async-start(s8[9437184]{0:T(1024)(128)(4,1)} %bitcast.273), calls=%async_computation.23 | async-start | bytes 2097152
  456.9 12.4 %slice-start.3 = ((s8[12582912]{0:T(1024)(128)(4,1)}), s8[4194304]{0:T(1024)(128)(4,1)S(1)}, s32[]{:S(2)}) async-start(s8[12582912]{0:T(1024)(128)(4,1)} %bitcast.233), calls=%async_computation.10 | async-start | bytes 8388608
  467.0 52.0 %collective-permute-start = (bf16[4,128,1536]{2,1,0:T(8,128)(2,1)}, bf16[4,128,1536]{2,1,0:T(8,128)(2,1)S(1)}, u32[]{:S(2)}, u32[]{:S(2)}) collective-permute-start(bf16[4,128,1536]{2,1,0:T(8,128)(2,1)} %bitcast.44), channel_id=1, source_target_pairs={{0,1},{1,0},{2,3},{3,2},{4,5},{5,4},{6,7},{7,6},{8,9},{9,8},{10,11... | collective-permute-start | bytes 4718600 | tf_op jit(solution)/shard_map/ppermute | solution.py:1502
  468.6 50.4 %collective-permute-start.1 = (bf16[4,128,1536]{2,1,0:T(8,128)(2,1)}, bf16[4,128,1536]{2,1,0:T(8,128)(2,1)}, u32[]{:S(2)}, u32[]{:S(2)}) collective-permute-start(bf16[4,128,1536]{2,1,0:T(8,128)(2,1)} %bitcast.46), channel_id=1, source_target_pairs={{0,2},{2,0},{1,3},{3,1},{4,6},{6,4},{5,7},{7,5},{8,10},{10,8},{9,1... | collective-permute-start | bytes 4718600 | tf_op jit(solution)/shard_map/ppermute | solution.py:1505
  477.0 117.3 %collective-permute-start.2 = (bf16[4,128,1536]{2,1,0:T(8,128)(2,1)}, bf16[4,128,1536]{2,1,0:T(8,128)(2,1)}, u32[]{:S(2)}, u32[]{:S(2)}) collective-permute-start(bf16[4,128,1536]{2,1,0:T(8,128)(2,1)} %bitcast.48), channel_id=1, source_target_pairs={{0,1},{1,0},{2,3},{3,2},{4,5},{5,4},{6,7},{7,6},{8,9},{9,8},{10,11... | collective-permute-start | bytes 4718600 | tf_op jit(solution)/shard_map/ppermute | solution.py:1502
  477.4 116.8 %collective-permute-start.3 = (bf16[4,128,1536]{2,1,0:T(8,128)(2,1)}, bf16[4,128,1536]{2,1,0:T(8,128)(2,1)}, u32[]{:S(2)}, u32[]{:S(2)}) collective-permute-start(bf16[4,128,1536]{2,1,0:T(8,128)(2,1)} %bitcast.50), channel_id=1, source_target_pairs={{0,2},{2,0},{1,3},{3,1},{4,6},{6,4},{5,7},{7,5},{8,10},{10,8},{9,1... | collective-permute-start | bytes 4718600 | tf_op jit(solution)/shard_map/ppermute | solution.py:1505
  487.2 18.4 %copy-start.12 = (bf16[256,384]{1,0:T(8,128)(2,1)S(1)}, bf16[256,384]{1,0:T(8,128)(2,1)}, u32[]{:S(2)}) copy-start(bf16[256,384]{1,0:T(8,128)(2,1)} %copy-done.11) | copy-start | bytes 589828
  606.6 18.8 %copy-start.47 = (f32[12,1536]{1,0:T(8,128)S(1)}, f32[12,1536]{1,0:T(8,128)}, u32[]{:S(2)}) copy-start(f32[12,1536]{1,0:T(8,128)} %reshape.207) | copy-start | bytes 221188
  606.6 18.8 %copy-start.48 = (f32[12,1536]{1,0:T(8,128)S(1)}, f32[12,1536]{1,0:T(8,128)}, u32[]{:S(2)}) copy-start(f32[12,1536]{1,0:T(8,128)} %reshape.208) | copy-start | bytes 221188
  606.6 18.8 %copy-start.49 = (f32[12,1536]{1,0:T(8,128)S(1)}, f32[12,1536]{1,0:T(8,128)}, u32[]{:S(2)}) copy-start(f32[12,1536]{1,0:T(8,128)} %reshape.209) | copy-start | bytes 221188
  628.2 22.2 %copy-start.46 = (f32[4,16,1536]{2,1,0:T(8,128)S(1)}, f32[4,16,1536]{2,1,0:T(8,128)}, u32[]{:S(2)}) copy-start(f32[4,16,1536]{2,1,0:T(8,128)} %get-tuple-element.276) | copy-start | bytes 1179652
  628.2 23.0 %copy-start.45 = (f32[4,16,1536]{2,1,0:T(8,128)S(1)}, f32[4,16,1536]{2,1,0:T(8,128)}, u32[]{:S(2)}) copy-start(f32[4,16,1536]{2,1,0:T(8,128)} %get-tuple-element.277) | copy-start | bytes 1179652
  (51 other events, 216.4 us)
Sparse Core Ops, SparseCore 0:
  11.4 93.4 all-gather.3
  107.1 89.1 all-gather.5
  198.5 89.1 all-gather.7
  309.5 97.9 reduce-scatter.2
  415.8 166.3 reduce-scatter.4
